TPU v7x, 32 devices: a whole 2x2x4 slice. The times are simulated.
32 devices in a mesh: batch: 4 (over y, x), seq: 8 (over z, core).
Axes of the slice: x: 2, y: 2, z: 4, core: 2. Of those that a mesh axis runs over, the one named last changes fastest.
Arguments:
- hidden_in: bfloat16 [16, 2048, 1024], P('batch', 'seq'), may hold values from -6 to 6
- cotangent: bfloat16 [16, 2048, 1024], P('batch', 'seq'), may hold values from -6 to 6
- lengths: int32 [16], P('batch'), may hold values from 256 to 2048, as said below
- key_mask: int32 [16, 2048], P('batch', 'seq'), may hold values 0 or 1
- ln1_gain: float32 [1024], replicated, may hold values from 0.5 to 1.5
- ln1_bias: float32 [1024], replicated, may hold values from -1.25 to 1.25
- ln2_gain: float32 [1024], replicated, may hold values from 0.5 to 1.5
- ln2_bias: float32 [1024], replicated, may hold values from -1.25 to 1.25
- w_qkv: bfloat16 [1024, 3072], replicated, may hold values from -0.1875 to 0.1875
- b_qkv: float32 [3072], replicated, may hold values from -1.25 to 1.25
- w_out: bfloat16 [1024, 1024], replicated, may hold values from -4 to 4
- b_out: float32 [1024], replicated, may hold values from -1.25 to 1.25
- w_up: bfloat16 [1024, 4096], replicated, may hold values from -0.1875 to 0.1875
- b_up: float32 [4096], replicated, may hold values from -1.25 to 1.25
- w_down: bfloat16 [4096, 1024], replicated, may hold values from -0.09375 to 0.09375
- b_down: float32 [1024], replicated, may hold values from -1.25 to 1.25
- feat_weight: float32 [1024], replicated, may hold values from 0.3 to 3
- directions: float32 [64, 64], replicated, may hold values from -2 to 2
Outputs:
- result: bfloat16 [16, 2048, 1024], P('batch', 'seq')
- grad_input: float32 [16, 2048, 1024], P('batch', 'seq')
- ln1_gain_grad: float32 [1024], P('seq')
- ln1_bias_grad: float32 [1024], P('seq')
- ln2_gain_grad: float32 [1024], P('seq')
- ln2_bias_grad: float32 [1024], P('seq')
- w_qkv_grad: float32 [1024, 3072], P('seq', 'batch')
- b_qkv_grad: float32 [3072], P('seq')
- w_out_grad: float32 [1024, 1024], P('seq', 'batch')
- b_out_grad: float32 [1024], P('seq')
- w_up_grad: float32 [1024, 4096], P('seq', 'batch')
- b_up_grad: float32 [4096], P('seq')
- w_down_grad: float32 [4096, 1024], P('seq', 'batch')
- b_down_grad: float32 [1024], P('seq')
- feat_weight_grad: float32 [1024], P('seq')
Inputs may be any that keep to these rules, and one draw needn't show every extreme that they name: `lengths`: of each 4 consecutive sequences (one index of batch), one, chosen by the seed, has length 2048; the others from 256 to 2048.
All inputs are finite; a program needn't handle non-finite values. No bound on the sum of `key_mask` on one device may be relied on, other than what follows from the above.
Results may differ from a plain program's by a relative error of at most 0.0089.
Values sent between devices are 32-bit elements; how exact they have to be, the bound alone decides.
No kernel may reach another device: no remote copies, remote signals or barrier semaphores. Data moves between devices by JAX's collectives and lax.ppermute only.
A program may use at most 448 MiB of HBM per device.

v0:
```python
import math

import jax
import jax.numpy as jnp
from jax import lax
from jax.sharding import PartitionSpec as P

HEADS = 16
HEAD_DIM = 64
ROT = 16
FEATS = 64


norm_epsilon = 1e-05
rope_base = 10000.0


def carried_in(value, axis, combine, identity, reverse):
    length, index = (lax.axis_size(axis), lax.axis_index(axis))
    everything = jax.tree.map(lambda part: lax.all_gather(part, axis), value)
    start = jax.tree.map(
        lambda part, zero: jnp.broadcast_to(jnp.asarray(zero, part.dtype), part.shape),
        value,
        identity,
    )

    def turn(k, before):
        at = length - 1 - k if reverse else k
        reached = at > index if reverse else at < index
        new = combine(before, jax.tree.map(lambda part: part[at], everything))
        return jax.tree.map(lambda a, b: jnp.where(reached, a, b), new, before)

    return lax.fori_loop(0, length, turn, start)


def layer_norm(values, gain, shift):
    centre = values - jnp.mean(values, axis=-1, keepdims=True)
    spread = jnp.mean(centre * centre, axis=-1, keepdims=True)
    return centre * lax.rsqrt(spread + norm_epsilon) * gain + shift


def gelu_exact(values):
    return jax.nn.gelu(values, approximate=False)


def dct_table(order):
    degree = jnp.arange(order, dtype=jnp.float32)[:, None]
    sample = jnp.arange(order, dtype=jnp.float32)[None, :]
    table = jnp.cos(math.pi * (sample + 0.5) * degree / order) * math.sqrt(2.0 / order)
    return jnp.where(degree == 0.0, table * math.sqrt(0.5), table)


def rotate_heads(heads, positions):
    half_rot = ROT // 2
    inverse = rope_base ** (-2.0 * jnp.arange(half_rot, dtype=jnp.float32) / ROT)
    angles = positions[:, None] * inverse[None, :]
    cosine = jnp.cos(angles)[:, None, :]
    sine = jnp.sin(angles)[:, None, :]
    first = heads[..., :half_rot]
    second = heads[..., half_rot:ROT]
    remain = heads[..., ROT:]
    return jnp.concatenate(
        [first * cosine - second * sine, second * cosine + first * sine, remain], axis=-1
    )


def featurize(heads, weights, directions):
    table = dct_table(HEAD_DIM)
    coeffs = jnp.einsum("glhd,kd->glhk", heads, table, precision=lax.Precision.HIGHEST)
    phases = jnp.einsum("glhk,mk->glhm", coeffs, directions, precision=lax.Precision.HIGHEST)
    return weights * jnp.exp(phases)


def add_pair(earlier, later):
    return (earlier[0] + later[0], earlier[1] + later[1])


def per_device(
    hidden_in,
    cotangent,
    lengths,
    key_mask,
    ln1_gain,
    ln1_bias,
    ln2_gain,
    ln2_bias,
    w_qkv,
    b_qkv,
    w_out,
    b_out,
    w_up,
    b_up,
    w_down,
    b_down,
    feat_weight,
    directions,
):
    seq_count, block_len, width = hidden_in.shape
    rows = seq_count * block_len
    places = lax.axis_index("seq") * block_len + jnp.arange(block_len, dtype=jnp.int32)
    positions = places.astype(jnp.float32)
    validity = (
        (places[None, :] < lengths[:, None]) & ((key_mask == 1) | (places[None, :] == 0))
    ).astype(jnp.float32)
    flat_in = hidden_in.astype(jnp.float32).reshape(rows, width)
    norm_one, pull_one = jax.vjp(layer_norm, flat_in, ln1_gain, ln1_bias)
    norm_two, pull_two = jax.vjp(layer_norm, flat_in, ln2_gain, ln2_bias)
    low_one = norm_one.astype(jnp.bfloat16)
    low_two = norm_two.astype(jnp.bfloat16)
    proj_all = jnp.dot(low_one, w_qkv, preferred_element_type=jnp.float32) + b_qkv
    shape4 = (seq_count, block_len, HEADS, HEAD_DIM)
    query = proj_all[:, :width].reshape(shape4)
    keys = proj_all[:, width : 2 * width].reshape(shape4)
    values_low = proj_all[:, 2 * width :].reshape(shape4).astype(jnp.bfloat16)

    def feature_pair(query_in, key_in, weight_flat):
        weights = weight_flat.reshape(HEADS, FEATS)
        return (
            featurize(rotate_heads(query_in, positions), weights, directions),
            featurize(rotate_heads(key_in, positions), weights, directions),
        )

    feats, pull_feat = jax.vjp(feature_pair, query, keys, feat_weight)
    key_gate = validity[:, :, None, None]
    query_low = feats[0].astype(jnp.bfloat16).transpose(0, 2, 1, 3)
    key_low = (feats[1].astype(jnp.bfloat16) * key_gate.astype(jnp.bfloat16)).transpose(0, 2, 1, 3)
    value_heads = values_low.transpose(0, 2, 1, 3)
    highest = lax.Precision.HIGHEST
    state_local = jnp.einsum(
        "ghsf,ghsd->ghfd", key_low, value_heads, preferred_element_type=jnp.float32
    )
    norm_local = jnp.sum(key_low, axis=2, dtype=jnp.float32)
    zero_pair = (jnp.zeros_like(state_local), jnp.zeros_like(norm_local))
    state_in, norm_in = carried_in((state_local, norm_local), "seq", add_pair, zero_pair, False)
    causal = (jnp.arange(block_len)[:, None] >= jnp.arange(block_len)[None, :]).astype(jnp.float32)
    scores = (
        jnp.einsum("ghtf,ghsf->ghts", query_low, key_low, preferred_element_type=jnp.float32)
        * causal
    )
    numer = jnp.einsum(
        "ghts,ghsd->ghtd",
        scores,
        value_heads,
        precision=highest,
        preferred_element_type=jnp.float32,
    )
    numer = numer + jnp.einsum(
        "ghtf,ghfd->ghtd",
        query_low,
        state_in,
        precision=highest,
        preferred_element_type=jnp.float32,
    )
    denom = jnp.sum(scores, axis=-1) + jnp.einsum(
        "ghtf,ghf->ght", query_low, norm_in, precision=highest, preferred_element_type=jnp.float32
    )
    attn_ratio = numer / denom[..., None]
    mixed_low = attn_ratio.transpose(0, 2, 1, 3).reshape(rows, width).astype(jnp.bfloat16)
    attn_out = jnp.dot(mixed_low, w_out, preferred_element_type=jnp.float32) + b_out
    hidden_pre = jnp.dot(low_two, w_up, preferred_element_type=jnp.float32) + b_up
    gelu_out, pull_gelu = jax.vjp(gelu_exact, hidden_pre)
    gelu_low = gelu_out.astype(jnp.bfloat16)
    ffn_out = jnp.dot(gelu_low, w_down, preferred_element_type=jnp.float32) + b_down
    result = (flat_in + attn_out + ffn_out).astype(jnp.bfloat16).reshape(hidden_in.shape)
    grad_out = cotangent.reshape(rows, width)
    grad_wide = grad_out.astype(jnp.float32)
    grad_bias_res = jnp.sum(grad_wide, axis=0)
    grad_w_out = jnp.einsum("rd,re->de", mixed_low, grad_out, preferred_element_type=jnp.float32)
    grad_mixed = jnp.einsum("re,de->rd", grad_out, w_out, preferred_element_type=jnp.float32)
    grad_w_down = jnp.einsum("rf,re->fe", gelu_low, grad_out, preferred_element_type=jnp.float32)
    grad_gelu = jnp.einsum("re,fe->rf", grad_out, w_down, preferred_element_type=jnp.float32)
    grad_pre = pull_gelu(grad_gelu)[0].astype(jnp.bfloat16)
    grad_b_up = jnp.sum(grad_pre, axis=0, dtype=jnp.float32)
    grad_w_up = jnp.einsum("rd,rf->df", low_two, grad_pre, preferred_element_type=jnp.float32)
    grad_two = jnp.einsum("rf,df->rd", grad_pre, w_up, preferred_element_type=jnp.float32)
    grad_heads = grad_mixed.reshape(shape4).transpose(0, 2, 1, 3)
    grad_numer = grad_heads / denom[..., None]
    grad_denom = -jnp.sum(grad_heads * attn_ratio, axis=-1) / denom
    state_grad = jnp.einsum(
        "ghtf,ghtd->ghfd",
        query_low,
        grad_numer,
        precision=highest,
        preferred_element_type=jnp.float32,
    )
    norm_grad = jnp.einsum(
        "ghtf,ght->ghf",
        query_low,
        grad_denom,
        precision=highest,
        preferred_element_type=jnp.float32,
    )
    state_later, norm_later = carried_in((state_grad, norm_grad), "seq", add_pair, zero_pair, True)
    grad_scores = (
        jnp.einsum(
            "ghtd,ghsd->ghts",
            grad_numer,
            value_heads,
            precision=highest,
            preferred_element_type=jnp.float32,
        )
        + grad_denom[..., None]
    ) * causal
    grad_qfeat = jnp.einsum(
        "ghts,ghsf->ghtf",
        grad_scores,
        key_low,
        precision=highest,
        preferred_element_type=jnp.float32,
    )
    grad_qfeat = grad_qfeat + jnp.einsum("ghtd,ghfd->ghtf", grad_numer, state_in, precision=highest)
    grad_qfeat = grad_qfeat + grad_denom[..., None] * norm_in[:, :, None, :]
    grad_kfeat = jnp.einsum(
        "ghts,ghtf->ghsf",
        grad_scores,
        query_low,
        precision=highest,
        preferred_element_type=jnp.float32,
    )
    grad_kfeat = grad_kfeat + jnp.einsum(
        "ghsd,ghfd->ghsf",
        value_heads,
        state_later,
        precision=highest,
        preferred_element_type=jnp.float32,
    )
    grad_kfeat = grad_kfeat + norm_later[:, :, None, :]
    grad_values = jnp.einsum("ghts,ghtd->ghsd", scores, grad_numer, precision=highest)
    grad_values = grad_values + jnp.einsum(
        "ghsf,ghfd->ghsd",
        key_low,
        state_later,
        precision=highest,
        preferred_element_type=jnp.float32,
    )
    grad_query, grad_keys, grad_feat = pull_feat(
        (grad_qfeat.transpose(0, 2, 1, 3), grad_kfeat.transpose(0, 2, 1, 3) * key_gate)
    )
    grad_proj = jnp.concatenate(
        [
            grad_query.reshape(rows, width),
            grad_keys.reshape(rows, width),
            grad_values.transpose(0, 2, 1, 3).reshape(rows, width),
        ],
        axis=1,
    ).astype(jnp.bfloat16)
    grad_b_qkv = jnp.sum(grad_proj, axis=0, dtype=jnp.float32)
    grad_w_qkv = jnp.einsum("rd,rc->dc", low_one, grad_proj, preferred_element_type=jnp.float32)
    grad_one = jnp.einsum("rc,dc->rd", grad_proj, w_qkv, preferred_element_type=jnp.float32)
    grad_in_one, grad_g1, grad_s1 = pull_one(grad_one)
    grad_in_two, grad_g2, grad_s2 = pull_two(grad_two)
    grad_input = (grad_wide + grad_in_one + grad_in_two).reshape(hidden_in.shape)
    parts = (
        lax.psum_scatter(grad_w_qkv, "seq", scatter_dimension=0, tiled=True),
        lax.psum_scatter(grad_w_out, "seq", scatter_dimension=0, tiled=True),
        lax.psum_scatter(grad_w_up, "seq", scatter_dimension=0, tiled=True),
        lax.psum_scatter(grad_w_down, "seq", scatter_dimension=0, tiled=True),
        lax.psum_scatter(grad_g1, "seq", scatter_dimension=0, tiled=True),
        lax.psum_scatter(grad_s1, "seq", scatter_dimension=0, tiled=True),
        lax.psum_scatter(grad_g2, "seq", scatter_dimension=0, tiled=True),
        lax.psum_scatter(grad_s2, "seq", scatter_dimension=0, tiled=True),
        lax.psum_scatter(grad_b_qkv, "seq", scatter_dimension=0, tiled=True),
        lax.psum_scatter(grad_bias_res, "seq", scatter_dimension=0, tiled=True),
        lax.psum_scatter(grad_b_up, "seq", scatter_dimension=0, tiled=True),
        lax.psum_scatter(grad_feat, "seq", scatter_dimension=0, tiled=True),
    )
    matrices = (
        lax.psum_scatter(parts[0], "batch", scatter_dimension=1, tiled=True),
        lax.psum_scatter(parts[1], "batch", scatter_dimension=1, tiled=True),
        lax.psum_scatter(parts[2], "batch", scatter_dimension=1, tiled=True),
        lax.psum_scatter(parts[3], "batch", scatter_dimension=1, tiled=True),
    )
    vectors = lax.psum(
        (parts[4], parts[5], parts[6], parts[7], parts[8], parts[9], parts[10], parts[11]), "batch"
    )
    return (
        result,
        grad_input,
        vectors[0],
        vectors[1],
        vectors[2],
        vectors[3],
        matrices[0],
        vectors[4],
        matrices[1],
        vectors[5],
        matrices[2],
        vectors[6],
        matrices[3],
        vectors[5],
        vectors[7],
    )


def solution(mesh):
    placed = (
        P("batch", "seq", None),
        P("batch", "seq", None),
        P("batch"),
        P("batch", "seq"),
        P(),
        P(),
        P(),
        P(),
        P(),
        P(),
        P(),
        P(),
        P(),
        P(),
        P(),
        P(),
        P(),
        P(),
    )
    return jax.shard_map(
        per_device,
        mesh=mesh,
        in_specs=placed,
        out_specs=(
            P("batch", "seq", None),
            P("batch", "seq", None),
            P("seq"),
            P("seq"),
            P("seq"),
            P("seq"),
            P("seq", "batch"),
            P("seq"),
            P("seq", "batch"),
            P("seq"),
            P("seq", "batch"),
            P("seq"),
            P("seq", "batch"),
            P("seq"),
            P("seq"),
        ),
        check_vma=False,
    )
```

profile of v0, /device:TPU:16, one launch (start us, length us, event | category | flops | bytes accessed | tf_op | source)
XLA Modules:
  0.0 1173.1 jit_solution(10230425960148426521)
XLA Ops:
  37.3 12.9 %fusion.137 = (f32[4,256,16,8]{3,2,1,0:T(8,128)}, f32[4,256,16,8]{3,2,1,0:T(8,128)}) fusion(f32[4,256,16,64]{3,2,1,0:T(8,128)} %reshape.294), kind=kLoop, calls=%fused_computation.208 | loop fusion | bytes 2097152 | tf_op jit(solution)/shard_map/jvp()/slice | solution.py:60
  67.0 13.1 %fusion.138 = (f32[4,256,16,8]{3,2,1,0:T(8,128)}, f32[4,256,16,8]{3,2,1,0:T(8,128)}) fusion(f32[4,256,16,64]{3,2,1,0:T(8,128)} %reshape.293), kind=kLoop, calls=%fused_computation.209 | loop fusion | bytes 2097152 | tf_op jit(solution)/shard_map/jvp()/slice | solution.py:60
  161.7 18.7 %all-gather.1 = f32[32,16,64]{2,1,0:T(8,128)} all-gather(f32[4,16,64]{2,1,0:T(8,128)S(1)} %get-tuple-element.379), channel_id=3, replica_groups=mesh['batch'=4,'seq'=8] {'seq'}, dimensions={0}, use_global_device_ids=true | all-gather | bytes 147456 | tf_op jit(solution)/shard_map/all_gather | solution.py:20
  202.4 15.9 %fusion.10 = f32[4,16,256,64]{2,3,1,0:T(8,128)} fusion(f32[4,16,256,256]{2,3,1,0:T(8,128)} %get-tuple-element.412, f32[256,256]{0,1:T(8,128)S(1)} %fusion.76, bf16[4,256,16,64]{1,3,2,0:T(8,128)(2,1)} %copy.83), kind=kOutput, calls=%fused_computation.28 | convolution fusion | flops 3225419776 | bytes 23330816 | tf_op jit(solution)/shard_map/ghts,ghsd->ghtd/dot_general | solution.py:140
  218.3 78.6 %all-gather.7.cloned.1.call-done = f32[32,16,64,64]{3,2,1,0:T(8,128)} async-done(((f32[4,16,64,64]{3,2,1,0:T(8,128)}), f32[32,16,64,64]{3,2,1,0:T(8,128)}) %all-gather.7.cloned.1.call-update) | async-done | bytes 8388624 | tf_op jit(solution)/shard_map/all_gather | solution.py:20
  296.8 39.5 %while.34 = (s32[]{:T(128)}, f32[4,16,64,64]{3,2,1,0:T(8,128)}, f32[4,16,64]{2,1,0:T(8,128)S(1)}, s32[]{:T(128)}, f32[8,4,16,64,64]{4,3,2,1,0:T(8,128)}, /*index=5*/f32[8,4,16,64]{3,2,1,0:T(8,128)}, s32[]{:T(128)}, s32[]{:T(128)}) while((s32[]{:T(128)}, f32[4,16,64,64]{3,2,1,0:T(8,128)}, f32[4,16,64]{2,1,0:T(8,128)S(1)}, ...), condition=%wide.region_4.5_spmd.clone, body=%wide.region_3.0_spmd.clone.sunk | while | flops 798724 | bytes 3194995 | solution.py:33
  355.4 16.6 %fusion.141 = f32[1024,4096]{1,0:T(8,128)} fusion(bf16[1024,1024]{1,0:T(8,128)(2,1)} %get-tuple-element.393, bf16[1024,4096]{1,0:T(8,128)(2,1)} %param.34), kind=kOutput, calls=%fused_computation.212 | convolution fusion | flops 8589934592 | bytes 27262976 | tf_op jit(solution)/shard_map/dot_general | solution.py:160
  380.8 52.0 %convert_reduce_fusion = (f32[4096]{0:T(1024)}, bf16[1024,4096]{1,0:T(8,128)(2,1)}, f32[1024,4096]{1,0:T(8,128)S(1)}) fusion(f32[1024,4096]{1,0:T(8,128)} %fusion.141, f32[4096]{0:T(1024)S(1)} %copy-done.60, bf16[1024,1024]{1,0:T(8,128)(2,1)} %bitcast.245, bf16[4096,1024]{1,0:T(8,128)(2,1)} %param.36), kind=kOutput, calls=%fused_computation.6 | convolution fusion | flops 8904503296 | bytes 52461568 | tf_op jit(solution)/shard_map/re,fe->rf/dot_general | solution.py:171
  456.2 16.5 %fusion.145 = f32[1024,4096]{1,0:T(8,128)} fusion(bf16[1024,1024]{1,0:T(8,128)(2,1)} %get-tuple-element.393, bf16[1024,4096]{1,0:T(8,128)(2,1)} %get-tuple-element.377), kind=kOutput, calls=%fused_computation.216 | convolution fusion | flops 8589934592 | bytes 27262976 | tf_op jit(solution)/shard_map/rd,rf->df/dot_general | solution.py:174
  473.7 14.0 %fusion.68 = f32[4,16,256,256]{2,3,1,0:T(8,128)} fusion(bf16[4,256,16,64]{1,3,2,0:T(8,128)(2,1)} %copy.83, f32[4,256,16,64]{1,3,2,0:T(8,128)} %copy-done.17, f32[4,16,256]{2,1,0:T(8,128)S(1)} %copy-done.32), kind=kOutput, calls=%fused_computation.111 | convolution fusion | flops 3222274048 | bytes 23134208 | tf_op jit(solution)/shard_map/ghtd,ghsd->ghts/dot_general | solution.py:195
  487.7 15.9 %fusion.7 = f32[4,16,256,64]{2,3,1,0:T(8,128)} fusion(bf16[4,16,256,64]{2,3,1,0:T(8,128)(2,1)} %copy-done.7, f32[4,16,256,256]{2,3,1,0:T(8,128)} %fusion.68, f32[4,16,256]{2,1,0:T(8,128)S(1)} %negate_divide_fusion, f32[256,256]{0,1:T(8,128)S(1)} %copy-done.19), kind=kOutput, calls=%fused_computation.24 | convolution fusion | flops 3229614080 | bytes 23396352 | tf_op jit(solution)/shard_map/ghts,ghsf->ghtf/dot_general | solution.py:204
  529.7 16.0 %all-gather.3 = f32[32,16,64]{2,1,0:T(8,128)S(1)} all-gather(f32[4,16,64]{2,1,0:T(8,128)S(1)} %bitcast.264), channel_id=5, replica_groups=mesh['batch'=4,'seq'=8] {'seq'}, dimensions={0}, use_global_device_ids=true | all-gather | bytes 147456 | tf_op jit(solution)/shard_map/all_gather | solution.py:20
  545.6 18.2 %fusion.6 = f32[4,16,256,64]{2,3,1,0:T(8,128)} fusion(bf16[4,16,256,64]{2,3,1,0:T(8,128)(2,1)} %copy-done.12, f32[4,16,256,256]{2,3,1,0:T(8,128)} %fusion.68, f32[4,16,256]{2,1,0:T(8,128)S(1)} %negate_divide_fusion, f32[256,256]{0,1:T(8,128)S(1)} %copy-done.19), kind=kOutput, calls=%fused_computation.23 | convolution fusion | flops 3229614080 | bytes 23396352 | tf_op jit(solution)/shard_map/ghts,ghtf->ghsf/dot_general | solution.py:213
  563.8 23.5 %fusion.8 = f32[4,16,256,64]{2,3,1,0:T(8,128)} fusion(f32[4,16,256,256]{2,3,1,0:T(8,128)} %get-tuple-element.412, f32[256,256]{0,1:T(8,128)S(1)} %copy-done.19, f32[4,256,16,64]{1,3,2,0:T(8,128)} %copy-done.17, f32[4,16,256]{2,1,0:T(8,128)S(1)} %copy-done.32), kind=kOutput, calls=%fused_computation.25 | convolution fusion | flops 3226468352 | bytes 25493504 | tf_op jit(solution)/shard_map/ghts,ghtd->ghsd/dot_general | solution.py:228
  587.3 33.7 %while.35 = (s32[]{:T(128)}, f32[4,16,64,64]{3,2,1,0:T(8,128)}, f32[4,16,64]{2,1,0:T(8,128)S(1)}, s32[]{:T(128)}, f32[8,4,16,64,64]{4,3,2,1,0:T(8,128)}, /*index...) while((s32[]{:T(128)}, f32[4,16,64,64]{3,2,1,0:T(8,128)}, ...), condition=%wide.region_8.9_spmd.clone, body=%wide.region_7.8_spmd.clone.sunk | while | flops 798728 | bytes 3195057 | solution.py:33
  665.0 60.4 %reduce-scatter.21.cloned.1.call-done = f32[512,1024]{1,0:T(8,128)} async-done(((f32[4096,1024]{1,0:T(8,128)}), f32[512,1024]{1,0:T(8,128)}) %reduce-scatter.21.cloned.1.call-update) | async-done | bytes 2097168 | tf_op jit(solution)/shard_map/reduce_scatter | solution.py:257
  725.4 168.8 %reduce-scatter.17.cloned.1.call-done = f32[128,4096]{1,0:T(8,128)} async-done(((f32[1024,4096]{1,0:T(8,128)}), f32[128,4096]{1,0:T(8,128)}) %reduce-scatter.17.cloned.1.call-update) | async-done | bytes 2097168 | tf_op jit(solution)/shard_map/reduce_scatter | solution.py:256
  894.3 15.0 %fusion.142 = f32[1024,1024]{1,0:T(8,128)} fusion(bf16[1024,4096]{1,0:T(8,128)(2,1)} %get-tuple-element.377, bf16[1024,4096]{1,0:T(8,128)(2,1)} %param.34), kind=kOutput, calls=%fused_computation.213 | convolution fusion | flops 8589934592 | bytes 20971520 | tf_op jit(solution)/shard_map/rf,df->rd/dot_general | solution.py:175
  918.1 14.9 %fusion.56 = bf16[1024,1024]{1,0:T(8,128)(2,1)} fusion(bf16[4,256,1024]{2,1,0:T(8,128)(2,1)S(1)} %copy-done.10, f32[1024,1024]{1,0:T(8,128)S(1)} %fusion.140, f32[1024]{0:T(1024)S(1)} %copy-done.74, f32[1024]{0:T(1024)S(1)} %copy-done.75, bf16[1024,4096]{1,0:T(8,128)(2,1)} %copy-done.27, bf16[4096,1024]{1,0:T(8,128)(2,1)} %param.36), kind=kOutput, calls=%fused_computation.88 | convolution fusion | flops 8596226048 | bytes 25174016 | tf_op jit(solution)/shard_map/dot_general | solution.py:163
  933.0 91.0 %reduce-scatter.9.cloned.1.call-done = f32[128,3072]{1,0:T(8,128)} async-done(((f32[1024,3072]{1,0:T(8,128)}), f32[128,3072]{1,0:T(8,128)}) %reduce-scatter.9.cloned.1.call-update) | async-done | bytes 1572880 | tf_op jit(solution)/shard_map/reduce_scatter | solution.py:254
  1024.0 14.7 %fusion.132 = (f32[1024]{0:T(1024)S(1)}, f32[1024]{0:T(1024)S(1)}, f32[1024]{0:T(1024)S(1)}, f32[1024]{0:T(1024)S(1)}, f32[1024,1024]{1,0:T(8,128)}) fusion(f32[1024]{0:T(1024)S(1)} %copy-done.59, f32[1024]{0:T(1024)S(1)} %bitcast.259, bf16[4,256,1024]{2,1,0:T(8,128)(2,1)} %param.22, f32[1024,1024]{1,0:T(8,128)} %fusion.142, f32[1024]{0:T(1024)S(1)} %copy-done.57, ...), kind=kOutput, calls=%fused_computation.205 | convolution fusion | flops 6452932608 | bytes 23097344 | tf_op jit(solution)/shard_map/rc,dc->rd/dot_general | solution.py:249
  1048.8 23.2 %all-reduce.14 = (f32[1024]{0:T(1024)S(1)}, f32[1024]{0:T(1024)S(1)}, f32[1024]{0:T(1024)S(1)}, f32[1024]{0:T(1024)S(1)}, f32[3072]{0:T(1024)S(1)}, /*index=5*/f...) all-reduce(f32[1024]{0:T(1024)S(1)} %get-tuple-element.335, ...), channel_id=6, replica_groups=mesh['batch'=4,'seq'=8] {'seq'}, use_global_device_ids=true, to_apply=%region_14.15.clone | all-reduce | flops 13312 | bytes 106496
  1092.1 38.8 %reduce-scatter.19.cloned.1.call-done = f32[128,1024]{1,0:T(8,128)} async-done(((f32[128,4096]{1,0:T(8,128)}), f32[128,1024]{1,0:T(8,128)}) %reduce-scatter.19.cloned.1.call-update) | async-done | bytes 524304 | tf_op jit(solution)/shard_map/reduce_scatter | solution.py:270
  1130.9 34.6 %reduce-scatter.11.cloned.1.call-done = f32[128,768]{1,0:T(8,128)} async-done(((f32[128,3072]{1,0:T(8,128)}), f32[128,768]{1,0:T(8,128)}) %reduce-scatter.11.cloned.1.call-update) | async-done | bytes 393232 | tf_op jit(solution)/shard_map/reduce_scatter | solution.py:268
  (314 shorter events, 382.0 us)
Async XLA Ops:
  7.2 339.0 %copy-start = (bf16[1024,1024]{1,0:T(8,128)(2,1)S(1)}, bf16[1024,1024]{1,0:T(8,128)(2,1)}, u32[]{:S(2)}) copy-start(bf16[1024,1024]{1,0:T(8,128)(2,1)} %param.32) | copy-start | bytes 6291460
  7.2 289.6 %all-gather.7.cloned.1.call-start = ((), (), s32[]{:S(2)}) async-start(), calls=%async_computation.16 | async-start | bytes 18874368 | tf_op jit(solution)/shard_map/all_gather | solution.py:20
  55.8 124.7 %copy-start.63 = (f32[64]{0:T(128)}, f32[64]{0:T(128)S(1)}, u32[]{:S(2)}) copy-start(f32[64]{0:T(128)S(1)} %add_multiply_fusion.4) | copy-start | bytes 772
  55.8 124.7 %copy-start.65 = (pred[64]{0:T(512)(128)(4,1)}, pred[64]{0:T(512)(128)(4,1)S(1)}, u32[]{:S(2)}) copy-start(pred[64]{0:T(512)(128)(4,1)S(1)} %iota_compare_fusion.1) | copy-start | bytes 196
  113.8 76.8 %copy-start.44 = (f32[16,64]{1,0:T(8,128)}, f32[16,64]{1,0:T(8,128)S(1)}, u32[]{:S(2)}) copy-start(f32[16,64]{1,0:T(8,128)S(1)} %mul.436) | copy-start | bytes 12292
  144.2 443.1 %all-gather.9.cloned.1.call-start = ((), (), s32[]{:S(2)}) async-start(), calls=%async_computation.17 | async-start | bytes 18874368 | tf_op jit(solution)/shard_map/all_gather | solution.py:20
  153.3 27.2 %copy-start.37 = (f32[4,256,16,8]{1,3,2,0:T(8,128)S(1)}, f32[4,256,16,8]{1,3,2,0:T(8,128)}, u32[]{:S(2)}) copy-start(f32[4,256,16,8]{1,3,2,0:T(8,128)} %get-tuple-element.403) | copy-start | bytes 1572868
  153.3 27.3 %copy-start.38 = (f32[4,256,16,8]{1,3,2,0:T(8,128)S(1)}, f32[4,256,16,8]{1,3,2,0:T(8,128)}, u32[]{:S(2)}) copy-start(f32[4,256,16,8]{1,3,2,0:T(8,128)} %get-tuple-element.404) | copy-start | bytes 1572868
  180.5 21.9 %copy-start.18 = (f32[256,256]{0,1:T(8,128)}, f32[256,256]{0,1:T(8,128)S(1)}, u32[]{:S(2)}) copy-start(f32[256,256]{0,1:T(8,128)S(1)} %fusion.76) | copy-start | bytes 786436
  355.4 308.9 %reduce-scatter.13.cloned.1.call-start = ((), (), s32[]{:S(2)}) async-start(), calls=%async_computation.10 | async-start | bytes 4718592 | tf_op jit(solution)/shard_map/reduce_scatter | solution.py:255
  355.4 16.6 %copy-start.36 = (bf16[4,256,16,64]{1,3,2,0:T(8,128)(2,1)S(1)}, bf16[4,256,16,64]{1,3,2,0:T(8,128)(2,1)}, u32[]{:S(2)}) copy-start(bf16[4,256,16,64]{1,3,2,0:T(8,128)(2,1)} %get-tuple-element.413) | copy-start | bytes 6291460
  380.1 345.3 %reduce-scatter.21.cloned.1.call-start = ((), (), s32[]{:S(2)}) async-start(), calls=%async_computation.14 | async-start | bytes 18874368 | tf_op jit(solution)/shard_map/reduce_scatter | solution.py:257
  456.2 438.0 %reduce-scatter.17.cloned.1.call-start = ((), (), s32[]{:S(2)}) async-start(), calls=%async_computation.12 | async-start | bytes 18874368 | tf_op jit(solution)/shard_map/reduce_scatter | solution.py:256
  472.8 551.2 %reduce-scatter.9.cloned.1.call-start = ((), (), s32[]{:S(2)}) async-start(), calls=%async_computation.8 | async-start | bytes 14155776 | tf_op jit(solution)/shard_map/reduce_scatter | solution.py:254
  487.7 16.0 %copy-start.40 = (f32[4,16,64]{2,1,0:T(8,128)S(1)}, f32[4,16,64]{2,1,0:T(8,128)}, u32[]{:S(2)}) copy-start(f32[4,16,64]{2,1,0:T(8,128)} %copy-done.39) | copy-start | bytes 49156
  664.2 426.5 %reduce-scatter.15.cloned.1.call-start = ((), (), s32[]{:S(2)}) async-start(), calls=%async_computation.11 | async-start | bytes 655360 | tf_op jit(solution)/shard_map/reduce_scatter | solution.py:269
  664.9 427.2 %reduce-scatter.23.cloned.1.call-start = ((), (), s32[]{:S(2)}) async-start(), calls=%async_computation.15 | async-start | bytes 2621440 | tf_op jit(solution)/shard_map/reduce_scatter | solution.py:271
  725.4 405.5 %reduce-scatter.19.cloned.1.call-start = ((), (), s32[]{:S(2)}) async-start(), calls=%async_computation.13 | async-start | bytes 2621440 | tf_op jit(solution)/shard_map/reduce_scatter | solution.py:270
  894.2 15.1 %copy-start.77 = (u32[32]{0:T(128)S(1)}, u32[32]{0:T(128)}, u32[]{:S(2)}) copy-start(u32[32]{0:T(128)} %constant.185) | copy-start | bytes 388
  894.2 271.3 %reduce-scatter.11.cloned.1.call-start = ((), (), s32[]{:S(2)}) async-start(), calls=%async_computation.9 | async-start | bytes 1966080 | tf_op jit(solution)/shard_map/reduce_scatter | solution.py:268
  918.1 105.9 %copy-start.53 = (f32[1,2,4,128]{3,1,2,0:T(2,128)S(1)}, f32[1,2,4,128]{3,1,2,0:T(2,128)}, u32[]{:S(2)}) copy-start(f32[1,2,4,128]{3,1,2,0:T(2,128)} %copy-done.52) | copy-start | bytes 12292
  918.1 105.9 %copy-start.57 = (f32[1024]{0:T(1024)S(1)}, f32[1024]{0:T(1024)}, u32[]{:S(2)}) copy-start(f32[1024]{0:T(1024)} %param.28) | copy-start | bytes 12292
  918.1 105.9 %copy-start.59 = (f32[1024]{0:T(1024)S(1)}, f32[1024]{0:T(1024)}, u32[]{:S(2)}) copy-start(f32[1024]{0:T(1024)} %param.26) | copy-start | bytes 12292
  1083.3 82.2 %copy-start.76 = (f32[128]{0:T(128)}, f32[128]{0:T(128)S(1)}, u32[]{:S(2)}) copy-start(f32[128]{0:T(128)S(1)} %get-tuple-element.580) | copy-start | bytes 1540
  (65 other events, 329.3 us)
Sparse Core Ops, SparseCore 0:
  144.3 152.4 all-gather.6
  355.5 149.3 all-gather.8
  507.2 49.5 reduce-scatter.12
  559.0 166.3 reduce-scatter.20
  727.6 166.5 reduce-scatter.16
  896.4 127.5 reduce-scatter.8
  1027.4 25.6 reduce-scatter.14
  1056.9 35.1 reduce-scatter.22
  1095.7 35.1 reduce-scatter.18
  1134.6 30.9 reduce-scatter.10
where the time goes:
time: 1190 us; the launch traced here: 1170 us
  waiting for transfers between devices  474 us (40%)
  matrix products  341 us (29%)
  local copies, waits for them, and re-layouts  159 us (13%)
  other arithmetic  112 us (9%)
  blocking collectives  68.6 us (6%)
  between operations  17.4 us (1%)
    reduce_scatter x1, waiting for transfers between devices, per_device(): lax.psum_scatter(grad_w_up, 'seq', scatter_dimension=0, tiled=True)  169 us
    reduce_scatter x1, waiting for transfers between devices, per_device(): lax.psum_scatter(grad_w_qkv, 'seq', scatter_dimension=0, tiled=True)  91 us
    all_gather x2, waiting for transfers between devices, carried_in(): everything = jax.tree.map(lambda part: lax.all_gather(part, axis), value)  78.6 us
    unnamed x180, local copies, waits for them, and re-layouts  74.4 us
    select_n x32, other arithmetic, turn(): return jax.tree.map(lambda a, b: jnp.where(reached, a, b), new, before)  72.7 us
    reduce_scatter x1, waiting for transfers between devices, per_device(): lax.psum_scatter(grad_w_down, 'seq', scatter_dimension=0, tiled=True)  60.4 us
    dot_general x1, matrix products, per_device(): jnp.einsum('re,fe->rf', grad_out, w_down, preferred_element_type=jnp.floa...  52 us
    reduce_scatter x1, waiting for transfers between devices, per_device(): lax.psum_scatter(parts[2], 'batch', scatter_dimension=1, tiled=True)  38.8 us
  transfers between devices with their start and end apart: 10, of which 7 were waited for; matrix products, arithmetic and copies ran while one was open for 34% of the time, Pallas kernels for 0%

commit v1 on v0

v1 whole, which is shorter than its diff:
```python
import functools
import math

import jax
import jax.numpy as jnp
from jax import lax
from jax.experimental import pallas as pl
from jax.experimental.pallas import tpu as pltpu
from jax.sharding import PartitionSpec as P

f32 = jnp.float32
bf16 = jnp.bfloat16
struct = jax.ShapeDtypeStruct
HEADS = 16
HEAD_DIM = 64
ROT = 16
LEN_BLK = 256
HG = 256
ROOT_HALF = math.sqrt(0.5)
NORMAL_PEAK = 1.0 / math.sqrt(2.0 * math.pi)
norm_epsilon = 1e-05
rope_base = 10000.0
VMEM_BYTES = 60 * 1024 * 1024


def params():
    return pltpu.CompilerParams(vmem_limit_bytes=VMEM_BYTES)


def dot(a, b, ca, cb):
    return lax.dot_general(a, b, (((ca,), (cb,)), ((), ())), preferred_element_type=f32)


def iota(shape, dim):
    return lax.broadcasted_iota(jnp.int32, shape, dim)


def split(x):
    hi = x.astype(bf16)
    return hi, (x - hi.astype(f32)).astype(bf16)


def split_outside(x):
    hi = lax.reduce_precision(x, 8, 7)
    return hi.astype(bf16), (x - hi).astype(bf16)


def ffn_kernel(aliased, pos, a2, g, wu0, wu1, wd0, wd1, bu0, bu1, *refs):
    refs = refs[4:] if aliased else refs
    gelu_a, gelu_b, gp_a, gp_b, up_send, up_keep, down_send, down_keep, b_sum = refs
    me, core = pos[0], pos[1]
    rows_in = a2[...]
    grad_in = g[...]
    w_up = jnp.concatenate([wu0[...], wu1[...]], axis=1)
    w_down = jnp.concatenate([wd0[...], wd1[...]], axis=0)
    bias = jnp.concatenate([bu0[...], bu1[...]], axis=1)
    pre = dot(rows_in, w_up, 1, 0) + bias
    grad_gelu = dot(grad_in, w_down, 1, 1)
    cdf = 0.5 + 0.5 * lax.erf(pre * ROOT_HALF)
    gelu = (pre * cdf).astype(bf16)
    grad_pre = (grad_gelu * (cdf + pre * (NORMAL_PEAK * jnp.exp(-0.5 * pre * pre)))).astype(bf16)
    gelu_a[...] = gelu[:, :128]
    gelu_b[...] = gelu[:, 128:]
    gp_a[...] = grad_pre[:, :128]
    gp_b[...] = grad_pre[:, 128:]
    b_sum[0] = jnp.sum(grad_pre.astype(f32), axis=0, keepdims=True)
    d_up = dot(grad_pre, rows_in, 0, 0)
    d_down = dot(gelu, grad_in, 0, 0)

    def put(c):
        for z in range(4):
            up_send[0, 0, z] = d_up[:, (2 * z + 1 - c) * 128 : (2 * z + 2 - c) * 128]
            up_keep[0, 0, z] = d_up[:, (2 * z + c) * 128 : (2 * z + c + 1) * 128]
        for b in range(4):
            rel = lax.bitwise_xor(jnp.int32(b), me)
            rx, ry = lax.rem(rel, 2), lax.div(rel, 2)
            down_send[ry, rx, 0] = d_down[(1 - c) * 128 : (2 - c) * 128, b * 256 : (b + 1) * 256]
            down_keep[ry, rx, 0] = d_down[c * 128 : (c + 1) * 128, b * 256 : (b + 1) * 256]

    pl.when(core == 0)(lambda: put(0))
    pl.when(core == 1)(lambda: put(1))


def ffn_chunk(first, count, pos, a2, g, w_up, w_down, b_up, earlier):
    rows, width = a2.shape
    hidden = w_up.shape[1]
    cols = lambda j: (lambda k, b, p: (0, (2 * b + j) * 4 + first + k))
    lines = lambda j: (lambda k, b, p: ((2 * b + j) * 4 + first + k, 0))
    whole = lambda k, b, p: (0, 0)
    place = lambda k, b, p: (0, b * 4 + first + k)

    def up_place(k, b, p):
        rel = lax.bitwise_xor(b, p[0])
        return (lax.rem(rel, 2), lax.div(rel, 2), 0, k, 0)

    down_place = lambda k, b, p: (0, 0, b, k, 0)
    in_specs = (
        [pl.BlockSpec((rows, width), whole)] * 2
        + [pl.BlockSpec((width, 128), cols(j)) for j in range(2)]
        + [pl.BlockSpec((128, width), lines(j)) for j in range(2)]
        + [pl.BlockSpec((1, 128), cols(j)) for j in range(2)]
    )
    args = [pos, a2, g, w_up, w_up, w_down, w_down, b_up, b_up]
    aliases = {}
    if earlier is not None:
        aliases = {len(args) + i: i for i in range(4)}
        in_specs = in_specs + [pl.BlockSpec(memory_space=pl.ANY)] * 4
        args = args + list(earlier)
    return pl.pallas_call(
        functools.partial(ffn_kernel, earlier is not None),
        grid_spec=pltpu.PrefetchScalarGridSpec(
            num_scalar_prefetch=1,
            grid=(count, 4),
            in_specs=in_specs,
            out_specs=[pl.BlockSpec((rows, 128), place)] * 4
            + [pl.BlockSpec((1, 1, 4, 256, 128), up_place)] * 2
            + [pl.BlockSpec((2, 2, 1, 128, 256), down_place)] * 2
            + [pl.BlockSpec((1, 1, 256), lambda k, b, p: (k * 4 + b, 0, 0))],
        ),
        out_shape=[struct((rows, hidden // 2), bf16)] * 4
        + [struct((2, 2, 4, count * 256, 128), f32)] * 2
        + [struct((2, 2, 4, count * 128, 256), f32)] * 2
        + [struct((count * 4, 1, 256), f32)],
        input_output_aliases=aliases,
        compiler_params=params(),
        cost_estimate=pl.CostEstimate(
            flops=8 * rows * width * 1024 * count,
            bytes_accessed=(4 + 20 * count) * 2**20,
            transcendentals=2 * rows * 1024 * count,
        ),
        name="ffn_chunk",
    )(*args)


def wgrad_kernel(pos, left, right, send, keep):
    tile = dot(left[...], right[0], 0, 0)
    core = pos[1]

    def put(c):
        for z in range(4):
            send[0, 0, z, 0] = tile[(2 * z + 1 - c) * 128 : (2 * z + 2 - c) * 128]
            keep[0, 0, z, 0] = tile[(2 * z + c) * 128 : (2 * z + c + 1) * 128]

    pl.when(core == 0)(lambda: put(0))
    pl.when(core == 1)(lambda: put(1))


def wgrad(pos, left, right, units, y_first):
    rows, width = left.shape
    per = len(units)

    def source(b, j, p):
        unit = b * 3 + units[0] + j if units is not WHOLE else b
        return (lax.div(unit, 4), 0, lax.rem(unit, 4))

    def target(b, j, p):
        rel = lax.bitwise_xor(b, p[0])
        rx, ry = lax.rem(rel, 2), lax.div(rel, 2)
        return (ry, rx, 0, j, 0, 0) if y_first else (rx, ry, 0, j, 0, 0)

    return pl.pallas_call(
        wgrad_kernel,
        grid_spec=pltpu.PrefetchScalarGridSpec(
            num_scalar_prefetch=1,
            grid=(4, per),
            in_specs=[
                pl.BlockSpec((rows, width), lambda b, j, p: (0, 0)),
                pl.BlockSpec((1, rows, 256), source),
            ],
            out_specs=[pl.BlockSpec((1, 1, 4, 1, 128, 256), target)] * 2,
        ),
        out_shape=[struct((2, 2, 4, per, 128, 256), f32)] * 2,
        compiler_params=params(),
        cost_estimate=pl.CostEstimate(
            flops=2 * rows * width * 1024 * per,
            bytes_accessed=(2 + 6 * per) * 2**20,
            transcendentals=0,
        ),
        name="wgrad",
    )(pos, left, right)


WHOLE = (0,)


def rotate(x, cos, sin_first, sin_second):
    n = x.shape[1]
    half = ROT // 2
    return x * cos + pltpu.roll(x, n - half, 1) * sin_first + pltpu.roll(x, half, 1) * sin_second


def three(x, w_hi, w_lo):
    hi, lo = split(x)
    return dot(hi, w_hi, 1, 0) + dot(lo, w_hi, 1, 0) + dot(hi, w_lo, 1, 0)


def pair_mask():
    return (iota((128, 128), 0) // 64) == (iota((128, 128), 1) // 64)


def pack(first, second):
    mask = pair_mask()
    first = jnp.where(mask, first, 0.0)
    second = jnp.where(mask, second, 0.0)
    first = first + pltpu.roll(first, 64, 1)
    second = second + pltpu.roll(second, 64, 1)
    return jnp.where(iota((128, 128), 1) < 64, first, second)


def unpack(packed):
    mask = pair_mask()
    low = iota((128, 128), 1) < 64
    turned = pltpu.roll(packed, 64, 1)
    return (
        jnp.where(mask, jnp.where(low, packed, turned), 0.0),
        jnp.where(mask, jnp.where(low, turned, packed), 0.0),
    )


def to_column(row):
    eye = iota((128, 128), 0) == iota((128, 128), 1)
    return jnp.sum(jnp.where(eye, jnp.broadcast_to(row, (128, 128)), 0.0), axis=1, keepdims=True)


def each_head(x):
    mask = iota((1, 128), 1) < 64
    zero = jnp.zeros_like(x)
    return jnp.where(mask, x, zero), jnp.where(mask, zero, x)


def feature_kernel(
    a1, wq, wk, wv, bq, bk, bv, fw, m_hi, m_lo, cos, sin1, sin2, valid, qf_o, kf_o, v_o, st_o
):
    x = a1[...]
    count = x.shape[0] // LEN_BLK
    turns = [jnp.concatenate([t[...]] * count, 0) for t in (cos, sin1, sin2)]
    q = dot(x, wq[...], 1, 0) + bq[...]
    k = dot(x, wk[...], 1, 0) + bk[...]
    v = (dot(x, wv[...], 1, 0) + bv[...]).astype(bf16)
    weight = fw[...]
    qf = (weight * jnp.exp(three(rotate(q, *turns), m_hi[...], m_lo[...]))).astype(bf16)
    kf = (weight * jnp.exp(three(rotate(k, *turns), m_hi[...], m_lo[...]))).astype(bf16)
    kf = kf * valid[...].astype(bf16)
    qf_o[...] = qf
    kf_o[...] = kf
    v_o[...] = v
    for i in range(count):
        r = slice(LEN_BLK * i, LEN_BLK * (i + 1))
        state = [
            dot(kf[r, 128 * p : 128 * p + 128], v[r, 128 * p : 128 * p + 128], 0, 0)
            for p in range(2)
        ]
        st_o[i, 0, :128] = pack(state[0], state[1])
        norm = jnp.sum(kf[r].astype(f32), axis=0, keepdims=True)
        st_o[i, 0, 128:] = norm_rows(norm[:, :128], norm[:, 128:])


def norm_rows(first, second):
    line = iota((8, 128), 0)
    return jnp.where(line == 0, first, jnp.where(line == 1, second, 0.0))


def scores(qp, kp, causal):
    return [jnp.where(causal, dot(qh, kp, 1, 1), 0.0).astype(bf16) for qh in each_head(qp)]


def lower(n):
    return iota((n, n), 0) >= iota((n, n), 1)


def mix_kernel(g, wo, qf, kf, v, st, mix_o, dn_o, dd_o, ds_o):
    count = qf.shape[0] // LEN_BLK
    grad_mixed = dot(g[...], wo[...], 1, 1)
    mask = pair_mask()
    lane = iota((1, 128), 1)
    first = lane < 64
    causal = lower(LEN_BLK)
    one0, one1 = each_head(jnp.ones((LEN_BLK, 128), bf16))
    for i in range(count):
        r = slice(LEN_BLK * i, LEN_BLK * (i + 1))
        state = unpack(st[i, 0, :128])
        grads, norms = [], []
        dd_lines = jnp.zeros((LEN_BLK, 128), f32)
        for p in range(2):
            sl = slice(128 * p, 128 * p + 128)
            qp, kp, vp = qf[r, sl], kf[r, sl], v[r, sl]
            s0, s1 = scores(qp, kp, causal)
            v0, v1 = each_head(vp)
            right = jnp.concatenate(
                [jnp.concatenate([v0, one0], 1), jnp.concatenate([v1, one1], 1)], 0
            )
            both = dot(jnp.concatenate([s0, s1], 1), right, 1, 0)
            column = to_column(st[i, 0, 128 + p : 129 + p])
            norm = jnp.where(mask, jnp.broadcast_to(column, (128, 128)), 0.0)
            hi, lo = split(jnp.concatenate([state[p], norm], 1))
            both = both + dot(jnp.concatenate([qp, qp], 1), jnp.concatenate([hi, lo], 0), 1, 0)
            inverse = 1.0 / both[:, 128:]
            mixed = both[:, :128] * inverse
            mix_o[r, sl] = mixed.astype(bf16)
            dn = (grad_mixed[r, sl] * inverse).astype(bf16)
            dn_o[r, sl] = dn
            product = -(dn.astype(f32) * mixed)
            d0 = jnp.sum(jnp.where(first, product, 0.0), axis=1, keepdims=True)
            d1 = jnp.sum(jnp.where(first, 0.0, product), axis=1, keepdims=True)
            dd_lines = jnp.where(
                lane == 2 * p, d0, jnp.where(lane == 2 * p + 1, d1, dd_lines)
            )
            grads.append(dot(qp, dn, 0, 0))
            norms.append(
                jnp.sum(qp.astype(f32) * jnp.where(first, d0, d1), axis=0, keepdims=True)
            )
        dd_o[0, r] = dd_lines
        ds_o[i, 0, :128] = pack(grads[0], grads[1])
        ds_o[i, 0, 128:] = norm_rows(norms[0], norms[1])


def back_kernel(
    qf, kf, v, dn, dd, st, ds, fw, m_hi, m_lo, cos, sin1, sin2, gp_o, bias_o, fw_o
):
    count = qf.shape[0] // LEN_BLK
    step = pl.program_id(1)
    causal = lower(LEN_BLK)
    lane = iota((1, 128), 1)
    first = lane < 64
    turns = cos[...], -sin1[...], -sin2[...]
    totals = None
    for i in range(count):
        r = slice(LEN_BLK * i, LEN_BLK * (i + 1))
        state, later = unpack(st[i, 0, :128]), unpack(ds[i, 0, :128])
        dq, dk, dv = [], [], []
        for p in range(2):
            sl = slice(128 * p, 128 * p + 128)
            qp, kp, vp, np_ = qf[r, sl], kf[r, sl], v[r, sl], dn[r, sl]
            s = scores(qp, kp, causal)
            dn_heads = each_head(np_)
            column = [
                jnp.sum(jnp.where(lane == 2 * p + h, dd[0, r], 0.0), axis=1, keepdims=True)
                for h in range(2)
            ]
            t = [
                jnp.where(causal, dot(dn_heads[h], vp, 1, 1) + column[h], 0.0).astype(bf16)
                for h in range(2)
            ]
            s_hi, s_lo = split(state[p])
            d_hi, d_lo = split(later[p])
            dqf = dot(jnp.concatenate(t, 1), jnp.concatenate(each_head(kp), 0), 1, 0)
            dqf = dqf + dot(
                jnp.concatenate([np_, np_], 1), jnp.concatenate([s_hi, s_lo], 1), 1, 1
            )
            dqf = dqf + jnp.where(first, column[0], column[1]) * st[i, 0, 128 + p : 129 + p]
            dkf = dot(jnp.concatenate(t, 0), jnp.concatenate(each_head(qp), 0), 0, 0)
            dkf = dkf + dot(
                jnp.concatenate([vp, vp], 1), jnp.concatenate([d_hi, d_lo], 1), 1, 1
            )
            dkf = dkf + ds[i, 0, 128 + p : 129 + p]
            dvv = dot(jnp.concatenate(s, 0), jnp.concatenate(dn_heads, 0), 0, 0)
            dvv = dvv + dot(
                jnp.concatenate([kp, kp], 1), jnp.concatenate([d_hi, d_lo], 0), 1, 0
            )
            dq.append(dqf * qp.astype(f32))
            dk.append(dkf * kp.astype(f32))
            dv.append(dvv)
        dq = jnp.concatenate(dq, 1)
        dk = jnp.concatenate(dk, 1)
        grads = (
            rotate(three(dq, m_hi[...], m_lo[...]), *turns).astype(bf16),
            rotate(three(dk, m_hi[...], m_lo[...]), *turns).astype(bf16),
            jnp.concatenate(dv, 1).astype(bf16),
        )
        for n in range(3):
            gp_o[n, r] = grads[n]
        sums = [jnp.sum(part.astype(f32), axis=0, keepdims=True) for part in grads]
        sums.append(jnp.sum(dq + dk, axis=0, keepdims=True) / fw[...])
        totals = sums if totals is None else [a + b for a, b in zip(totals, sums)]

    @pl.when(step == 0)
    def _():
        for n in range(3):
            bias_o[n] = totals[n]
        fw_o[...] = totals[3]

    @pl.when(step > 0)
    def _():
        for n in range(3):
            bias_o[n] = bias_o[n] + totals[n]
        fw_o[...] = fw_o[...] + totals[3]


def attention_specs(seqs, per):
    rows = LEN_BLK * per
    return dict(
        grid=(4, seqs // per),
        wide=pl.BlockSpec((rows, 1024), lambda h, g: (g, 0)),
        head=pl.BlockSpec((rows, HG), lambda h, g: (g, h)),
        state=pl.BlockSpec((per, 1, 136, 128), lambda h, g: (g, h, 0, 0)),
        row=pl.BlockSpec((1, HG), lambda h, g: (0, h)),
        table=pl.BlockSpec((256, 256), lambda h, g: (0, 0)),
        dden=pl.BlockSpec((1, rows, 128), lambda h, g: (h, g, 0)),
    )


def cost(giga, mega):
    return pl.CostEstimate(
        flops=int(giga * 1e9), bytes_accessed=mega * 2**20, transcendentals=0
    )


def features(a1, w_qkv, b_qkv, feat_weight, tables, turns, valid, per=4):
    rows = a1.shape[0]
    seqs = rows // LEN_BLK
    s = attention_specs(seqs, per)
    weights = [pl.BlockSpec((1024, HG), lambda h, g, o=o: (0, 4 * o + h)) for o in range(3)]
    biases = [pl.BlockSpec((1, HG), lambda h, g, o=o: (0, 4 * o + h)) for o in range(3)]
    return pl.pallas_call(
        feature_kernel,
        grid=s["grid"],
        in_specs=[s["wide"], *weights, *biases, s["row"]]
        + [s["table"]] * 5
        + [pl.BlockSpec((LEN_BLK * per, 1), lambda h, g: (g, 0))],
        out_specs=[s["head"]] * 3 + [s["state"]],
        out_shape=[struct((rows, 1024), bf16)] * 3 + [struct((seqs, 4, 136, 128), f32)],
        compiler_params=params(),
        cost_estimate=cost(15, 20),
        name="features",
    )(a1, w_qkv, w_qkv, w_qkv, b_qkv, b_qkv, b_qkv, feat_weight, *tables, *turns, valid)


def mixing(g, w_out, qf, kf, v, state, per=2):
    rows = g.shape[0]
    seqs = rows // LEN_BLK
    s = attention_specs(seqs, per)
    return pl.pallas_call(
        mix_kernel,
        grid=s["grid"],
        in_specs=[s["wide"], pl.BlockSpec((HG, 1024), lambda h, g: (h, 0))]
        + [s["head"]] * 3
        + [s["state"]],
        out_specs=[s["head"]] * 2 + [s["dden"], s["state"]],
        out_shape=[struct((rows, 1024), bf16)] * 2
        + [struct((4, rows, 128), f32), struct((seqs, 4, 136, 128), f32)],
        compiler_params=params(),
        cost_estimate=cost(16, 20),
        name="mixing",
    )(g, w_out, qf, kf, v, state)


def backward(qf, kf, v, dn, dd, state, later, feat_weight, tables, turns, per=4):
    rows = qf.shape[0]
    seqs = rows // LEN_BLK
    s = attention_specs(seqs, per)
    return pl.pallas_call(
        back_kernel,
        grid=s["grid"],
        in_specs=[s["head"]] * 4
        + [s["dden"], s["state"], s["state"], s["row"]]
        + [s["table"]] * 5,
        out_specs=[
            pl.BlockSpec((3, LEN_BLK * per, HG), lambda h, g: (0, g, h)),
            pl.BlockSpec((3, 1, HG), lambda h, g: (0, 0, h)),
            s["row"],
        ],
        out_shape=[struct((3, rows, 1024), bf16), struct((3, 1, 1024), f32), struct((1, 1024), f32)],
        compiler_params=params(),
        cost_estimate=cost(20, 24),
        name="backward",
    )(qf, kf, v, dn, dd, state, later, feat_weight, *tables, *turns)


def norm_parts(x):
    centre = x - jnp.mean(x, axis=-1, keepdims=True)
    r = lax.rsqrt(jnp.mean(centre * centre, axis=-1, keepdims=True) + norm_epsilon)
    return centre * r, r


def norm_back(grad, xhat, r, gain):
    e = grad * gain
    return r * (
        e
        - jnp.mean(e, axis=-1, keepdims=True)
        - xhat * jnp.mean(e * xhat, axis=-1, keepdims=True)
    )


def add_sums(out, sums):
    step = pl.program_id(0)
    new = jnp.concatenate(sums, 0)

    @pl.when(step == 0)
    def _():
        out[...] = new

    @pl.when(step > 0)
    def _():
        out[...] = out[...] + new


def column_sum(x):
    return jnp.sum(x, axis=0, keepdims=True)


def in_order(a, b):
    parts = []
    for n in range(4):
        parts += [a[:, 512 * n : 512 * n + 512], b[:, 512 * n : 512 * n + 512]]
    return jnp.concatenate(parts, axis=1)


def ends_kernel(
    x, g, mixed, gelu_a, gelu_b, gp_a, gp_b, w_out, w_down, w_up, bias, gain, res_o, part_o, sum_o
):
    value = x[...].astype(f32)
    out = dot(mixed[...], w_out[...], 1, 0)
    out = out + dot(in_order(gelu_a[...], gelu_b[...]), w_down[...], 1, 0)
    res_o[...] = (value + out + bias[...]).astype(bf16)
    grad = dot(in_order(gp_a[...], gp_b[...]), w_up[...], 1, 1)
    xhat, r = norm_parts(value)
    grad_res = g[...].astype(f32)
    part_o[...] = grad_res + norm_back(grad, xhat, r, gain[...])
    zero = jnp.zeros((5, 1024), f32)
    add_sums(sum_o, [column_sum(grad * xhat), column_sum(grad), column_sum(grad_res), zero])


def ends(x, g, mixed, gelu_a, gelu_b, gp_a, gp_b, w_out, w_down, w_up, bias, gain):
    rows = x.shape[0]
    tile = 256
    wide = lambda n: pl.BlockSpec((tile, n), lambda i: (i, 0))
    fixed = lambda a: pl.BlockSpec(a.shape, lambda i: (0, 0), pipeline_mode=pl.Buffered(1))
    return pl.pallas_call(
        ends_kernel,
        grid=(rows // tile,),
        in_specs=[wide(1024)] * 3
        + [wide(2048)] * 4
        + [fixed(a) for a in (w_out, w_down, w_up, bias, gain)],
        out_specs=[wide(1024), wide(1024), pl.BlockSpec((8, 1024), lambda i: (0, 0))],
        out_shape=[struct((rows, 1024), bf16), struct((rows, 1024), f32), struct((8, 1024), f32)],
        compiler_params=params(),
        cost_estimate=cost(19, 48),
        name="ends",
    )(x, g, mixed, gelu_a, gelu_b, gp_a, gp_b, w_out, w_down, w_up, bias, gain)


def last_kernel(x, part, gp, w_qkv, gain, out_o, sum_o):
    value = x[...].astype(f32)
    grad = dot(jnp.concatenate([gp[0], gp[1], gp[2]], 1), w_qkv[...], 1, 1)
    xhat, r = norm_parts(value)
    out_o[...] = part[...] + norm_back(grad, xhat, r, gain[...])
    zero = jnp.zeros((6, 1024), f32)
    add_sums(sum_o, [column_sum(grad * xhat), column_sum(grad), zero])


def last(x, part, gp, w_qkv, gain):
    rows = x.shape[0]
    tile = 256
    wide = pl.BlockSpec((tile, 1024), lambda i: (i, 0))
    fixed = lambda a: pl.BlockSpec(a.shape, lambda i: (0, 0), pipeline_mode=pl.Buffered(1))
    return pl.pallas_call(
        last_kernel,
        grid=(rows // tile,),
        in_specs=[
            wide,
            wide,
            pl.BlockSpec((3, tile, 1024), lambda i: (0, i, 0)),
            fixed(w_qkv),
            fixed(gain),
        ],
        out_specs=[wide, pl.BlockSpec((8, 1024), lambda i: (0, 0))],
        out_shape=[struct((rows, 1024), f32), struct((8, 1024), f32)],
        compiler_params=params(),
        cost_estimate=cost(6.4, 22),
        name="last",
    )(x, part, gp, w_qkv, gain)


class Links:
    def __init__(self, mesh):
        self.nb, self.ns = mesh.shape["batch"], mesh.shape["seq"]
        self.tuned = (self.nb, self.ns) == (4, 8)

    def send(self, value, move):
        pairs = []
        for b in range(self.nb):
            for s in range(self.ns):
                to = move(b, s)
                if to is not None:
                    pairs.append((b * self.ns + s, to[0] * self.ns + to[1]))
        return lax.ppermute(value, ("batch", "seq"), pairs)

    def core(self, value):
        return self.send(value, lambda b, s: (b, s ^ 1))

    def x(self, value):
        return self.send(value, lambda b, s: (b ^ 1, s))

    def y(self, value):
        return self.send(value, lambda b, s: (b ^ 2, s))

    def shift(self, value, by):
        inside = lambda s: 0 <= s < self.ns
        return self.send(value, lambda b, s: (b, s + by) if inside(s + by) else None)


def reduce_pairs(links, send, keep, y_first):
    first, second = (links.y, links.x) if y_first else (links.x, links.y)
    got = links.core(send)
    one = first(keep[1] + got[1])
    two = second(keep[0, 1] + got[0, 1] + one[1])
    return keep[0, 0] + got[0, 0] + one[0] + two


def reduce_z(value):
    groups = [[0, 2, 4, 6], [1, 3, 5, 7]]
    return lax.psum_scatter(
        value, "seq", scatter_dimension=0, axis_index_groups=groups, tiled=True
    )[0]


def carried(links, state, reverse):
    sign = -1 if reverse else 1
    if not links.tuned:
        total, step = state, 1
        while step < links.ns:
            total = total + links.shift(total, sign * step)
            step *= 2
        return links.shift(total, sign)
    core = lax.rem(lax.axis_index("seq"), 2)
    other = links.core(state)
    half = state.shape[0] // 2
    mine = lax.dynamic_slice_in_dim(state, core * half, half, 0)
    mine = mine + lax.dynamic_slice_in_dim(other, core * half, half, 0)
    near = links.shift(mine, sign * 2)
    far = links.shift(mine + near, sign * 4)
    before = near + far
    rest = links.core(before)
    low = jnp.where(core == 0, before, rest)
    high = jnp.where(core == 0, rest, before)
    whole = jnp.concatenate([low, high], 0)
    behind = core == (0 if reverse else 1)
    return whole + jnp.where(behind, other, 0.0)


def dct_table(order):
    degree = jnp.arange(order, dtype=f32)[:, None]
    sample = jnp.arange(order, dtype=f32)[None, :]
    table = jnp.cos(math.pi * (sample + 0.5) * degree / order) * math.sqrt(2.0 / order)
    return jnp.where(degree == 0.0, table * math.sqrt(0.5), table)


def rotation_tables(positions):
    half = ROT // 2
    inverse = rope_base ** (-2.0 * jnp.arange(half, dtype=f32) / ROT)
    angles = positions[:, None] * inverse[None, :]
    cos, sin = jnp.cos(angles), jnp.sin(angles)
    rest = jnp.zeros((positions.shape[0], HEAD_DIM - ROT), f32)
    zero = jnp.zeros_like(cos)
    rows = ([cos, cos, rest + 1.0], [-sin, zero, rest], [zero, sin, rest])
    return tuple(jnp.tile(jnp.concatenate(r, 1), (1, HG // HEAD_DIM)) for r in rows)


def four_blocks(matrix):
    return jnp.kron(jnp.eye(HG // HEAD_DIM, dtype=f32), matrix)


def per_device(
    links,
    hidden_in,
    cotangent,
    lengths,
    key_mask,
    ln1_gain,
    ln1_bias,
    ln2_gain,
    ln2_bias,
    w_qkv,
    b_qkv,
    w_out,
    b_out,
    w_up,
    b_up,
    w_down,
    b_down,
    feat_weight,
    directions,
):
    seqs, block, width = hidden_in.shape
    rows = seqs * block
    tuned = links.tuned
    place = lax.axis_index("seq")
    if tuned:
        pos = jnp.stack([lax.axis_index("batch"), lax.rem(place, 2)]).astype(jnp.int32)
    else:
        pos = jnp.zeros((2,), jnp.int32)
    places = place * block + jnp.arange(block, dtype=jnp.int32)
    valid = (places[None, :] < lengths[:, None]) & ((key_mask == 1) | (places[None, :] == 0))
    valid = valid.astype(f32).reshape(rows, 1)
    x = hidden_in.reshape(rows, width)
    g = cotangent.reshape(rows, width)
    xhat, _ = norm_parts(x.astype(f32))
    a2 = (xhat * ln2_gain + ln2_bias).astype(bf16)
    a1 = (xhat * ln1_gain + ln1_bias).astype(bf16)
    row = lambda v: v.reshape(1, -1)

    table = jnp.dot(directions, dct_table(HEAD_DIM), precision=lax.Precision.HIGHEST)
    forth = split_outside(four_blocks(table.T))
    back = split_outside(four_blocks(table))
    turns = rotation_tables(places.astype(f32))

    ffn = functools.partial(ffn_chunk, pos=pos, a2=a2, g=g, w_up=w_up, w_down=w_down, b_up=row(b_up))
    chunks = []
    earlier = None
    for first, count in ((0, 1), (1, 1), (2, 2)):
        out = ffn(first, count, earlier=earlier)
        earlier = out[:4]
        chunks.append(out[4:])

    qf, kf, v, state = features(a1, w_qkv, row(b_qkv), row(feat_weight), forth, turns, valid)
    state_in = carried(links, state, False)
    mixed, dn, dd, state_grad = mixing(g, w_out, qf, kf, v, state_in)
    state_later = carried(links, state_grad, True)
    out_pair = wgrad(pos, mixed, g[None], WHOLE, False)
    result, partial, sums2 = ends(
        x, g, mixed, *earlier, w_out, w_down, w_up, row(b_out + b_down), row(ln2_gain)
    )
    grad_proj, bias_qkv, grad_feat = backward(
        qf, kf, v, dn, dd, state_in, state_later, row(feat_weight), back, turns
    )
    qkv_pairs = [wgrad(pos, a1, grad_proj, (j,), j != 1) for j in range(3)]
    grad_input, sums1 = last(x, partial, grad_proj, w_qkv, row(ln1_gain))

    b_up_parts = [c[4].reshape(-1, 4, 2, 128) for c in chunks]
    b_up_grad = jnp.concatenate(b_up_parts, 0).transpose(1, 2, 0, 3).reshape(-1)
    vectors = [sums1[0], sums1[1], sums2[0], sums2[1], bias_qkv.reshape(-1), sums2[2], b_up_grad, grad_feat[0]]
    sizes = [v_.shape[0] for v_ in vectors]
    total = lax.psum(jnp.concatenate(vectors), ("batch", "seq"))
    shares, at = [], 0
    for n in sizes:
        share = n // links.ns
        shares.append(lax.dynamic_slice_in_dim(total, at + place * share, share, 0))
        at += n

    if tuned:
        ups, downs = [], []
        for c in chunks:
            u = reduce_pairs(links, c[0], c[1], False)
            d = reduce_pairs(links, c[2], c[3], True)
            n = u.shape[1] // 256
            both = jnp.concatenate([u, d[..., :128], d[..., 128:]], 1)
            both = reduce_z(both)
            ups.append(both[: n * 256].reshape(n, 2, 128, 128))
            downs.append(jnp.concatenate([both[n * 256 : n * 384], both[n * 384 :]], 1))
        w_up_grad = jnp.concatenate(ups, 0).transpose(3, 1, 0, 2).reshape(128, 1024)
        w_down_grad = jnp.concatenate(downs, 0)
        pairs = [reduce_pairs(links, *out_pair, False)] + [
            reduce_pairs(links, *p, j != 1) for j, p in enumerate(qkv_pairs)
        ]
        w_out_grad = reduce_z(pairs[0]).reshape(128, 256)
        w_qkv_grad = jnp.concatenate([reduce_z(p).reshape(128, 256) for p in pairs[1:]], 1)
    else:

        def scatter(full):
            part = lax.psum_scatter(full, "batch", scatter_dimension=1, tiled=True)
            return lax.psum_scatter(part, "seq", scatter_dimension=0, tiled=True)

        ups = [jnp.stack([c[1], c[0]], 3).reshape(2, 2, 4, 2, -1, 2, 128, 128) for c in chunks]
        up = jnp.concatenate(ups, 4)
        up = up.transpose(2, 3, 7, 1, 0, 5, 4, 6).reshape(1024, 4096)
        downs = [jnp.stack([c[3], c[2]], 3).reshape(2, 2, 4, 2, -1, 128, 256) for c in chunks]
        down = jnp.concatenate(downs, 4)
        down = down.transpose(2, 3, 4, 5, 0, 1, 6).reshape(4096, 1024)

        def square(pair, y_first):
            both = jnp.stack([pair[1], pair[0]], 3)
            order = (2, 3, 4, 5, 0, 1, 6) if y_first else (2, 3, 4, 5, 1, 0, 6)
            return both.transpose(order).reshape(1024, 4, 256)

        w_out_full = square(out_pair, False).reshape(1024, 1024)
        qkv = jnp.stack([square(p, j != 1) for j, p in enumerate(qkv_pairs)], 2)
        w_up_grad, w_down_grad = scatter(up), scatter(down)
        w_out_grad, w_qkv_grad = scatter(w_out_full), scatter(qkv.reshape(1024, 3072))

    shape = hidden_in.shape
    return (
        result.reshape(shape),
        grad_input.reshape(shape),
        shares[0],
        shares[1],
        shares[2],
        shares[3],
        w_qkv_grad,
        shares[4],
        w_out_grad,
        shares[5],
        w_up_grad,
        shares[6],
        w_down_grad,
        shares[5],
        shares[7],
    )


def solution(mesh):
    links = Links(mesh)
    rows = P("batch", "seq", None)
    spread = P("seq", "batch")
    return jax.shard_map(
        functools.partial(per_device, links),
        mesh=mesh,
        in_specs=(rows, rows, P("batch"), P("batch", "seq")) + (P(),) * 14,
        out_specs=(rows, rows)
        + (P("seq"),) * 4
        + (spread, P("seq"), spread, P("seq"), spread, P("seq"), spread, P("seq"), P("seq")),
        check_vma=False,
    )
```

time: 1190 us -> 580 us (0.49)
  matrix products: 341 us -> 0.36 us
  waiting for transfers between devices: 474 us -> 172 us
  Pallas kernels: 0 us -> 205 us
  local copies, waits for them, and re-layouts: 159 us -> 12 us
  starting transfers between devices: 0.4 us -> 42.8 us
  other arithmetic: 112 us -> 78.8 us
  blocking collectives: 68.6 us -> 42.6 us
    reduce_scatter x8 -> x7, waiting for transfers between devices: 395 us -> 16.9 us  [reduce_z(): lax.psum_scatter(value, 'seq', scatter_dimension=0, axis_index_groups=gro...]
    dot_general x34 -> x1, matrix products: 341 us -> 0.36 us  [per_device(): jnp.dot(directions, dct_table(HEAD_DIM), precision=lax.Precision.HIGHEST)]
    pallas_call x0 -> x12, Pallas kernels: none -> 205 us  [the longest x3 62 us: ffn_chunk(): pl.pallas_call(functools.partial(ffn_kernel, earlier is not None), grid_s...]
    ppermute x0 -> x38, waiting for transfers between devices: none -> 155 us  [send(): return lax.ppermute(value, ('batch', 'seq'), pairs)]
    all_gather x2 -> x0, waiting for transfers between devices: 78.6 us -> none  [carried_in(): everything = jax.tree.map(lambda part: lax.all_gather(part, axis), value)]
    unnamed x180 -> x80, local copies, waits for them, and re-layouts: 74.4 us -> 1.73 us
    select_n x32 -> x2, other arithmetic: 72.7 us -> 1.21 us  [carried(): low = jnp.where(core == 0, before, rest)]
    add x3 -> x40, other arithmetic: 7.44 us -> 62 us  [the longest x10 20.3 us: reduce_pairs(): one = first(keep[1] + got[1])]
  transfers between devices with their start and end apart: 10 -> 45, of which waited for: 7 -> 17; matrix products, arithmetic and copies ran while one was open for 34% -> 13% of each run, Pallas kernels for 0% -> 33%
where the time goes in v1:
time: 580 us; the launch traced here: 569 us
  Pallas kernels  205 us (35%)
  waiting for transfers between devices  172 us (30%)
  other arithmetic  78.8 us (14%)
  starting transfers between devices  42.8 us (7%)
  blocking collectives  42.6 us (7%)
  between operations  15.3 us (3%)
  local copies, waits for them, and re-layouts  12 us (2%)
    ppermute x38, waiting for transfers between devices, send(): return lax.ppermute(value, ('batch', 'seq'), pairs)  155 us
    pallas_call x3, Pallas kernels, ffn_chunk(): pl.pallas_call(functools.partial(ffn_kernel, earlier is not None), grid_s...  62 us
    psum x1, blocking collectives, per_device(): total = lax.psum(jnp.concatenate(vectors), ('batch', 'seq'))  42.6 us
    ppermute x38, starting transfers between devices, send(): return lax.ppermute(value, ('batch', 'seq'), pairs)  42 us
    pallas_call x1, Pallas kernels, ends(): pl.pallas_call(ends_kernel, grid=(rows // tile,), in_specs=[wide(1024)] *...  32.7 us
    pallas_call x4, Pallas kernels, wgrad(): pl.pallas_call(wgrad_kernel, grid_spec=pltpu.PrefetchScalarGridSpec(num_s...  30.4 us
    pallas_call x1, Pallas kernels, backward(): pl.pallas_call(back_kernel, grid=s['grid'], in_specs=[s['head']] * 4 + [s...  26 us
    pallas_call x1, Pallas kernels, mixing(): pl.pallas_call(mix_kernel, grid=s['grid'], in_specs=[s['wide'], pl.BlockS...  21.3 us
  transfers between devices with their start and end apart: 45, of which 17 were waited for; matrix products, arithmetic and copies ran while one was open for 13% of the time, Pallas kernels for 33%

profile of v1, /device:TPU:16, one launch (start us, length us, event | category | flops | bytes accessed | tf_op | source)
XLA Modules:
  0.0 569.2 jit_solution(10988873280336550345)
XLA Ops:
  20.7 18.4 %features.1 = (bf16[1024,1024]{1,0:T(8,128)(2,1)}, bf16[1024,1024]{1,0:T(8,128)(2,1)}, bf16[1024,1024]{1,0:T(8,128)(2,1)}, f32[4,4,136,128]{3,2,1,0:T(8,128)}) custom-call(bf16[1024,1024]{1,0:T(8,128)(2,1)} %get-tuple-element.118.a1.left, bf16[1024,3072]{1,0:T(8,128)(2,1)} %w_qkv.1, bf16[1024,3072]{1,0:T(8,128)(2,1)} %w_qkv.1, bf16[1024,3072]{1,0:T(8,128)(2,1)} %w_qkv.1, ...), custom_call_target="tpu_custom_call" | custom-call | flops 15000000512 | bytes 20971520 | tf_op jit(solution)/shard_map/features/pallas_call | solution.py:414
  47.3 12.5 %collective-permute-done.1 = f32[2,4,136,128]{3,2,1,0:T(8,128)S(1)} collective-permute-done((f32[2,4,136,128]{3,2,1,0:T(8,128)S(1)}, f32[2,4,136,128]{3,2,1,0:T(8,128)S(1)}, u32[]{:S(2)}, u32[]{:S(2)}) %collective-permute-start.1) | collective-permute-done | bytes 557088 | tf_op jit(solution)/shard_map/ppermute | solution.py:586
  61.6 16.7 %ffn_chunk.3 = (bf16[1024,2048]{1,0:T(8,128)(2,1)}, bf16[1024,2048]{1,0:T(8,128)(2,1)}, bf16[1024,2048]{1,0:T(8,128)(2,1)}, bf16[1024,2048]{1,0:T(8,128)(2,1)}, ...) custom-call(s32[2]{0:T(128)} %pad_add_fusion.pos, ...), custom_call_target="tpu_custom_call" | custom-call | flops 8589934592 | bytes 25165824 | tf_op jit(solution)/shard_map/ffn_chunk/pallas_call | solution.py:109
  79.1 16.6 %ffn_chunk.4 = (bf16[1024,2048]{1,0:T(8,128)(2,1)}, bf16[1024,2048]{1,0:T(8,128)(2,1)}, bf16[1024,2048]{1,0:T(8,128)(2,1)}, bf16[1024,2048]{1,0:T(8,128)(2,1)}, ...) custom-call(s32[2]{0:T(128)} %pad_add_fusion.pos, ...), custom_call_target="tpu_custom_call", output_to_operand_aliasing={{0}: (9, {}), {1}: (10, {}), {2}: (11, {}), {3}: (12, {})} | custom-call | flops 8589934592 | bytes 25165824 | tf_op jit(solution)/shard_map/ffn_chunk/pallas_call | solution.py:109
  98.9 21.3 %mixing.1 = (bf16[1024,1024]{1,0:T(8,128)(2,1)}, bf16[1024,1024]{1,0:T(8,128)(2,1)}, f32[4,1024,128]{2,1,0:T(8,128)}, f32[4,4,136,128]{3,2,1,0:T(8,128)}) custom-call(bf16[1024,1024]{1,0:T(8,128)(2,1)} %bitcast.323, bf16[1024,1024]{1,0:T(8,128)(2,1)} %w_out.1, bf16[1024,1024]{1,0:T(8,128)(2,1)} %get-tuple-element.66.qf, ...), custom_call_target="tpu_custom_call" | custom-call | flops 16000000000 | bytes 20971520 | tf_op jit(solution)/shard_map/mixing/pallas_call | solution.py:432
  120.7 28.6 %ffn_chunk.5 = (bf16[1024,2048]{1,0:T(8,128)(2,1)}, bf16[1024,2048]{1,0:T(8,128)(2,1)}, bf16[1024,2048]{1,0:T(8,128)(2,1)}, bf16[1024,2048]{1,0:T(8,128)(2,1)}, ...) custom-call(s32[2]{0:T(128)} %pad_add_fusion.pos, ...), custom_call_target="tpu_custom_call", output_to_operand_aliasing={{0}: (9, {}), {1}: (10, {}), {2}: (11, {}), {3}: (12, {})} | custom-call | flops 17179869184 | bytes 46137344 | tf_op jit(solution)/shard_map/ffn_chunk/pallas_call | solution.py:109
  152.6 11.2 %collective-permute-start.5 = (f32[2,4,136,128]{3,2,1,0:T(8,128)S(1)}, f32[2,4,136,128]{3,2,1,0:T(8,128)S(1)}, u32[]{:S(2)}, u32[]{:S(2)}) collective-permute-start(f32[2,4,136,128]{3,2,1,0:T(8,128)S(1)} %dynamic-slice_add_fusion), channel_id=1, source_target_pairs={{2,0},{3,1},{4,2},{5,3},{6,4},{7,5},{10,8},{11,9},{12,10},{13,11},... | collective-permute-start | bytes 1671176 | tf_op jit(solution)/shard_map/ppermute | solution.py:586
  169.5 7.9 %collective-permute-done.5 = f32[2,4,136,128]{3,2,1,0:T(8,128)S(1)} collective-permute-done((f32[2,4,136,128]{3,2,1,0:T(8,128)S(1)}, f32[2,4,136,128]{3,2,1,0:T(8,128)S(1)}, u32[]{:S(2)}, u32[]{:S(2)}) %collective-permute-start.5) | collective-permute-done | bytes 557088 | tf_op jit(solution)/shard_map/ppermute | solution.py:586
  183.4 7.9 %collective-permute-done.21 = f32[2,4,256,128]{3,2,1,0:T(8,128)S(1)} collective-permute-done((f32[2,4,256,128]{3,2,1,0:T(8,128)S(1)}, f32[2,4,256,128]{3,2,1,0:T(8,128)S(1)}, u32[]{:S(2)}, u32[]{:S(2)}) %collective-permute-start.21) | collective-permute-done | bytes 1048608 | tf_op jit(solution)/shard_map/ppermute | solution.py:586
  194.6 9.4 %collective-permute-done.6 = f32[2,4,136,128]{3,2,1,0:T(8,128)S(1)} collective-permute-done((f32[2,4,136,128]{3,2,1,0:T(8,128)S(1)}, f32[2,4,136,128]{3,2,1,0:T(8,128)S(1)}, u32[]{:S(2)}, u32[]{:S(2)}) %collective-permute-start.6) | collective-permute-done | bytes 557088 | tf_op jit(solution)/shard_map/ppermute | solution.py:586
  204.8 9.0 %collective-permute-done.27 = f32[2,4,256,128]{3,2,1,0:T(8,128)S(1)} collective-permute-done((f32[2,4,256,128]{3,2,1,0:T(8,128)S(1)}, f32[2,4,256,128]{3,2,1,0:T(8,128)S(1)}, u32[]{:S(2)}, u32[]{:S(2)}) %collective-permute-start.27) | collective-permute-done | bytes 1048608 | tf_op jit(solution)/shard_map/ppermute | solution.py:586
  226.5 26.0 %backward.1 = (bf16[3,1024,1024]{2,1,0:T(8,128)(2,1)}, f32[3,1,1024]{2,1,0:T(1,128)}, f32[1,1024]{1,0:T(1,128)}) custom-call(bf16[1024,1024]{1,0:T(8,128)(2,1)} %get-tuple-element.66.qf, bf16[1024,1024]{1,0:T(8,128)(2,1)} %get-tuple-element.67.kf, bf16[1024,1024]{1,0:T(8,128)(2,1)} %get-tuple-element.68.v, bf16[1024,1024]{1,0:T(8,128)(2,1)} %get-tuple-element.85.dn, ...), custom_call_target="tpu_custom_call" | custom-call | flops 20000000000 | bytes 25165824 | tf_op jit(solution)/shard_map/backward/pallas_call | solution.py:451
  252.5 7.7 %wgrad.4 = (f32[2,2,4,1,128,256]{5,4,3,2,1,0:T(8,128)}, f32[2,2,4,1,128,256]{5,4,3,2,1,0:T(8,128)}) custom-call(s32[2]{0:T(128)} %pad_add_fusion.pos, bf16[1024,1024]{1,0:T(8,128)(2,1)} %get-tuple-element.118.a1.left, bf16[3,1024,1024]{2,1,0:T(8,128)(2,1)} %get-tuple-element.88.gp.right), custom_call_target="tpu_custom_call" | custom-call | flops 2147483648 | bytes 8388608 | tf_op jit(solution)/shard_map/wgrad/pallas_call | solution.py:161
  281.3 7.7 %wgrad.6 = (f32[2,2,4,1,128,256]{5,4,3,2,1,0:T(8,128)}, f32[2,2,4,1,128,256]{5,4,3,2,1,0:T(8,128)}) custom-call(s32[2]{0:T(128)} %pad_add_fusion.pos, bf16[1024,1024]{1,0:T(8,128)(2,1)} %get-tuple-element.118.a1.left, bf16[3,1024,1024]{2,1,0:T(8,128)(2,1)} %get-tuple-element.88.gp.right), custom_call_target="tpu_custom_call" | custom-call | flops 2147483648 | bytes 8388608 | tf_op jit(solution)/shard_map/wgrad/pallas_call | solution.py:161
  302.5 15.1 %collective-permute-done.9 = f32[2,4,1,128,256]{4,3,1,2,0:T(8,128)} collective-permute-done((f32[2,4,1,128,256]{4,3,1,2,0:T(8,128)}, f32[2,4,1,128,256]{4,3,1,2,0:T(8,128)}, u32[]{:S(2)}, u32[]{:S(2)}) %collective-permute-start.9) | collective-permute-done | bytes 1048608 | tf_op jit(solution)/shard_map/ppermute | solution.py:586
  325.3 13.2 %collective-permute-done.10 = f32[4,1,128,256]{3,2,1,0:T(8,128)S(1)} collective-permute-done((f32[4,1,128,256]{3,2,1,0:T(8,128)S(1)}, f32[4,1,128,256]{3,2,1,0:T(8,128)S(1)}, u32[]{:S(2)}, u32[]{:S(2)}) %collective-permute-start.10) | collective-permute-done | bytes 524320 | tf_op jit(solution)/shard_map/ppermute | solution.py:586
  344.5 18.1 %collective-permute-done.36 = f32[2,4,256,256]{3,2,1,0:T(8,128)} collective-permute-done((f32[2,4,256,256]{3,2,1,0:T(8,128)}, f32[2,4,256,256]{3,2,1,0:T(8,128)}, u32[]{:S(2)}, u32[]{:S(2)}) %collective-permute-start.36) | collective-permute-done | bytes 2097184 | tf_op jit(solution)/shard_map/ppermute | solution.py:586
  367.1 28.8 %collective-permute-done.13 = f32[4,1,128,256]{3,2,1,0:T(8,128)} collective-permute-done((f32[4,1,128,256]{3,2,1,0:T(8,128)}, f32[4,1,128,256]{3,2,1,0:T(8,128)}, u32[]{:S(2)}, u32[]{:S(2)}) %collective-permute-start.13) | collective-permute-done | bytes 524320 | tf_op jit(solution)/shard_map/ppermute | solution.py:586
  404.2 7.5 %wgrad.7 = (f32[2,2,4,1,128,256]{5,4,3,2,1,0:T(8,128)}, f32[2,2,4,1,128,256]{5,4,3,2,1,0:T(8,128)}) custom-call(s32[2]{0:T(128)} %pad_add_fusion.pos, bf16[1024,1024]{1,0:T(8,128)(2,1)} %get-tuple-element.70.mixed.left, bf16[1,1024,1024]{2,1,0:T(8,128)(2,1)} %bitcast.325), custom_call_target="tpu_custom_call" | custom-call | flops 2147483648 | bytes 8388608 | tf_op jit(solution)/shard_map/wgrad/pallas_call | solution.py:161
  431.9 32.7 %ends.1 = (bf16[1024,1024]{1,0:T(8,128)(2,1)}, f32[1024,1024]{1,0:T(8,128)}, f32[8,1024]{1,0:T(8,128)}) custom-call(bf16[1024,1024]{1,0:T(8,128)(2,1)} %bitcast.319, bf16[1024,1024]{1,0:T(8,128)(2,1)} %bitcast.326, bf16[1024,1024]{1,0:T(8,128)(2,1)} %get-tuple-element.70.mixed.left, bf16[1024,2048]{1,0:T(8,128)(2,1)} %get-tuple-element.79.gelu_a, ...), custom_call_target="tpu_custom_call" | custom-call | flops 19000000512 | bytes 50331648 | tf_op jit(solution)/shard_map/ends/pallas_call | solution.py:528
  467.5 14.2 %last.1 = (f32[1024,1024]{1,0:T(8,128)}, f32[8,1024]{1,0:T(8,128)}) custom-call(bf16[1024,1024]{1,0:T(8,128)(2,1)} %bitcast.320, f32[1024,1024]{1,0:T(8,128)} %get-tuple-element.84.part, bf16[3,1024,1024]{2,1,0:T(8,128)(2,1)} %get-tuple-element.88.gp.right, bf16[1024,3072]{1,0:T(8,128)(2,1)} %w_qkv.1, f32[1,1024]{1,0:T(1,128)} %bitcast.366), custom_call_target="tpu_custom_call" | custom-call | flops 6400000000 | bytes 23068672 | tf_op jit(solution)/shard_map/last/pallas_call | solution.py:556
  482.6 8.1 %collective-permute-done.18 = f32[2,4,1,128,256]{4,3,1,2,0:T(8,128)} collective-permute-done((f32[2,4,1,128,256]{4,3,1,2,0:T(8,128)S(1)}, f32[2,4,1,128,256]{4,3,1,2,0:T(8,128)}, u32[]{:S(2)}, u32[]{:S(2)}) %collective-permute-start.18) | collective-permute-done | bytes 1048608 | tf_op jit(solution)/shard_map/ppermute | solution.py:586
  492.7 42.6 %psum.7 = f32[13312]{0:T(1024)S(1)} all-reduce(f32[13312]{0:T(1024)S(1)} %constant_dynamic-update-slice_fusion), channel_id=1, replica_groups=mesh['batch'=4,'seq'=8] {'batch','seq'}, use_global_device_ids=true, to_apply=%region_2.3 | all-reduce | flops 13312 | bytes 106496 | tf_op jit(solution)/shard_map/psum | solution.py:733
  544.7 16.9 %reduce-scatter.14.cloned.1.call-done = f32[1,1,128,256]{3,2,0,1:T(8,128)} async-done(((f32[4,1,128,256]{3,2,0,1:T(8,128)}), f32[1,1,128,256]{3,2,0,1:T(8,128)}) %reduce-scatter.14.cloned.1.call-update) | async-done | bytes 131088 | tf_op jit(solution)/shard_map/reduce_scatter | solution.py:612
  (268 shorter events, 155.8 us)
Async XLA Ops:
  7.2 530.0 %reduce-scatter.16.cloned.1.call-start = ((), (), s32[]{:S(2)}) async-start(), calls=%async_computation.11 | async-start | bytes 1310720 | tf_op jit(solution)/shard_map/reduce_scatter | solution.py:612
  78.3 85.5 %collective-permute-start.20 = (f32[2,2,4,256,128]{4,3,2,1,0:T(8,128)}, f32[2,2,4,256,128]{4,3,2,1,0:T(8,128)}, u32[]{:S(2)}, u32[]{:S(2)}) collective-permute-start(f32[2,2,4,256,128]{4,3,2,1,0:T(8,128)} %get-tuple-element.106), channel_id=1, source_target_pairs={{0,1},{1,0},{2,3},{3,2},{4,5},{5,4},{6,7},{7,6},{8,9},{9,8},{10,11... | collective-permute-start | bytes 6291464 | tf_op jit(solution)/shard_map/ppermute | solution.py:586
  78.4 71.0 %collective-permute-start.23 = (f32[2,2,4,128,256]{4,3,2,1,0:T(8,128)}, f32[2,2,4,128,256]{4,3,2,1,0:T(8,128)}, u32[]{:S(2)}, u32[]{:S(2)}) collective-permute-start(f32[2,2,4,128,256]{4,3,2,1,0:T(8,128)} %get-tuple-element.108), channel_id=1, source_target_pairs={{0,1},{1,0},{2,3},{3,2},{4,5},{5,4},{6,7},{7,6},{8,9},{9,8},{10,11... | collective-permute-start | bytes 6291464 | tf_op jit(solution)/shard_map/ppermute | solution.py:586
  95.7 70.9 %collective-permute-start.26 = (f32[2,2,4,256,128]{4,3,2,1,0:T(8,128)}, f32[2,2,4,256,128]{4,3,2,1,0:T(8,128)}, u32[]{:S(2)}, u32[]{:S(2)}) collective-permute-start(f32[2,2,4,256,128]{4,3,2,1,0:T(8,128)} %get-tuple-element.110), channel_id=1, source_target_pairs={{0,1},{1,0},{2,3},{3,2},{4,5},{5,4},{6,7},{7,6},{8,9},{9,8},{10,11... | collective-permute-start | bytes 6291464 | tf_op jit(solution)/shard_map/ppermute | solution.py:586
  96.2 81.3 %collective-permute-start.29 = (f32[2,2,4,128,256]{4,3,2,1,0:T(8,128)}, f32[2,2,4,128,256]{4,3,2,1,0:T(8,128)}, u32[]{:S(2)}, u32[]{:S(2)}) collective-permute-start(f32[2,2,4,128,256]{4,3,2,1,0:T(8,128)} %get-tuple-element.112), channel_id=1, source_target_pairs={{0,1},{1,0},{2,3},{3,2},{4,5},{5,4},{6,7},{7,6},{8,9},{9,8},{10,11... | collective-permute-start | bytes 6291464 | tf_op jit(solution)/shard_map/ppermute | solution.py:586
  168.1 45.6 %collective-permute-start.27 = (f32[2,4,256,128]{3,2,1,0:T(8,128)S(1)}, f32[2,4,256,128]{3,2,1,0:T(8,128)S(1)}, u32[]{:S(2)}, u32[]{:S(2)}) collective-permute-start(f32[2,4,256,128]{3,2,1,0:T(8,128)S(1)} %fusion.15), channel_id=1, source_target_pairs={{0,8},{1,9},{2,10},{3,11},{4,12},{5,13},{6,14},{7,15},{8,0},{9,1},... | collective-permute-start | bytes 3145736 | tf_op jit(solution)/shard_map/ppermute | solution.py:586
  177.4 143.1 %collective-permute-start.32 = (f32[2,2,4,512,128]{4,3,2,1,0:T(8,128)}, f32[2,2,4,512,128]{4,3,2,1,0:T(8,128)}, u32[]{:S(2)}, u32[]{:S(2)}) collective-permute-start(f32[2,2,4,512,128]{4,3,2,1,0:T(8,128)} %get-tuple-element.114), channel_id=1, source_target_pairs={{0,1},{1,0},{2,3},{3,2},{4,5},{5,4},{6,7},{7,6},{8,9},{9,8},{10,11... | collective-permute-start | bytes 12582920 | tf_op jit(solution)/shard_map/ppermute | solution.py:586
  182.1 111.1 %collective-permute-start.35 = (f32[2,2,4,256,256]{4,3,2,1,0:T(8,128)}, f32[2,2,4,256,256]{4,3,2,1,0:T(8,128)}, u32[]{:S(2)}, u32[]{:S(2)}) collective-permute-start(f32[2,2,4,256,256]{4,3,2,1,0:T(8,128)} %get-tuple-element.116), channel_id=1, source_target_pairs={{0,1},{1,0},{2,3},{3,2},{4,5},{5,4},{6,7},{7,6},{8,9},{9,8},{10,11... | collective-permute-start | bytes 12582920 | tf_op jit(solution)/shard_map/ppermute | solution.py:586
  204.1 60.5 %collective-permute-start.30 = (f32[2,4,128,256]{3,2,1,0:T(8,128)}, f32[2,4,128,256]{3,2,1,0:T(8,128)}, u32[]{:S(2)}, u32[]{:S(2)}) collective-permute-start(f32[2,4,128,256]{3,2,1,0:T(8,128)} %fusion.14), channel_id=1, source_target_pairs={{0,16},{1,17},{2,18},{3,19},{4,20},{5,21},{6,22},{7,23},{8,24},{9,... | collective-permute-start | bytes 3145736 | tf_op jit(solution)/shard_map/ppermute | solution.py:586
  223.4 36.8 %collective-permute-start.22 = (f32[4,256,128]{2,1,0:T(8,128)}, f32[4,256,128]{2,1,0:T(8,128)}, u32[]{:S(2)}, u32[]{:S(2)}) collective-permute-start(f32[4,256,128]{2,1,0:T(8,128)} %fusion.37), channel_id=1, source_target_pairs={{0,16},{1,17},{2,18},{3,19},{4,20},{5,21},{6,22},{7,23},{8,24},{9,... | collective-permute-start | bytes 1572872 | tf_op jit(solution)/shard_map/ppermute | solution.py:586
  264.3 272.9 %reduce-scatter.18.cloned.1.call-start = ((), (), s32[]{:S(2)}) async-start(), calls=%async_computation.12 | async-start | bytes 1310720 | tf_op jit(solution)/shard_map/reduce_scatter | solution.py:612
  293.1 246.5 %reduce-scatter.8.cloned.1.call-start = ((), (), s32[]{:S(2)}) async-start(), calls=%async_computation.7 | async-start | bytes 655360 | tf_op jit(solution)/shard_map/reduce_scatter | solution.py:612
  297.1 65.5 %collective-permute-start.36 = (f32[2,4,256,256]{3,2,1,0:T(8,128)}, f32[2,4,256,256]{3,2,1,0:T(8,128)}, u32[]{:S(2)}, u32[]{:S(2)}) collective-permute-start(f32[2,4,256,256]{3,2,1,0:T(8,128)} %fusion.2), channel_id=1, source_target_pairs={{0,16},{1,17},{2,18},{3,19},{4,20},{5,21},{6,22},{7,23},{8,24},{9,... | collective-permute-start | bytes 6291464 | tf_op jit(solution)/shard_map/ppermute | solution.py:586
  301.1 39.9 %collective-permute-start.12 = (f32[2,4,1,128,256]{4,3,1,2,0:T(8,128)}, f32[2,4,1,128,256]{4,3,1,2,0:T(8,128)}, u32[]{:S(2)}, u32[]{:S(2)}) collective-permute-start(f32[2,4,1,128,256]{4,3,1,2,0:T(8,128)} %fusion.20), channel_id=1, source_target_pairs={{0,8},{1,9},{2,10},{3,11},{4,12},{5,13},{6,14},{7,15},{8,0},{9,1},... | collective-permute-start | bytes 3145736 | tf_op jit(solution)/shard_map/ppermute | solution.py:586
  322.5 78.9 %collective-permute-start.33 = (f32[2,4,512,128]{3,2,1,0:T(8,128)S(1)}, f32[2,4,512,128]{3,2,1,0:T(8,128)}, u32[]{:S(2)}, u32[]{:S(2)}) collective-permute-start(f32[2,4,512,128]{3,2,1,0:T(8,128)S(1)} %fusion.3), channel_id=1, source_target_pairs={{0,8},{1,9},{2,10},{3,11},{4,12},{5,13},{6,14},{7,15},{8,0},{9,1},... | collective-permute-start | bytes 6291464 | tf_op jit(solution)/shard_map/ppermute | solution.py:586
  324.7 73.8 %collective-permute-start.15 = (f32[2,4,1,128,256]{4,3,1,2,0:T(8,128)S(1)}, f32[2,4,1,128,256]{4,3,1,2,0:T(8,128)}, u32[]{:S(2)}, u32[]{:S(2)}) collective-permute-start(f32[2,4,1,128,256]{4,3,1,2,0:T(8,128)S(1)} %fusion.19), channel_id=1, source_target_pairs={{0,16},{1,17},{2,18},{3,19},{4,20},{5,21},{6,22},{7,23},{8,24},{9,... | collective-permute-start | bytes 3145736 | tf_op jit(solution)/shard_map/ppermute | solution.py:586
  340.9 198.7 %reduce-scatter.10.cloned.1.call-start = ((), (), s32[]{:S(2)}) async-start(), calls=%async_computation.8 | async-start | bytes 655360 | tf_op jit(solution)/shard_map/reduce_scatter | solution.py:612
  343.3 52.7 %collective-permute-start.13 = (f32[4,1,128,256]{3,2,1,0:T(8,128)}, f32[4,1,128,256]{3,2,1,0:T(8,128)}, u32[]{:S(2)}, u32[]{:S(2)}) collective-permute-start(f32[4,1,128,256]{3,2,1,0:T(8,128)} %fusion.54), channel_id=1, source_target_pairs={{0,16},{1,17},{2,18},{3,19},{4,20},{5,21},{6,22},{7,23},{8,24},{9,... | collective-permute-start | bytes 1572872 | tf_op jit(solution)/shard_map/ppermute | solution.py:586
  365.6 52.9 %collective-permute-start.37 = (f32[4,256,256]{2,1,0:T(8,128)}, f32[4,256,256]{2,1,0:T(8,128)}, u32[]{:S(2)}, u32[]{:S(2)}) collective-permute-start(f32[4,256,256]{2,1,0:T(8,128)} %fusion.4), channel_id=1, source_target_pairs={{0,8},{1,9},{2,10},{3,11},{4,12},{5,13},{6,14},{7,15},{8,0},{9,1},... | collective-permute-start | bytes 3145736 | tf_op jit(solution)/shard_map/ppermute | solution.py:586
  398.4 141.3 %reduce-scatter.12.cloned.1.call-start = ((), (), s32[]{:S(2)}) async-start(), calls=%async_computation.9 | async-start | bytes 655360 | tf_op jit(solution)/shard_map/reduce_scatter | solution.py:612
  411.7 53.7 %collective-permute-start.17 = (f32[2,2,4,1,128,256]{5,4,2,1,3,0:T(8,128)}, f32[2,2,4,1,128,256]{5,4,2,1,3,0:T(8,128)}, u32[]{:S(2)}, u32[]{:S(2)}) collective-permute-start(f32[2,2,4,1,128,256]{5,4,2,1,3,0:T(8,128)} %bitcast.372), channel_id=1, source_target_pairs={{0,1},{1,0},{2,3},{3,2},{4,5},{5,4},{6,7},{7,6},{8,9},{9,8},{10,11... | collective-permute-start | bytes 6291464 | tf_op jit(solution)/shard_map/ppermute | solution.py:586
  418.5 123.0 %reduce-scatter.20.cloned.1.call-start = ((), (), s32[]{:S(2)}) async-start(), calls=%async_computation.13 | async-start | bytes 2621440 | tf_op jit(solution)/shard_map/reduce_scatter | solution.py:612
  431.5 130.1 %reduce-scatter.14.cloned.1.call-start = ((), (), s32[]{:S(2)}) async-start(), calls=%async_computation.10 | async-start | bytes 655360 | tf_op jit(solution)/shard_map/reduce_scatter | solution.py:612
  492.0 45.2 %collective-permute-start.19 = (f32[4,1,128,256]{3,2,0,1:T(8,128)S(1)}, f32[4,1,128,256]{3,2,0,1:T(8,128)S(1)}, u32[]{:S(2)}, u32[]{:S(2)}) collective-permute-start(f32[4,1,128,256]{3,2,0,1:T(8,128)S(1)} %fusion.42), channel_id=1, source_target_pairs={{0,16},{1,17},{2,18},{3,19},{4,20},{5,21},{6,22},{7,23},{8,24},{9,... | collective-permute-start | bytes 1572872 | tf_op jit(solution)/shard_map/ppermute | solution.py:586
  (57 other events, 883.2 us)
Sparse Core Ops, SparseCore 0:
  264.4 25.9 reduce-scatter.15
  293.2 26.7 reduce-scatter.17
  341.1 20.0 reduce-scatter.7
  398.5 20.1 reduce-scatter.9
  421.4 19.9 reduce-scatter.11
  443.6 43.1 reduce-scatter.19
  539.7 21.9 reduce-scatter.13

commit v2 on v1

v2 whole, which is shorter than its diff:
```python
import functools
import math

import jax
import jax.numpy as jnp
import numpy as np
from jax import lax
from jax.experimental import pallas as pl
from jax.experimental.pallas import tpu as pltpu
from jax.sharding import PartitionSpec as P

f32 = jnp.float32
bf16 = jnp.bfloat16
struct = jax.ShapeDtypeStruct
HEADS = 16
HEAD_DIM = 64
ROT = 16
LEN_BLK = 256
ROW_TILE = 256
HG = 256
ROOT_HALF = math.sqrt(0.5)
NORMAL_PEAK = 1.0 / math.sqrt(2.0 * math.pi)
norm_epsilon = 1e-05
rope_base = 10000.0
VMEM_BYTES = 60 * 1024 * 1024


def params():
    return pltpu.CompilerParams(vmem_limit_bytes=VMEM_BYTES)


def dot(a, b, ca, cb):
    return lax.dot_general(a, b, (((ca,), (cb,)), ((), ())), preferred_element_type=f32)


def iota(shape, dim):
    return lax.broadcasted_iota(jnp.int32, shape, dim)


def split(x):
    hi = x.astype(bf16)
    return hi, (x - hi.astype(f32)).astype(bf16)


def ordered_call(kernel, args, after, *, in_specs, grid, out_specs, out_shape, prefetch=0, **kw):
    after = [a for a in after if a is not None]
    n_in = len(args)

    def body(*refs):
        kernel(*refs[:n_in], *refs[n_in + len(after) :])

    in_specs = list(in_specs) + [pl.BlockSpec(memory_space=pl.ANY)] * len(after)
    return pl.pallas_call(
        body,
        grid_spec=pltpu.PrefetchScalarGridSpec(
            num_scalar_prefetch=prefetch, grid=grid, in_specs=in_specs, out_specs=out_specs
        ),
        out_shape=out_shape,
        compiler_params=params(),
        **kw,
    )(*args, *after)


def ffn_kernel(aliased, pos, a2_own, a2_other, g_own, g_other, *refs):
    w_ups, w_downs, biases = refs[:2], refs[2:4], refs[4:6]
    refs = refs[6 + aliased :]
    gelus, grads, (up_send, up_keep, down_send, down_keep, b_sum) = refs[:2], refs[2:4], refs[4:]
    me = pos[0]
    w_up = jnp.concatenate([w[...] for w in w_ups], axis=1)
    w_down = jnp.concatenate([w[...] for w in w_downs], axis=0)
    bias = jnp.concatenate([b[...] for b in biases], axis=1)
    d_up = d_down = total = None
    for half, (a2, g) in enumerate(((a2_own, g_own), (a2_other, g_other))):
        rows_in, grad_in = a2[...], g[...]
        pre = dot(rows_in, w_up, 1, 0) + bias
        grad_gelu = dot(grad_in, w_down, 1, 1)
        cdf = 0.5 + 0.5 * lax.erf(pre * ROOT_HALF)
        gelu = (pre * cdf).astype(bf16)
        slope = cdf + pre * (NORMAL_PEAK * jnp.exp(-0.5 * pre * pre))
        grad_pre = (grad_gelu * slope).astype(bf16)
        for j in range(2):
            gelus[j][half, 0] = gelu[:, 128 * j : 128 * j + 128]
            grads[j][half, 0] = grad_pre[:, 128 * j : 128 * j + 128]
        parts = (
            dot(grad_pre, rows_in, 0, 0),
            dot(gelu, grad_in, 0, 0),
            jnp.sum(grad_pre.astype(f32), axis=0, keepdims=True),
        )
        if half == 0:
            d_up, d_down, total = parts
        else:
            d_up, d_down, total = d_up + parts[0], d_down + parts[1], total + parts[2]
    b_sum[0] = total
    mx = lax.rem(me, 2)
    keep, send = swapped(mx, d_up[:128], d_up[128:])
    for n in range(8):
        up_send[0, n // 2, n % 2] = send[:, n * 128 : (n + 1) * 128]
        up_keep[0, n // 2, n % 2] = keep[:, n * 128 : (n + 1) * 128]
    for j in range(2):
        squares = relative(d_down[128 * j : 128 * j + 128], me)
        for rx in range(2):
            for half in range(2):
                part = slice(128 * half, 128 * half + 128)
                down_send[rx, j, half] = squares[rx][1][:, part]
                down_keep[rx, j, half] = squares[rx][0][:, part]


def swapped(bit, first, second):
    return jnp.where(bit == 0, first, second), jnp.where(bit == 0, second, first)


def relative(tile, me):
    by_y = swapped(lax.div(me, 2), tile[:, :512], tile[:, 512:])
    by_yx = [swapped(lax.rem(me, 2), part[:, :256], part[:, 256:]) for part in by_y]
    return [[by_yx[y][x] for y in range(2)] for x in range(2)]


def once(shape, where):
    return pl.BlockSpec(shape, where, pipeline_mode=pl.Buffered(1))


def ffn_chunk(first, count, pos, a2, g, w_up, w_down, b_up, earlier=(), filled=(), more=0, after=()):
    rows, width = a2[0].shape
    block = lambda j, k, i, p: (2 * (2 * i + j) + p[1]) * 4 + first + k
    cols = lambda j: (lambda k, i, p: (0, block(j, k, i, p)))
    lines = lambda j: (lambda k, i, p: (block(j, k, i, p), 0))
    whole = lambda k, i, p: (0, 0)
    place = lambda k, i, p: (0, i * 4 + first + k, 0, 0)
    in_specs = (
        [once((rows, width), whole)] * 4
        + [pl.BlockSpec((width, 128), cols(j)) for j in range(2)]
        + [pl.BlockSpec((128, width), lines(j)) for j in range(2)]
        + [pl.BlockSpec((1, 128), cols(j)) for j in range(2)]
    )
    args = [pos, *a2, *g, w_up, w_up, w_down, w_down, b_up, b_up]
    given = [*enumerate(earlier), *enumerate(filled, 4)]
    aliases = {len(args) + i: out for i, (out, _) in enumerate(given)}
    in_specs = in_specs + [pl.BlockSpec(memory_space=pl.ANY)] * len(given)
    args = args + [value for _, value in given]
    pieces = [struct((2, 4, 2 * count + extra, 128, 128), f32) for extra in (more, 0)] * 2
    pieces = [struct(v.shape, f32) for v in filled] or pieces
    skip = 1 if filled else 0
    return ordered_call(
        functools.partial(ffn_kernel, len(given)),
        args,
        after,
        prefetch=1,
        grid=(count, 2),
        in_specs=in_specs,
        out_specs=[pl.BlockSpec((2, 1, rows, 128), place)] * 4
        + [
            pl.BlockSpec(
                (1, 4, 2, 128, 128),
                lambda k, i, p, n=n: (lax.bitwise_xor(i, lax.div(p[0], 2)), 0, k + n, 0, 0),
            )
            for n in (skip, 0)
        ]
        + [
            pl.BlockSpec((2, 2, 2, 128, 128), lambda k, i, p, n=n: (0, i, k + n, 0, 0))
            for n in (skip, 0)
        ]
        + [pl.BlockSpec((1, 1, 256), lambda k, i, p: (k * 2 + i, 0, 0))],
        out_shape=[struct((2, 8, rows, 128), bf16)] * 4
        + pieces
        + [struct((count * 2, 1, 256), f32)],
        input_output_aliases=aliases,
        cost_estimate=cost(f"ffn{first}"),
        name="ffn_chunk",
    )


def out_grad_kernel(pos, own, early, late, g_own, g_other, x_send, x_keep, y_send, y_keep):
    other = jnp.where(pl.program_id(0) < 2, early[...], late[...]).astype(bf16)
    tile = dot(own[...], g_own[...], 0, 0) + dot(other, g_other[...], 0, 0)
    squares = relative(tile, pos[0])
    for n in range(2):
        x_send[n, 0, 0] = squares[1][n][:, :128]
        x_keep[n, 0, 0] = squares[0][n][:, :128]
        y_send[n, 0, 0] = squares[n][1][:, 128:]
        y_keep[n, 0, 0] = squares[n][0][:, 128:]


def out_grad(pos, mixed, others, g, after=()):
    rows, width = g[0].shape
    whole = lambda z, p: (0, 0)
    return ordered_call(
        out_grad_kernel,
        [pos, mixed, *others, *g],
        after,
        prefetch=1,
        grid=(4,),
        in_specs=[
            pl.BlockSpec((rows, 128), lambda z, p: (0, 2 * z + p[1])),
            pl.BlockSpec((rows, 128), lambda z, p: (0, lax.min(z, 1))),
            pl.BlockSpec((rows, 128), lambda z, p: (0, lax.max(z - 2, 0))),
            once((rows, width), whole),
            once((rows, width), whole),
        ],
        out_specs=[
            pl.BlockSpec((2, 1, 1, 128, 128), lambda z, p: (0, z, 4, 0, 0)),
            pl.BlockSpec((2, 1, 1, 128, 128), lambda z, p: (0, z, 2, 0, 0)),
        ]
        * 2,
        out_shape=[struct((2, 4, 5, 128, 128), f32), struct((2, 4, 3, 128, 128), f32)] * 2,
        cost_estimate=cost("out_grad"),
        name="out_grad",
    )


def second_kernel(at, slots, u_keep, u_one, d_keep, d_one, *refs):
    x_o, y_o = refs[-2:]
    own = slice(at, at + slots)
    y_o[...] = (u_keep[...] + u_one[:, :, own]).reshape(y_o.shape)
    x_o[...] = (d_keep[...] + d_one[:, :, own]).reshape(x_o.shape)


def second_stage(keeps, ones, at, bundles=None, into=0):
    slots, total = keeps[0].shape[2], ones[0].shape[2]
    half = slots // 2
    keep = pl.BlockSpec((1, 2, slots, 128, 128), lambda i: (1, i, 0, 0, 0))
    one = pl.BlockSpec((1, 2, total, 128, 128), lambda i: (1, i, 0, 0, 0))
    if bundles:
        out = pl.BlockSpec((1, 4, half, 128, 128), lambda i: (i, 0, into // half, 0, 0))
        shapes = [struct(v.shape, f32) for v in bundles]
    else:
        out = pl.BlockSpec((2, slots, 128, 128), lambda i: (i, 0, 0, 0))
        shapes = [struct((4, slots, 128, 128), f32)] * 2
    return ordered_call(
        functools.partial(second_kernel, at, slots),
        [keeps[0], ones[0], keeps[1], ones[1], *(bundles or [])],
        [],
        grid=(2,),
        in_specs=[keep, one] * 2 + [pl.BlockSpec(memory_space=pl.ANY)] * len(bundles or []),
        out_specs=[out] * 2,
        out_shape=shapes,
        input_output_aliases={4: 0, 5: 1} if bundles else {},
        cost_estimate=cost("second_stage"),
        name="second_stage",
    )


def finish_kernel(at, slots, cut, u_keep, u_one, u_two, d_keep, d_one, d_two, out):
    own = slice(at, at + slots)
    for n, (keep, one, two) in enumerate(((u_keep, u_one, u_two), (d_keep, d_one, d_two))):
        if cut is None:
            second = two[...]
        else:
            second = two[0, :, cut[0] : cut[1]].reshape(2, slots, 128, 128)
        out[:, n * slots : (n + 1) * slots] = keep[0] + one[0, :, own] + second


def finish(keeps, ones, at, twos, cut):
    slots, total = keeps[0].shape[2], ones[0].shape[2]
    keep = pl.BlockSpec((1, 2, slots, 128, 128), lambda i: (0, i, 0, 0, 0))
    one = pl.BlockSpec((1, 2, total, 128, 128), lambda i: (0, i, 0, 0, 0))
    if cut is None:
        two = pl.BlockSpec((2, slots, 128, 128), lambda i: (i, 0, 0, 0))
    else:
        two = pl.BlockSpec((1, 4, twos[0].shape[2], 128, 128), lambda i: (i, 0, 0, 0, 0))
    return ordered_call(
        functools.partial(finish_kernel, at, slots, cut),
        [keeps[0], ones[0], twos[0], keeps[1], ones[1], twos[1]],
        [],
        grid=(2,),
        in_specs=[keep, one, two] * 2,
        out_specs=pl.BlockSpec((2, 2 * slots, 128, 128), lambda i: (i, 0, 0, 0)),
        out_shape=struct((4, 2 * slots, 128, 128), f32),
        cost_estimate=cost("finish"),
        name="finish",
    )


def qkv_grad_kernel(pos, a1_own, a1_other, *refs):
    own, other, (x_send, x_keep, y_send, y_keep) = refs[:3], refs[3:12], refs[12:]
    left = jnp.concatenate([r[0] for r in own], 1)
    left_other = []
    for j in range(3):
        part = lax.div(lax.bitwise_xor(pl.program_id(0), pos[0]) * 3 + j, 4)
        parts = [r[...] for r in other[3 * j : 3 * j + 3]]
        chosen = jnp.where(part == 0, parts[0], jnp.where(part == 1, parts[1], parts[2]))
        left_other.append(chosen.astype(bf16))
    left_other = jnp.concatenate(left_other, 1)
    tile = dot(left, a1_own[...], 0, 0) + dot(left_other, a1_other[...], 0, 0)
    step = pl.program_id(0)
    block = lambda j, n: tile[128 * j : 128 * j + 128, n * 128 : (n + 1) * 128]

    def put(out, whole, half):
        for z in range(4):
            out[0, z, 0] = block(whole, 2 * z)
            out[0, z, 1] = block(whole, 2 * z + 1)
            out[0, z, 2] = block(2, 2 * z + half)

    pl.when(lax.rem(step, 2) == 1)(lambda: put(x_send, 0, 0))
    pl.when(lax.rem(step, 2) == 0)(lambda: put(x_keep, 0, 0))
    pl.when(step >= 2)(lambda: put(y_send, 1, 1))
    pl.when(step < 2)(lambda: put(y_keep, 1, 1))


def qkv_grad(pos, a1, grad_proj, other, after=()):
    rows, width = a1[0].shape
    whole = lambda n, p: (0, 0)

    def source(j):
        def where(n, p):
            unit = lax.bitwise_xor(n, p[0]) * 3 + j
            return (lax.div(unit, 4), 0, lax.rem(unit, 4) * 2 + p[1])

        return where

    def other_place(j, part):
        if part != j:
            return lambda n, p: (0, [u % 4 for u in range(j, 12, 3) if u // 4 == part][0])
        return lambda n, p: (0, lax.select(lax.bitwise_xor(n, p[0]) <= j, 0 * n, 0 * n + 3))

    out = lambda at: pl.BlockSpec((1, 4, 3, 128, 128), lambda n, p: (at(n), 0, 0, 0, 0))
    return ordered_call(
        qkv_grad_kernel,
        [pos, *a1] + [grad_proj] * 3 + [part for _ in range(3) for part in other],
        after,
        prefetch=1,
        grid=(4,),
        in_specs=[once((rows, width), whole)] * 2
        + [pl.BlockSpec((1, rows, 128), source(j)) for j in range(3)]
        + [pl.BlockSpec((rows, 128), other_place(j, part)) for j in range(3) for part in range(3)],
        out_specs=[
            out(lambda n: lax.div(n, 2)),
            out(lambda n: lax.div(n, 2)),
            out(lambda n: lax.max(n - 2, 0)),
            out(lambda n: lax.min(n, 1)),
        ],
        out_shape=[struct((2, 4, 3, 128, 128), f32)] * 4,
        cost_estimate=cost("qkv_grad"),
        name="qkv_grad",
    )


LONG, SHORT = 10**11, 1
WEIGHTS = {"first_norm": LONG, "hidden0": LONG, "blocks": LONG}


def cost(name):
    flops = WEIGHTS.get(name, SHORT)
    return pl.CostEstimate(flops=flops, bytes_accessed=1, transcendentals=0)


def rotate(x, cos, sin_first, sin_second):
    n = x.shape[1]
    half = ROT // 2
    return x * cos + pltpu.roll(x, n - half, 1) * sin_first + pltpu.roll(x, half, 1) * sin_second


def three(x, w_hi, w_lo):
    hi, lo = split(x)
    return dot(hi, w_hi, 1, 0) + dot(lo, w_hi, 1, 0) + dot(hi, w_lo, 1, 0)


def pair_mask():
    return (iota((128, 128), 0) // 64) == (iota((128, 128), 1) // 64)


def pack(first, second):
    mask = pair_mask()
    first = jnp.where(mask, first, 0.0)
    second = jnp.where(mask, second, 0.0)
    first = first + pltpu.roll(first, 64, 1)
    second = second + pltpu.roll(second, 64, 1)
    return jnp.where(iota((128, 128), 1) < 64, first, second)


def unpack(packed):
    mask = pair_mask()
    low = iota((128, 128), 1) < 64
    turned = pltpu.roll(packed, 64, 1)
    return (
        jnp.where(mask, jnp.where(low, packed, turned), 0.0),
        jnp.where(mask, jnp.where(low, turned, packed), 0.0),
    )


def to_column(row):
    eye = iota((128, 128), 0) == iota((128, 128), 1)
    return jnp.sum(jnp.where(eye, jnp.broadcast_to(row, (128, 128)), 0.0), axis=1, keepdims=True)


def each_head(x):
    mask = iota((1, 128), 1) < 64
    zero = jnp.zeros_like(x)
    return jnp.where(mask, x, zero), jnp.where(mask, zero, x)


def feature_kernel(
    a1, wq, wk, wv, bq, bk, bv, fw, matrix, cos, sin1, sin2, valid, qf_o, kf_o, v_o, st_o
):
    x = a1[...]
    count = x.shape[0] // LEN_BLK
    rows = lambda i: slice(LEN_BLK * i, LEN_BLK * (i + 1))
    turns = cos[...], sin1[...], sin2[...]
    weight = fw[...]
    halves = split(matrix[...])
    q = [dot(x[rows(i)], wq[...], 1, 0) for i in range(count)]
    k = [dot(x[rows(i)], wk[...], 1, 0) for i in range(count)]
    q = [rotate(part + bq[...], *turns) for part in q]
    v = [(dot(x[rows(i)], wv[...], 1, 0) + bv[...]).astype(bf16) for i in range(count)]
    k = [rotate(part + bk[...], *turns) for part in k]
    q = [three(part, *halves) for part in q]
    k = [three(part, *halves) for part in k]
    for i in range(count):
        qf_o[rows(i)] = (weight * jnp.exp(q[i])).astype(bf16)
        kf = (weight * jnp.exp(k[i])).astype(bf16) * valid[rows(i)].astype(bf16)
        kf_o[rows(i)] = kf
        k[i] = kf
        v_o[rows(i)] = v[i]
    for i in range(count):
        state = [
            dot(k[i][:, 128 * p : 128 * p + 128], v[i][:, 128 * p : 128 * p + 128], 0, 0)
            for p in range(2)
        ]
        st_o[i, 0, :128] = pack(state[0], state[1])
        norm = jnp.sum(k[i].astype(f32), axis=0, keepdims=True)
        st_o[i, 0, 128:] = norm_rows(norm[:, :128], norm[:, 128:])


def norm_rows(first, second):
    line = iota((8, 128), 0)
    return jnp.where(line == 0, first, jnp.where(line == 1, second, 0.0))


def scores(qp, kp, causal):
    raw = dot(jnp.concatenate(each_head(qp), 0), kp, 1, 1)
    return [
        jnp.where(causal, raw[LEN_BLK * h : LEN_BLK * (h + 1)], 0.0).astype(bf16)
        for h in range(2)
    ]


def lower(n):
    return iota((n, n), 0) >= iota((n, n), 1)


def mix_kernel(pos, g, wo, qf, kf, v, st, mix_o, dn_o, dd_o, ds_o, *sends):
    count = qf.shape[0] // LEN_BLK
    mask = pair_mask()
    lane = iota((1, 128), 1)
    first = lane < 64
    causal = lower(LEN_BLK)
    one0, one1 = each_head(jnp.ones((LEN_BLK, 128), bf16))
    cells = [(i, p) for i in range(count) for p in range(2)]
    rows = lambda i: slice(LEN_BLK * i, LEN_BLK * (i + 1))
    cols = lambda p: slice(128 * p, 128 * p + 128)
    q = {(i, p): qf[rows(i), cols(p)] for i, p in cells}
    s = {(i, p): scores(q[i, p], kf[rows(i), cols(p)], causal) for i, p in cells}
    grad_mixed = dot(g[...], wo[...], 1, 1)
    both = {}
    for i in range(count):
        state = unpack(st[i, 0, :128])
        for p in range(2):
            column = to_column(st[i, 0, 128 + p : 129 + p])
            norm = jnp.where(mask, jnp.broadcast_to(column, (128, 128)), 0.0)
            hi, lo = split(jnp.concatenate([state[p], norm], 1))
            qp = q[i, p]
            both[i, p] = dot(jnp.concatenate([qp, qp], 1), jnp.concatenate([hi, lo], 0), 1, 0)
    for i, p in cells:
        v0, v1 = each_head(v[rows(i), cols(p)])
        right = jnp.concatenate(
            [jnp.concatenate([v0, one0], 1), jnp.concatenate([v1, one1], 1)], 0
        )
        both[i, p] = both[i, p] + dot(jnp.concatenate(s[i, p], 1), right, 1, 0)
    mixes, dns, norms, grads, sums = {}, {}, {}, {}, {}
    for i, p in cells:
        inverse = 1.0 / both[i, p][:, 128:]
        mixed = both[i, p][:, :128] * inverse
        low = mixed.astype(bf16)
        mix_o[rows(i), cols(p)] = low
        mixes[i, p] = low
        dn = (grad_mixed[rows(i), cols(p)] * inverse).astype(bf16)
        dn_o[rows(i), cols(p)] = dn
        dns[i, p] = dn
        product = -(dn.astype(f32) * mixed)
        d0 = jnp.sum(jnp.where(first, product, 0.0), axis=1, keepdims=True)
        d1 = jnp.sum(jnp.where(first, 0.0, product), axis=1, keepdims=True)
        sums[i, p] = d0, d1
    for i, p in cells:
        grads[i, p] = dot(q[i, p], dns[i, p], 0, 0)
    for i, p in cells:
        d0, d1 = sums[i, p]
        norms[i, p] = column_sum(q[i, p].astype(f32) * jnp.where(first, d0, d1))
    for i in range(count):
        lines = jnp.zeros((LEN_BLK, 128), f32)
        for p in range(2):
            d0, d1 = sums[i, p]
            lines = jnp.where(lane == 2 * p, d0, jnp.where(lane == 2 * p + 1, d1, lines))
        dd_o[0, rows(i)] = lines
        ds_o[i, 0, :128] = pack(grads[i, 0], grads[i, 1])
        ds_o[i, 0, 128:] = norm_rows(norms[i, 0], norms[i, 1])
        other_half = jnp.where(pos[1] == 0, mixes[i, 1].astype(f32), mixes[i, 0].astype(f32))

        def put(out, lines=rows(i), other_half=other_half):
            out[lines] = other_half

        for n, out in enumerate(sends):
            pl.when(lax.div(pl.program_id(0), 2) == n)(functools.partial(put, out))


def back_kernel(
    pos, qf, kf, v, dn, dd, st, ds, fw, matrix, cos, sin1, sin2, gp_o, bias_o, fw_o, *sends
):
    count = qf.shape[0] // LEN_BLK
    step = pl.program_id(1)
    causal = lower(LEN_BLK)
    lane = iota((1, 128), 1)
    first = lane < 64
    turns = cos[...], -sin1[...], -sin2[...]
    halves = split(matrix[...])
    cells = [(i, p) for i in range(count) for p in range(2)]
    rows = lambda i: slice(LEN_BLK * i, LEN_BLK * (i + 1))
    cols = lambda p: slice(128 * p, 128 * p + 128)
    q, k, vv, d, s, t, col = {}, {}, {}, {}, {}, {}, {}
    for i, p in cells:
        q[i, p], k[i, p] = qf[rows(i), cols(p)], kf[rows(i), cols(p)]
        vv[i, p], d[i, p] = v[rows(i), cols(p)], dn[rows(i), cols(p)]
        col[i, p] = [
            jnp.sum(jnp.where(lane == 2 * p + h, dd[0, rows(i)], 0.0), axis=1, keepdims=True)
            for h in range(2)
        ]
    for c in cells:
        s[c] = scores(q[c], k[c], causal)
        raw = dot(jnp.concatenate(each_head(d[c]), 0), vv[c], 1, 1)
        t[c] = [
            jnp.where(causal, raw[LEN_BLK * h : LEN_BLK * (h + 1)] + col[c][h], 0.0).astype(bf16)
            for h in range(2)
        ]
    dq, dk, dv = {}, {}, {}
    for i in range(count):
        state, later = unpack(st[i, 0, :128]), unpack(ds[i, 0, :128])
        for p in range(2):
            c = i, p
            s_hi, s_lo = split(state[p])
            d_hi, d_lo = split(later[p])
            twice = lambda x: jnp.concatenate([x, x], 1)
            dq[c] = dot(twice(d[c]), jnp.concatenate([s_hi, s_lo], 1), 1, 1)
            dk[c] = dot(twice(vv[c]), jnp.concatenate([d_hi, d_lo], 1), 1, 1)
            dv[c] = dot(twice(k[c]), jnp.concatenate([d_hi, d_lo], 0), 1, 0)
    for c in cells:
        dq[c] = dq[c] + dot(jnp.concatenate(t[c], 1), jnp.concatenate(each_head(k[c]), 0), 1, 0)
        dk[c] = dk[c] + dot(jnp.concatenate(t[c], 0), jnp.concatenate(each_head(q[c]), 0), 0, 0)
        dv[c] = dv[c] + dot(jnp.concatenate(s[c], 0), jnp.concatenate(each_head(d[c]), 0), 0, 0)
    for i, p in cells:
        c = i, p
        norm = jnp.where(first, *col[c]) * st[i, 0, 128 + p : 129 + p]
        dq[c] = (dq[c] + norm) * q[c].astype(f32)
        dk[c] = (dk[c] + ds[i, 0, 128 + p : 129 + p]) * k[c].astype(f32)
    whole = lambda parts: jnp.concatenate(
        [jnp.concatenate([parts[i, 0], parts[i, 1]], 1) for i in range(count)], 0
    )
    dq, dk, dv = whole(dq), whole(dk), whole(dv)
    tall = [jnp.concatenate([turn] * count, 0) for turn in turns]
    grads = (
        rotate(three(dq, *halves), *tall).astype(bf16),
        rotate(three(dk, *halves), *tall).astype(bf16),
        dv.astype(bf16),
    )
    for n in range(3):
        gp_o[n] = grads[n]
        wide = grads[n].astype(f32)
        other_half = jnp.where(pos[1] == 0, wide[:, 128:], wide[:, :128])
        sends[n][...] = other_half
    totals = [column_sum(part.astype(f32)) for part in grads]
    totals.append(column_sum(dq + dk) / fw[...])

    @pl.when(step == 0)
    def _():
        for n in range(3):
            bias_o[n] = totals[n]
        fw_o[...] = totals[3]

    @pl.when(step > 0)
    def _():
        for n in range(3):
            bias_o[n] = bias_o[n] + totals[n]
        fw_o[...] = fw_o[...] + totals[3]


def attention_specs(seqs, per, more=0):
    rows = LEN_BLK * per
    return dict(
        grid=(4, seqs // per),
        wide=pl.BlockSpec((rows, 1024), lambda h, g, *_: (g, 0)),
        head=pl.BlockSpec((rows, HG), lambda h, g, *_: (g, h)),
        state=pl.BlockSpec((per, 1, 136, 128), lambda h, g, *_: (g, h, 0, 0)),
        row=pl.BlockSpec((1, HG), lambda h, g, *_: (0, h)),
        table=pl.BlockSpec((256, 256), lambda h, g, *_: (0, 0)),
        dden=pl.BlockSpec((1, rows, 128), lambda h, g, *_: (h, g, 0)),
    )


def features(a1, w_qkv, b_qkv, feat_weight, matrix, turns, valid, after=(), per=4):
    rows = a1.shape[0]
    seqs = rows // LEN_BLK
    s = attention_specs(seqs, per)
    weights = [pl.BlockSpec((1024, HG), lambda h, g, o=o: (0, 4 * o + h)) for o in range(3)]
    biases = [pl.BlockSpec((1, HG), lambda h, g, o=o: (0, 4 * o + h)) for o in range(3)]
    return ordered_call(
        feature_kernel,
        [a1, w_qkv, w_qkv, w_qkv, b_qkv, b_qkv, b_qkv, feat_weight, matrix, *turns, valid],
        after,
        grid=s["grid"],
        in_specs=[s["wide"], *weights, *biases, s["row"]]
        + [s["table"]] * 4
        + [pl.BlockSpec((LEN_BLK * per, 1), lambda h, g: (g, 0))],
        out_specs=[s["head"]] * 3 + [s["state"]],
        out_shape=[struct((rows, 1024), bf16)] * 3 + [struct((seqs, 4, 136, 128), f32)],
        cost_estimate=cost("features"),
        name="features",
    )


def mixing(pos, g, w_out, qf, kf, v, state, after=(), per=2):
    rows = g.shape[0]
    seqs = rows // LEN_BLK
    steps = seqs // per
    s = attention_specs(seqs, per)
    return ordered_call(
        mix_kernel,
        [pos, g, w_out, qf, kf, v, state],
        after,
        prefetch=1,
        grid=s["grid"],
        in_specs=[s["wide"], pl.BlockSpec((HG, 1024), lambda h, g, *_: (h, 0))]
        + [s["head"]] * 3
        + [s["state"]],
        out_specs=[
            s["head"],
            s["head"],
            s["dden"],
            s["state"],
            pl.BlockSpec(
                (LEN_BLK * per, 128),
                lambda h, g, *_: (lax.select(h < 2, g, 0 * g + steps - 1), lax.min(h, 1)),
            ),
            pl.BlockSpec(
                (LEN_BLK * per, 128),
                lambda h, g, *_: (lax.select(h < 2, 0 * g, g), lax.max(h - 2, 0)),
            ),
        ],
        out_shape=[
            struct((rows, 1024), bf16),
            struct((rows, 1024), bf16),
            struct((4, rows, 128), f32),
            struct((seqs, 4, 136, 128), f32),
            struct((rows, 256), f32),
            struct((rows, 256), f32),
        ],
        cost_estimate=cost("mixing"),
        name="mixing",
    )

def backward(pos, qf, kf, v, dn, dd, state, later, feat_weight, matrix, turns, after=(), per=4):
    rows = qf.shape[0]
    seqs = rows // LEN_BLK
    s = attention_specs(seqs, per)
    return ordered_call(
        back_kernel,
        [pos, qf, kf, v, dn, dd, state, later, feat_weight, matrix, *turns],
        after,
        prefetch=1,
        grid=s["grid"],
        in_specs=[s["head"]] * 4
        + [s["dden"], s["state"], s["state"], s["row"]]
        + [s["table"]] * 4,
        out_specs=[
            pl.BlockSpec((3, LEN_BLK * per, HG), lambda h, g, *_: (0, g, h)),
            pl.BlockSpec((3, 1, HG), lambda h, g, *_: (0, 0, h)),
            s["row"],
        ]
        + [pl.BlockSpec((LEN_BLK * per, 128), lambda h, g, *_: (g, h))] * 3,
        out_shape=[
            struct((3, rows, 1024), bf16),
            struct((3, 1, 1024), f32),
            struct((1, 1024), f32),
        ]
        + [struct((rows, 512), f32)] * 3,
        cost_estimate=cost("backward"),
        name="backward",
    )


def norm_parts(x):
    centre = x - jnp.mean(x, axis=-1, keepdims=True)
    r = lax.rsqrt(jnp.mean(centre * centre, axis=-1, keepdims=True) + norm_epsilon)
    return centre * r, r


def norm_back(grad, xhat, r, gain):
    e = grad * gain
    return r * (
        e
        - jnp.mean(e, axis=-1, keepdims=True)
        - xhat * jnp.mean(e * xhat, axis=-1, keepdims=True)
    )


def add_sums(out, sums):
    step = pl.program_id(0)
    new = jnp.concatenate(sums, 0)

    @pl.when(step == 0)
    def _():
        out[...] = new

    @pl.when(step > 0)
    def _():
        out[...] = out[...] + new


def column_sum(x):
    return jnp.sum(x, axis=0, keepdims=True)


def tiles(tile, fixed):
    wide = lambda n: pl.BlockSpec((tile, n), lambda i, *_: (i, 0))
    keep = [once(a.shape, lambda i, *_: (0, 0)) for a in fixed]
    return wide, keep


def norms_kernel(x, g, gain1, bias1, gain2, bias2, a1_o, a2_o, g_o):
    xhat, _ = norm_parts(x[...].astype(f32))
    a1_o[...] = (xhat * gain1[...] + bias1[...]).astype(bf16)
    a2_o[...] = (xhat * gain2[...] + bias2[...]).astype(bf16)
    g_o[...] = g[...].astype(g_o.dtype)


def norms(x, g, *vectors, after=(), g_type=f32):
    rows, tile = x.shape[0], 256
    wide, keep = tiles(tile, vectors)
    return ordered_call(
        norms_kernel,
        [x, g, *vectors],
        after,
        grid=(rows // tile,),
        in_specs=[wide(1024)] * 2 + keep,
        out_specs=[wide(1024)] * 3,
        out_shape=[struct((rows, 1024), bf16)] * 2 + [struct((rows, 1024), g_type)],
        cost_estimate=cost("norms"),
        name="norms",
    )


def hidden_rows_kernel(grad, filled, pos, *refs):
    acts, weights, (send, keep) = refs[:2], refs[2:6], refs[6 + filled :]
    total = None
    for b in range(4):
        act = acts[b % 2]
        act = jnp.concatenate([act[0, 4 * (b // 2) + n] for n in range(4)], 1)
        part = dot(act, weights[b][...], 1, 1 if grad else 0)
        total = part if total is None else total + part
    step = pl.program_id(0)
    steps = pl.num_programs(0) // 2

    @pl.when(step < steps)
    def _():
        send[0] = total

    @pl.when(step >= steps)
    def _():
        keep[...] = total


def hidden_rows(pos, acts, weight, grad, sends=None, after=()):
    rows, tile = acts[0].shape[2], ROW_TILE
    steps = rows // tile
    act = pl.BlockSpec(
        (1, 8, tile, 128), lambda i, p: (1 - lax.div(i, steps), 0, lax.rem(i, steps), 0)
    )
    if grad:
        part = lambda b: once((1024, 512), lambda i, p: (0, 2 * b + p[1]))
    else:
        part = lambda b: once((512, 1024), lambda i, p: (2 * b + p[1], 0))
    filled = [] if sends is None else [sends]
    return ordered_call(
        functools.partial(hidden_rows_kernel, grad, len(filled)),
        [pos, *acts] + [weight] * 4 + filled,
        after,
        prefetch=1,
        grid=(2 * steps,),
        in_specs=[act] * 2
        + [part(b) for b in range(4)]
        + [pl.BlockSpec(memory_space=pl.ANY)] * len(filled),
        out_specs=[
            pl.BlockSpec((1, tile, 1024), lambda i, p: (int(grad), lax.min(i, steps - 1), 0)),
            pl.BlockSpec((tile, 1024), lambda i, p: (lax.max(i - steps, 0), 0)),
        ],
        out_shape=[struct((2, rows, 1024), f32), struct((rows, 1024), f32)],
        input_output_aliases={7: 0} if filled else {},
        cost_estimate=cost(f"hidden{grad:d}"),
        name="hidden_rows",
    )


def result_kernel(x, mixed, own, other, w_out, bias, res_o):
    out = dot(mixed[...], w_out[...], 1, 0) + (own[...] + other[0])
    res_o[...] = (x[...].astype(f32) + out + bias[...]).astype(bf16)


def result_rows(x, mixed, own, other, w_out, bias, after=()):
    rows, tile = x.shape[0], ROW_TILE
    fixed = (w_out, bias)
    wide, keep = tiles(tile, fixed)
    return ordered_call(
        result_kernel,
        [x, mixed, own, other, *fixed],
        after,
        grid=(rows // tile,),
        in_specs=[wide(1024)] * 3 + [pl.BlockSpec((1, tile, 1024), lambda i: (0, i, 0))] + keep,
        out_specs=wide(1024),
        out_shape=struct((rows, 1024), bf16),
        cost_estimate=cost("result_rows"),
        name="result_rows",
    )


def first_norm_kernel(x, g, gp, w_qkv, gain, part_o, sum_o):
    xhat, r = norm_parts(x[...].astype(f32))
    grad_res = g[...].astype(f32)
    grad = dot(jnp.concatenate([gp[0], gp[1], gp[2]], 1), w_qkv[...], 1, 1)
    part_o[...] = grad_res + norm_back(grad, xhat, r, gain[...])
    sums = [column_sum(v) for v in (grad * xhat, grad, grad_res)]
    add_sums(sum_o, sums + [jnp.zeros((5, 1024), f32)])


def first_norm(x, g, gp, w_qkv, gain, after=()):
    rows, tile = x.shape[0], ROW_TILE
    fixed = (w_qkv, gain)
    wide, keep = tiles(tile, fixed)
    return ordered_call(
        first_norm_kernel,
        [x, g, gp, *fixed],
        after,
        grid=(rows // tile,),
        in_specs=[wide(1024)] * 2 + [pl.BlockSpec((3, tile, 1024), lambda i: (0, i, 0))] + keep,
        out_specs=[wide(1024), pl.BlockSpec((8, 1024), lambda i: (0, 0))],
        out_shape=[struct((rows, 1024), f32), struct((8, 1024), f32)],
        cost_estimate=cost("first_norm"),
        name="first_norm",
    )


def second_norm_kernel(x, part, own, other, gain, out_o, sum_o):
    xhat, r = norm_parts(x[...].astype(f32))
    grad = own[...] + other[0]
    out_o[...] = part[...] + norm_back(grad, xhat, r, gain[...])
    sums = [column_sum(v) for v in (grad * xhat, grad)]
    add_sums(sum_o, sums + [jnp.zeros((6, 1024), f32)])


def second_norm(x, part, own, other, gain, after=()):
    rows, tile = x.shape[0], ROW_TILE
    wide, keep = tiles(tile, (gain,))
    return ordered_call(
        second_norm_kernel,
        [x, part, own, other, gain],
        after,
        grid=(rows // tile,),
        in_specs=[wide(1024)] * 3 + [pl.BlockSpec((1, tile, 1024), lambda i: (1, i, 0))] + keep,
        out_specs=[wide(1024), pl.BlockSpec((8, 1024), lambda i: (0, 0))],
        out_shape=[struct((rows, 1024), f32), struct((8, 1024), f32)],
        cost_estimate=cost("second_norm"),
        name="second_norm",
    )


class Links:
    def __init__(self, mesh):
        self.nb, self.ns = mesh.shape["batch"], mesh.shape["seq"]
        self.tuned = (self.nb, self.ns) == (4, 8)

    def send(self, value, move):
        pairs = []
        for b in range(self.nb):
            for s in range(self.ns):
                to = move(b, s)
                if to is not None:
                    pairs.append((b * self.ns + s, to[0] * self.ns + to[1]))
        return lax.ppermute(value, ("batch", "seq"), pairs)

    def core(self, value):
        return self.send(value, lambda b, s: (b, s ^ 1))

    def x(self, value):
        return self.send(value, lambda b, s: (b ^ 1, s))

    def y(self, value):
        return self.send(value, lambda b, s: (b ^ 2, s))

    def ring(self, value, by):
        s = lax.axis_index("seq")
        got = self.send(value, lambda b, s: (b, (s + by) % self.ns))
        kept = s >= by if by > 0 else s < self.ns + by
        return got, kept

    def shift(self, value, by):
        inside = lambda s: 0 <= s < self.ns
        return self.send(value, lambda b, s: (b, s + by) if inside(s + by) else None)


def hold(value, behind):
    behind = [b for b in behind if b is not None]
    return lax.optimization_barrier((value, *behind))[0] if behind else value


class Group:
    def __init__(self, links, x_send, x_keep, y_send, y_keep, at=0):
        self.links, self.at = links, at
        self.keeps = x_keep, y_keep
        self.slots = x_keep.shape[2]
        if links.tuned:
            self.ones = [links.x(x_send), links.y(y_send)]
            self.twos = None

    def arrived(self, *behind):
        self.ones = [hold(one, behind) for one in self.ones]

    def second(self):
        x_out, y_out = second_stage(self.keeps, self.ones, self.at)
        self.twos, self.cut = [self.links.y(y_out), self.links.x(x_out)], None
        return x_out

    def second_in(self, x_send, y_send, into):
        return second_stage(self.keeps, self.ones, self.at, (x_send, y_send), into)

    def second_with(self, group):
        total = group.ones[0].shape[2]
        self.twos = group.ones[::-1]
        self.cut = (0, group.at) if group.at else (group.slots, total)

    def done(self, *behind):
        twos = [hold(two, behind) for two in self.twos]
        return finish(self.keeps, self.ones, self.at, twos, self.cut)


def reduce_z(value):
    groups = [[0, 2, 4, 6], [1, 3, 5, 7]]
    return lax.psum_scatter(
        value, "seq", scatter_dimension=0, axis_index_groups=groups, tiled=True
    )[0]


class Carried:
    def __init__(self, links, state, reverse):
        self.links, self.state, self.reverse = links, state, reverse
        self.sign = -1 if reverse else 1
        self.mine = self.sum = None
        if links.tuned:
            self.core = lax.rem(lax.axis_index("seq"), 2)
            self.half = state.shape[0] // 2
            self.other = links.core(self.of_half(1 - self.core))

    def of_half(self, which):
        return lax.dynamic_slice_in_dim(self.state, which * self.half, self.half, 0)

    def near(self, *behind):
        if not self.links.tuned:
            return None
        self.other = hold(self.other, behind)
        self.mine = self.of_half(self.core) + self.other
        self.one, self.one_kept = self.links.ring(self.mine, self.sign * 2)
        return self.mine

    def far(self, *behind):
        if not self.links.tuned:
            return None
        self.one = jnp.where(self.one_kept, hold(self.one, behind), 0.0)
        self.sum = self.mine + self.one
        self.two, self.two_kept = self.links.ring(self.sum, self.sign * 4)
        return self.sum

    def done(self, *behind):
        links = self.links
        if not links.tuned:
            total, step = self.state, 1
            while step < links.ns:
                total = total + links.shift(total, self.sign * step)
                step *= 2
            return links.shift(total, self.sign)
        self.two = hold(self.two, behind)
        before = self.one + jnp.where(self.two_kept, self.two, 0.0)
        second = self.core == (0 if self.reverse else 1)
        here = before + jnp.where(second, self.other, 0.0)
        there = before + jnp.where(second, 0.0, self.of_half(self.core))
        rest = links.core(there)
        low = jnp.where(self.core == 0, here, rest)
        high = jnp.where(self.core == 0, rest, here)
        return jnp.concatenate([low, high], 0)


class Line:
    def __init__(self, links, value):
        self.z = lax.div(lax.axis_index("seq"), 2)
        self.value = value
        self.parts = []
        for by in (2, 1, 3):
            part = self.pick(lax.rem(self.z + by, 4))
            self.parts.append(links.send(part, lambda b, s: (b, (s + 2 * by) % 8)))

    def pick(self, at):
        return lax.dynamic_index_in_dim(self.value, at, 0, keepdims=False)

    def done(self, *behind):
        total = self.pick(self.z)
        for part in self.parts:
            total = total + hold(part, behind)
        return total


class Halves:
    def __init__(self, links, value):
        self.links = links
        self.z = lax.div(lax.axis_index("seq"), 2)
        both = value.reshape((2, 2) + value.shape[1:])
        low = lax.rem(self.z, 2)
        pick = lambda i: lax.dynamic_index_in_dim(both, i, 1, keepdims=False)
        self.kept = pick(low)
        self.one = links.send(pick(1 - low), lambda b, s: (b, s ^ 2))

    def stage_two(self, *behind):
        self.one = hold(self.one, behind)
        self.high = lax.div(self.z, 2)
        out = self.pick(1 - self.high)
        self.two = self.links.send(out, lambda b, s: (b, s ^ 4))
        return out

    def pick(self, i):
        at = lambda v: lax.dynamic_index_in_dim(v, i, 0, keepdims=False)
        return at(self.kept) + at(self.one)

    def done(self, *behind):
        self.two = hold(self.two, behind)
        return self.pick(self.high) + self.two


def plane_sum(links, rows):
    split_rows = rows.reshape((4, 2) + rows.shape[1:])
    core = lax.rem(lax.axis_index("seq"), 2)
    pick = lambda i: lax.dynamic_index_in_dim(split_rows, i, 1, keepdims=False)
    total = pick(core) + links.core(pick(1 - core))
    total = total + links.x(total)
    return total + links.y(total)


def dct_table(order):
    degree = np.arange(order, dtype=np.float64)[:, None]
    sample = np.arange(order, dtype=np.float64)[None, :]
    table = np.cos(math.pi * (sample + 0.5) * degree / order) * math.sqrt(2.0 / order)
    return np.where(degree == 0.0, table * math.sqrt(0.5), table).astype(np.float32)


def rotation_tables(positions):
    half = ROT // 2
    at = jnp.arange(HG, dtype=jnp.int32) % HEAD_DIM
    inverse = rope_base ** (-2.0 * (at % half).astype(f32) / ROT)
    angles = positions[:, None] * inverse[None, :]
    at = at[None, :]
    sin = jnp.sin(angles)
    return (
        jnp.where(at < ROT, jnp.cos(angles), 1.0),
        jnp.where(at < half, -sin, 0.0),
        jnp.where((at >= half) & (at < ROT), sin, 0.0),
    )


def head_blocks(directions, transposed):
    times = HG // HEAD_DIM
    left = jnp.tile(directions, (times, 1))
    right = np.tile(dct_table(HEAD_DIM), (1, times))
    dims = (((0,), (1,)), ((), ())) if transposed else (((1,), (0,)), ((), ()))
    args = (jnp.asarray(right), left) if transposed else (left, jnp.asarray(right))
    full = lax.dot_general(*args, dims, precision=lax.Precision.HIGHEST)
    block = np.arange(HG) // HEAD_DIM
    return jnp.where(block[:, None] == block[None, :], full, 0.0)


def blocks_kernel(left, right, out):
    full = lax.dot_general(
        left[...],
        right[...],
        (((1,), (0,)), ((), ())),
        precision=lax.Precision.HIGHEST,
        preferred_element_type=f32,
    )
    same = iota((HG, HG), 0) // HEAD_DIM == iota((HG, HG), 1) // HEAD_DIM
    out[...] = jnp.where(same, full, 0.0)


def head_blocks_after(directions, after):
    times = HG // HEAD_DIM
    left = jnp.tile(directions, (times, 1))
    right = jnp.asarray(np.tile(dct_table(HEAD_DIM), (1, times)))
    whole = lambda a: pl.BlockSpec(a.shape, lambda i: (0, 0))
    return ordered_call(
        blocks_kernel,
        [left, right],
        after,
        grid=(1,),
        in_specs=[whole(left), whole(right)],
        out_specs=pl.BlockSpec((HG, HG), lambda i: (0, 0)),
        out_shape=struct((HG, HG), f32),
        cost_estimate=cost("blocks"),
        name="head_blocks",
    )


def per_device(
    links,
    hidden_in,
    cotangent,
    lengths,
    key_mask,
    ln1_gain,
    ln1_bias,
    ln2_gain,
    ln2_bias,
    w_qkv,
    b_qkv,
    w_out,
    b_out,
    w_up,
    b_up,
    w_down,
    b_down,
    feat_weight,
    directions,
):
    seqs, block, width = hidden_in.shape
    rows = seqs * block
    tuned = links.tuned
    place = lax.axis_index("seq")
    me = lax.axis_index("batch") if tuned else 0 * place
    core = lax.rem(place, 2)
    pos = jnp.stack([me, core]).astype(jnp.int32)
    places = place * block + jnp.arange(block, dtype=jnp.int32)
    valid = (places[None, :] < lengths[:, None]) & ((key_mask == 1) | (places[None, :] == 0))
    valid = valid.astype(f32).reshape(rows, 1)
    x = hidden_in.reshape(rows, width)
    g = cotangent.reshape(rows, width)
    row = lambda v: v.reshape(1, -1)
    gains = row(ln1_gain), row(ln1_bias), row(ln2_gain), row(ln2_bias)
    x_other = links.core(x.astype(f32))
    a1, a2, g_wide = norms(x, g, *gains)
    g_other = links.core(g_wide)

    forth = head_blocks(directions, True)
    turns = rotation_tables(places.astype(f32))
    weights = row(feat_weight)

    qf, kf, v, state = features(a1, w_qkv, row(b_qkv), weights, forth, turns, valid)
    forward = Carried(links, state, False)
    a1_o, a2_o, g_o = norms(
        hold(x_other, [state]), hold(g_other, [state]), *gains, g_type=bf16, after=[state]
    )
    ffn = functools.partial(
        ffn_chunk,
        pos=pos,
        a2=(a2, a2_o),
        g=(g, g_o),
        w_up=w_up,
        w_down=w_down,
        b_up=row(b_up),
    )
    c0 = ffn(0, 1, after=[forward.near(a1_o)])
    g0 = Group(links, *c0[4:8])
    c1 = ffn(1, 2, earlier=c0[:4], more=1, after=[forward.far(c0[8])])
    first = list(c1[4:8])
    if tuned:
        g0.arrived(c1[8])
        first[0::2] = g0.second_in(*first[0::2], 4)
    g1 = Group(links, *first)
    state_in = forward.done(c1[8])
    mixed, dn, dd, state_grad, *mixed_send = mixing(
        pos, g, w_out, qf, kf, v, state_in, after=first[:1]
    )
    reverse = Carried(links, state_grad, True)
    mixed_other = [links.core(part) for part in mixed_send]
    back = head_blocks_after(directions, [mixed])
    held = [reverse.near(back)]
    out_pieces = out_grad(
        pos, mixed, [hold(part, [back]) for part in mixed_other], (g, g_o), after=held
    )
    c2 = ffn(3, 1, earlier=c1[:4], filled=out_pieces, after=[reverse.far(out_pieces[0])])
    first = list(c2[4:8])
    z0 = None
    if tuned:
        g1.arrived(c2[8])
        g0.second_with(g1)
        first[0::2] = g1.second_in(*first[0::2], 0)
        z0 = g0.done()
    g2 = Group(links, *first, at=2)
    state_later = reverse.done(c2[8])
    grad_proj, bias_qkv, grad_feat, *grad_send = backward(
        pos,
        qf,
        kf,
        v,
        dn,
        dd,
        state_in,
        state_later,
        weights,
        back,
        turns,
        after=[first[0], z0],
    )
    grad_other = [links.core(part) for part in grad_send]
    last_parts = qkv_grad(
        pos, (a1, a1_o), grad_proj, [hold(part, [grad_proj]) for part in grad_other]
    )
    g3 = Group(links, *last_parts)
    acts = c2[:4]
    held = [last_parts[0]]
    if tuned:
        g2.arrived(last_parts[0])
        g1.second_with(g2)
        z1 = g1.done()
        early = reduce_z(z0), reduce_z(z1)
        held = [z1, g2.second()]
    own_g = hidden_rows(pos, acts[2:], w_up, True, after=held)
    own_r = hidden_rows(pos, acts[:2], w_down, False, own_g[0], after=[own_g[1]])
    others = links.core(own_r[0])
    held = [own_r[1]]
    if tuned:
        g3.arrived(own_r[1])
        held = [g3.second()]
    partial, sums1 = first_norm(x, g, grad_proj, w_qkv, row(ln1_gain), after=held)
    held = [partial]
    if tuned:
        z2 = g2.done(partial)
        middle = Halves(links, z2)
        z3 = g3.done(partial)
        tail = Line(links, z3)
        held = [z2, z3]
    grad_input, sums2 = second_norm(
        x, partial, own_g[1], hold(others, [partial]), row(ln2_gain), after=held
    )
    if tuned:
        middle.stage_two(grad_input)
    result = result_rows(
        x,
        mixed,
        own_r[1],
        hold(others, [partial]),
        w_out,
        row(b_out + b_down),
        after=[grad_input],
    )

    half_up = jnp.concatenate([c[8].reshape(-1, 2, 2, 128) for c in (c0, c1, c2)], 0)
    half_up = half_up.transpose(1, 2, 0, 3).reshape(4, 1, 512)
    b_up_grad = jnp.where(core == np.arange(2)[None, :, None], half_up, 0.0).reshape(-1)
    vectors = [
        sums1[0],
        sums1[1],
        sums2[0],
        sums2[1],
        bias_qkv.reshape(-1),
        sums1[2],
        b_up_grad,
        grad_feat[0],
    ]
    if tuned:
        lines = jnp.concatenate([v_.reshape(8, -1, 128) for v_ in vectors], 1)
        lines = plane_sum(links, jnp.pad(lines, ((0, 0), (0, 3), (0, 0))))
        lines = Line(links, lines).done()
        shares, at = [], 0
        for v_ in vectors:
            n = v_.shape[0] // 1024
            shares.append(lines[at : at + n].reshape(-1))
            at += n
        tail = tail.done(lines)
        middle = middle.done(lines)
        sizes = (1, 2, 1)
        parts = [*early, middle]
        units = [v_[: 2 * n].reshape(n, 2, 128, 128) for v_, n in zip(parts, sizes)]
        halves = jnp.concatenate(units, 0).swapaxes(0, 1)
        start = (2, 4, 3)
        units = [v_[m : m + 2 * n].reshape(n, 2, 128, 128) for v_, n, m in zip(parts, sizes, start)]
        w_down_grad = jnp.concatenate(units, 0).transpose(0, 2, 1, 3).reshape(512, 256)
        w_out_grad = jnp.concatenate([middle[2], middle[5]], 1)
        blocks = [[tail[i] for i in (0, 3, 2)], [tail[i] for i in (1, 4, 5)]]
        blocks = jnp.stack([jnp.stack(b, 0) for b in blocks], 0)
        halves = jnp.concatenate([halves, blocks], 1)
        pick = lambda i: lax.dynamic_index_in_dim(halves, i, 0, keepdims=False)
        mine, other = pick(core), links.core(pick(1 - core))
        first, second = jnp.where(core == 0, mine, other), jnp.where(core == 0, other, mine)
        both = jnp.stack([first, second], 0)
        w_up_grad = both[:, :4].reshape(1024, 128).T
        w_qkv_grad = both[:, 4:].transpose(1, 0, 2, 3).reshape(768, 128).T
    else:
        total = lax.psum(jnp.concatenate(vectors), ("batch", "seq"))
        shares, at = [], 0
        for v_ in vectors:
            share = v_.shape[0] // links.ns
            shares.append(lax.dynamic_slice_in_dim(total, at + place * share, share, 0))
            at += v_.shape[0]

        def scatter(full):
            part = lax.psum_scatter(full, "batch", scatter_dimension=1, tiled=True)
            return lax.psum_scatter(part, "seq", scatter_dimension=0, tiled=True)

        def of_core(half, axis):
            zero = jnp.zeros_like(half)
            pair = jnp.where(core == 0, half, zero), jnp.where(core == 1, half, zero)
            return jnp.stack(pair, axis)

        both = lambda send, keep: jnp.stack([keep, send], 0)
        groups = (c0, c1, c2)
        slots = lambda pair, n, m, k: both(pair[0][:, :, m : m + n], pair[1][:, :, k : k + n])
        sizes = ((2, 0, 0), (4, 0, 0), (2, 2, 0))
        up = [slots(c[4:6], *size) for c, size in zip(groups, sizes)]
        up = jnp.concatenate(up, 3).reshape(2, 2, 4, 4, 2, 128, 128)
        up = of_core(up.transpose(2, 4, 6, 1, 0, 3, 5).reshape(1024, 4, 512), 2)
        down = [slots(c[6:8], *size) for c, size in zip(groups, sizes)]
        down = jnp.concatenate(down, 3).reshape(2, 2, 4, 4, 2, 128, 128)
        down = of_core(down.transpose(2, 3, 5, 0, 1, 4, 6).reshape(4, 512, 1024), 1)
        by_x = slots(out_pieces[:2], 1, 4, 2).swapaxes(0, 1)
        out = jnp.concatenate([by_x, slots(out_pieces[2:], 1, 4, 2)], 3)
        out = out.transpose(2, 4, 0, 1, 3, 5).reshape(4, 128, 1024)
        by_x = both(*last_parts[:2]).swapaxes(0, 1)
        by_y = both(*last_parts[2:])
        parts = [by_x[:, :, :, :2], by_y[:, :, :, :2]]
        parts.append(jnp.stack([by_x[:, :, :, 2], by_y[:, :, :, 2]], 3))
        qkv = [p.transpose(2, 3, 5, 0, 1, 4).reshape(1024, 4, 128) for p in parts]
        w_up_grad = scatter(up.reshape(1024, 4096))
        w_down_grad = scatter(down.reshape(4096, 1024))
        w_out_grad = scatter(of_core(out, 1).reshape(1024, 1024))
        w_qkv_grad = scatter(of_core(jnp.stack(qkv, 2), 3).reshape(1024, 3072))

    shape = hidden_in.shape
    return (
        result.reshape(shape),
        grad_input.reshape(shape),
        shares[0],
        shares[1],
        shares[2],
        shares[3],
        w_qkv_grad,
        shares[4],
        w_out_grad,
        shares[5],
        w_up_grad,
        shares[6],
        w_down_grad,
        shares[5],
        shares[7],
    )


def solution(mesh):
    links = Links(mesh)
    rows = P("batch", "seq", None)
    spread = P("seq", "batch")
    return jax.shard_map(
        functools.partial(per_device, links),
        mesh=mesh,
        in_specs=(rows, rows, P("batch"), P("batch", "seq")) + (P(),) * 14,
        out_specs=(rows, rows)
        + (P("seq"),) * 4
        + (spread, P("seq"), spread, P("seq"), spread, P("seq"), spread, P("seq"), P("seq")),
        check_vma=False,
    )
```

time: 580 us -> 431 us (0.74)
  the two profiles are of different devices: /device:TPU:16 before, /device:TPU:1 now
where the time goes in v2:
time: 431 us; the launch traced here: 424 us
  Pallas kernels  255 us (59%)
  waiting for transfers between devices  67.5 us (16%)
  starting transfers between devices  38.2 us (9%)
  other arithmetic  25.5 us (6%)
  local copies, waits for them, and re-layouts  22.1 us (5%)
  between operations  14.9 us (3%)
    pallas_call x24, Pallas kernels, ordered_call(): pl.pallas_call(body, grid_spec=pltpu.PrefetchScalarGridSpec(num_scalar_pr...  255 us
    ppermute x40, waiting for transfers between devices, send(): return lax.ppermute(value, ('batch', 'seq'), pairs)  67.5 us
    ppermute x40, starting transfers between devices, send(): return lax.ppermute(value, ('batch', 'seq'), pairs)  38.1 us
    unnamed x75, local copies, waits for them, and re-layouts  10.1 us
  transfers between devices with their start and end apart: 42, of which 11 were waited for; matrix products, arithmetic and copies ran while one was open for 8% of the time, Pallas kernels for 58%

profile of v2, /device:TPU:1, one launch (start us, length us, event | category | flops | bytes accessed | tf_op | source)
XLA Modules:
  0.0 423.8 jit_solution(7263012815193757766)
XLA Ops:
  7.2 6.8 %norms.2 = (bf16[1024,1024]{1,0:T(8,128)(2,1)}, bf16[1024,1024]{1,0:T(8,128)(2,1)}, f32[1024,1024]{1,0:T(8,128)}) custom-call(bf16[1024,1024]{1,0:T(8,128)(2,1)} %bitcast.164, bf16[1024,1024]{1,0:T(8,128)(2,1)} %bitcast.157, f32[1,1024]{1,0:T(1,128)} %bitcast.203, f32[1,1024]{1,0:T(1,128)} %bitcast.199, f32[1,1024]{1,0:T(1,128)} %bitcast.194, ...), custom_call_target="tpu_custom_call" | custom-call | flops 1 | bytes 1 | tf_op jit(solution)/shard_map/norms/pallas_call | solution.py:53
  21.5 17.2 %features.1 = (bf16[1024,1024]{1,0:T(8,128)(2,1)}, bf16[1024,1024]{1,0:T(8,128)(2,1)}, bf16[1024,1024]{1,0:T(8,128)(2,1)}, f32[4,4,136,128]{3,2,1,0:T(8,128)}) custom-call(bf16[1024,1024]{1,0:T(8,128)(2,1)} %get-tuple-element.119.refs_0_.refs_1_, bf16[1024,3072]{1,0:T(8,128)(2,1)} %refs_3_.7, bf16[1024,3072]{1,0:T(8,128)(2,1)} %refs_3_.7, ...), custom_call_target="tpu_custom_call" | custom-call | flops 1 | bytes 1 | tf_op jit(solution)/shard_map/features/pallas_call | solution.py:53
  39.9 7.1 %norms.3 = (bf16[1024,1024]{1,0:T(8,128)(2,1)}, bf16[1024,1024]{1,0:T(8,128)(2,1)}, bf16[1024,1024]{1,0:T(8,128)(2,1)}) custom-call(f32[1024,1024]{1,0:T(8,128)} %collective-permute-done.1.refs_0_, f32[1024,1024]{1,0:T(8,128)} %collective-permute-done.2.refs_1_, f32[1,1024]{1,0:T(1,128)} %bitcast.204, f32[1,1024]{1,0:T(1,128)} %bitcast.200, ...), custom_call_target="tpu_custom_call" | custom-call | flops 1 | bytes 1 | tf_op jit(solution)/shard_map/norms/pallas_call | solution.py:53
  50.5 16.9 %ffn_chunk.3 = (bf16[2,8,1024,128]{3,2,1,0:T(8,128)(2,1)}, bf16[2,8,1024,128]{3,2,1,0:T(8,128)(2,1)}, bf16[2,8,1024,128]{3,2,1,0:T(8,128)(2,1)}, bf16[2,8,1024,1...) custom-call(s32[2]{0:T(128)} %pad_add_fusion.refs_0_, ...), custom_call_target="tpu_custom_call" | custom-call | flops 1 | bytes 1 | tf_op jit(solution)/shard_map/ffn_chunk/pallas_call | solution.py:53
  74.3 27.3 %ffn_chunk.4 = (bf16[2,8,1024,128]{3,2,1,0:T(8,128)(2,1)}, bf16[2,8,1024,128]{3,2,1,0:T(8,128)(2,1)}, bf16[2,8,1024,128]{3,2,1,0:T(8,128)(2,1)}, bf16[2,8,1024,1...) custom-call(s32[2]{0:T(128)} %pad_add_fusion.refs_0_, ...), custom_call_target="tpu_custom_call", output_to_operand_aliasing={{0}: (11, {}), {1}: (12, {}), {2}: (13, {}), {3}: (14, {})} | custom-call | flops 1 | bytes 1 | tf_op jit(solution)/shard_map/ffn_chunk/pallas_call | solution.py:53
  110.6 17.9 %mixing.1 = (bf16[1024,1024]{1,0:T(8,128)(2,1)}, bf16[1024,1024]{1,0:T(8,128)(2,1)}, f32[4,1024,128]{2,1,0:T(8,128)}, f32[4,4,136,128]{3,2,1,0:T(8,128)}, f32[1024,256]{1,0:T(8,128)}, /*index=5*/f32[1024,256]{1,0:T(8,128)}) custom-call(s32[2]{0:T(128)} %pad_add_fusion.refs_0_, bf16[1024,1024]{1,0:T(8,128)(2,1)} %bitcast.160, bf16[1024,1024]{1,0:T(8,128)(2,1)} %refs_4_.5, ...), custom_call_target="tpu_custom_call" | custom-call | flops 1 | bytes 1 | tf_op jit(solution)/shard_map/mixing/pallas_call | solution.py:53
  136.8 8.0 %out_grad.1 = (f32[2,4,5,128,128]{4,3,2,1,0:T(8,128)}, f32[2,4,3,128,128]{4,3,2,1,0:T(8,128)}, f32[2,4,5,128,128]{4,3,2,1,0:T(8,128)}, f32[2,4,3,128,128]{4,3,2,1,0:T(8,128)}) custom-call(s32[2]{0:T(128)} %pad_add_fusion.refs_0_, bf16[1024,1024]{1,0:T(8,128)(2,1)} %get-tuple-element.149.refs_2_.refs_1_, f32[1024,256]{1,0:T(8,128)} %collective-permute-done.8.refs_2_, ...), custom_call_target="tpu_custom_call" | custom-call | flops 1 | bytes 1 | tf_op jit(solution)/shard_map/out_grad/pallas_call | solution.py:53
  144.8 4.2 collective-permute-done.11
  151.4 16.7 %ffn_chunk.5 = (bf16[2,8,1024,128]{3,2,1,0:T(8,128)(2,1)}, bf16[2,8,1024,128]{3,2,1,0:T(8,128)(2,1)}, bf16[2,8,1024,128]{3,2,1,0:T(8,128)(2,1)}, bf16[2,8,1024,1...) custom-call(s32[2]{0:T(128)} %pad_add_fusion.refs_0_, ...), custom_call_target="tpu_custom_call", output_to_operand_aliasing={{0}: (11, {}), {1}: (12, {}), {2}: (13, {}), {3}: (14, {}),... | custom-call | flops 1 | bytes 1 | tf_op jit(solution)/shard_map/ffn_chunk/pallas_call | solution.py:53
  168.2 8.4 %collective-permute-done.15 = f32[2,4,136,128]{3,2,1,0:T(8,128)} collective-permute-done((f32[2,4,136,128]{3,2,1,0:T(8,128)S(1)}, f32[2,4,136,128]{3,2,1,0:T(8,128)}, u32[]{:S(2)}, u32[]{:S(2)}) %collective-permute-start.15) | collective-permute-done | bytes 557088 | tf_op jit(solution)/shard_map/ppermute | solution.py:883
  182.3 3.4 second_stage.5
  188.2 4.1 finish.4.refs_14_
  194.7 27.1 %backward.1 = (bf16[3,1024,1024]{2,1,0:T(8,128)(2,1)}, f32[3,1,1024]{2,1,0:T(1,128)}, f32[1,1024]{1,0:T(1,128)}, f32[1024,512]{1,0:T(8,128)}, f32[1024,512]{1,0:T(8,128)}, /*index=5*/f32[1024,512]{1,0:T(8,128)}) custom-call(s32[2]{0:T(128)} %pad_add_fusion.refs_0_, bf16[1024,1024]{1,0:T(8,128)(2,1)} %get-tuple-element.120.refs_3_.refs_1_, ...), custom_call_target="tpu_custom_call" | custom-call | flops 1 | bytes 1 | tf_op jit(solution)/shard_map/backward/pallas_call | solution.py:53
  232.6 15.1 %qkv_grad.1 = (f32[2,4,3,128,128]{4,3,2,1,0:T(8,128)}, f32[2,4,3,128,128]{4,3,2,1,0:T(8,128)}, f32[2,4,3,128,128]{4,3,2,1,0:T(8,128)}, f32[2,4,3,128,128]{4,3,2,1,0:T(8,128)}) custom-call(s32[2]{0:T(128)} %pad_add_fusion.refs_0_, bf16[1024,1024]{1,0:T(8,128)(2,1)} %get-tuple-element.119.refs_0_.refs_1_, bf16[1024,1024]{1,0:T(8,128)(2,1)} %get-tuple-element.127.refs_2_, ...), custom_call_target="tpu_custom_call" | custom-call | flops 1 | bytes 1 | tf_op jit(solution)/shard_map/qkv_grad/pallas_call | solution.py:53
  249.7 5.4 %finish.5.refs_7_ = f32[4,8,128,128]{3,2,1,0:T(8,128)} custom-call(f32[2,4,4,128,128]{4,3,2,1,0:T(8,128)} %get-tuple-element.169.refs_0_, f32[2,4,5,128,128]{4,3,2,1,0:T(8,128)} %collective-permute-done.12.refs_1_.refs_5_, f32[2,4,5,128,128]{4,3,2,1,0:T(8,128)} %collective-permute-done.14.refs_2_.refs_3_.refs_4_, ...), custom_call_target="tpu_custom_call" | custom-call | flops 1 | bytes 1 | tf_op jit(solution)/shard_map/finish/pallas_call | solution.py:53
  260.8 16.2 %hidden_rows.2 = (f32[2,1024,1024]{2,1,0:T(8,128)}, f32[1024,1024]{1,0:T(8,128)}) custom-call(s32[2]{0:T(128)} %pad_add_fusion.refs_0_, bf16[2,8,1024,128]{3,2,1,0:T(8,128)(2,1)} %get-tuple-element.167.refs_1_, bf16[2,8,1024,128]{3,2,1,0:T(8,128)(2,1)} %get-tuple-element.168.refs_2_, bf16[1024,4096]{1,0:T(8,128)(2,1)} %refs_6_.8, ...), custom_call_target="tpu_custom_call" | custom-call | flops 1 | bytes 1 | tf_op jit(solution)/shard_map/hidden_rows/pallas_call | solution.py:53
  277.0 15.9 %hidden_rows.3 = (f32[2,1024,1024]{2,1,0:T(8,128)}, f32[1024,1024]{1,0:T(8,128)}) custom-call(s32[2]{0:T(128)} %pad_add_fusion.refs_0_, bf16[2,8,1024,128]{3,2,1,0:T(8,128)(2,1)} %get-tuple-element.165.refs_1_, bf16[2,8,1024,128]{3,2,1,0:T(8,128)(2,1)} %get-tuple-element.166.refs_2_, bf16[4096,1024]{1,0:T(8,128)(2,1)} %refs_6_.9, ...), custom_call_target="tpu_custom_call", output_to_operand_aliasing={{0}: (7, {})} | custom-call | flops 99999997952 | bytes 1 | tf_op jit(solution)/shard_map/hidden_rows/pallas_call | solution.py:53
  297.6 14.6 %first_norm.1 = (f32[1024,1024]{1,0:T(8,128)}, f32[8,1024]{1,0:T(8,128)}) custom-call(bf16[1024,1024]{1,0:T(8,128)(2,1)} %bitcast.165, bf16[1024,1024]{1,0:T(8,128)(2,1)} %bitcast.163, bf16[3,1024,1024]{2,1,0:T(8,128)(2,1)} %get-tuple-element.182.refs_3_.refs_4_.refs_5_.refs_2_, bf16[1024,3072]{1,0:T(8,128)(2,1)} %refs_3_.7, f32[1,1024]{1,0:T(1,128)} %bitcast.205, ...), custom_call_target="tpu_custom_call" | custom-call | flops 99999997952 | bytes 1 | tf_op jit(solution)/shard_map/first_norm/pallas_call | solution.py:53
  312.2 3.7 finish.6.refs_5_
  322.3 8.9 %second_norm.1 = (f32[1024,1024]{1,0:T(8,128)}, f32[8,1024]{1,0:T(8,128)}) custom-call(bf16[1024,1024]{1,0:T(8,128)(2,1)} %bitcast.166, f32[1024,1024]{1,0:T(8,128)} %get-tuple-element.205.refs_1_, f32[1024,1024]{1,0:T(8,128)} %get-tuple-element.196.refs_8_.refs_2_, f32[2,1024,1024]{2,1,0:T(8,128)} %collective-permute-done.21.refs_3_, f32[1,1024]{1,0:T(1,128)} %bitcast.196, ...), custom_call_target="tpu_custom_call" | custom-call | flops 1 | bytes 1 | tf_op jit(solution)/shard_map/second_norm/pallas_call | solution.py:53
  346.8 15.8 %collective-permute-done.34 = f32[2,6,128,128]{3,2,1,0:T(8,128)} collective-permute-done((f32[2,6,128,128]{3,2,1,0:T(8,128)}, f32[2,6,128,128]{3,2,1,0:T(8,128)}, u32[]{:S(2)}, u32[]{:S(2)}) %collective-permute-start.34) | collective-permute-done | bytes 786464 | tf_op jit(solution)/shard_map/ppermute | solution.py:883
  362.6 15.0 %collective-permute-done.31 = f32[16,128]{1,0:T(8,128)S(1)} collective-permute-done((f32[16,128]{1,0:T(8,128)S(1)}, f32[16,128]{1,0:T(8,128)S(1)}, u32[]{:S(2)}, u32[]{:S(2)}) %collective-permute-start.31) | collective-permute-done | bytes 8224 | tf_op jit(solution)/shard_map/ppermute | solution.py:883
  381.1 8.6 %result_rows.1 = bf16[1024,1024]{1,0:T(8,128)(2,1)} custom-call(bf16[1024,1024]{1,0:T(8,128)(2,1)} %bitcast.167, bf16[1024,1024]{1,0:T(8,128)(2,1)} %get-tuple-element.149.refs_2_.refs_1_, f32[1024,1024]{1,0:T(8,128)} %get-tuple-element.197.refs_2_, f32[2,1024,1024]{2,1,0:T(8,128)} %collective-permute-done.21.refs_3_, bf16[1024,1024]{1,0:T(8,128)(2,1)} %refs_4_.5, ...), custom_call_target="tpu_custom_call" | custom-call | flops 1 | bytes 1 | tf_op jit(solution)/shard_map/result_rows/pallas_call | solution.py:53
  394.9 15.0 %collective-permute-done.35 = f32[6,128,128]{2,1,0:T(8,128)S(1)} collective-permute-done((f32[6,128,128]{2,1,0:T(8,128)}, f32[6,128,128]{2,1,0:T(8,128)S(1)}, u32[]{:S(2)}, u32[]{:S(2)}) %collective-permute-start.35) | collective-permute-done | bytes 393248 | tf_op jit(solution)/shard_map/ppermute | solution.py:883
  (230 shorter events, 109.7 us)
Async XLA Ops:
  7.2 327.8 %reduce-scatter.3.cloned.1.call-start = ((), (), s32[]{:S(2)}) async-start(), calls=%async_computation.2 | async-start | bytes 1310720 | tf_op jit(solution)/shard_map/reduce_scatter | solution.py:942
  14.0 25.9 %collective-permute-start.2 = (f32[1024,1024]{1,0:T(8,128)}, f32[1024,1024]{1,0:T(8,128)}, u32[]{:S(2)}, u32[]{:S(2)}) collective-permute-start(f32[1024,1024]{1,0:T(8,128)} %get-tuple-element.125), channel_id=1, source_target_pairs={{0,1},{1,0},{2,3},{3,2},{4,5},{5,4},{6,7},{7,6},{8,9},{9,8},{10,11... | collective-permute-start | bytes 12582920 | tf_op jit(solution)/shard_map/ppermute | solution.py:883
  16.8 23.1 %collective-permute-start.1 = (f32[1024,1024]{1,0:T(8,128)}, f32[1024,1024]{1,0:T(8,128)}, u32[]{:S(2)}, u32[]{:S(2)}) collective-permute-start(f32[1024,1024]{1,0:T(8,128)} %bitcast_convert_fusion), channel_id=1, source_target_pairs={{0,1},{1,0},{2,3},{3,2},{4,5},{5,4},{6,7},{7,6},{8,9},{9,8},{10,11... | collective-permute-start | bytes 12582920 | tf_op jit(solution)/shard_map/ppermute | solution.py:883
  47.1 20.3 %collective-permute-start.3 = (f32[2,4,136,128]{3,2,1,0:T(8,128)S(1)}, f32[2,4,136,128]{3,2,1,0:T(8,128)S(1)}, u32[]{:S(2)}, u32[]{:S(2)}) collective-permute-start(f32[2,4,136,128]{3,2,1,0:T(8,128)S(1)} %dynamic-slice_add_fusion.1.refs_11_), channel_id=1, source_target_pairs={{0,2},{1,3},{2,4},{3,5},{4,6},{5,7},{6,0},{7,1},{8,10},{9,11},{10,... | collective-permute-start | bytes 1671176 | tf_op jit(solution)/shard_map/ppermute | solution.py:883
  69.5 32.1 %collective-permute-start.4 = (f32[2,4,136,128]{3,2,1,0:T(8,128)}, f32[2,4,136,128]{3,2,1,0:T(8,128)}, u32[]{:S(2)}, u32[]{:S(2)}) collective-permute-start(f32[2,4,136,128]{3,2,1,0:T(8,128)} %select_add_fusion.7.refs_15_), channel_id=1, source_target_pairs={{0,4},{1,5},{2,6},{3,7},{4,0},{5,1},{6,2},{7,3},{8,12},{9,13},{10,... | collective-permute-start | bytes 1671176 | tf_op jit(solution)/shard_map/ppermute | solution.py:883
  71.9 32.1 %collective-permute-start.7 = (f32[2,4,2,128,128]{4,3,2,1,0:T(8,128)}, f32[2,4,2,128,128]{4,3,2,1,0:T(8,128)S(1)}, u32[]{:S(2)}, u32[]{:S(2)}) collective-permute-start(f32[2,4,2,128,128]{4,3,2,1,0:T(8,128)} %get-tuple-element.144), channel_id=1, source_target_pairs={{0,16},{1,17},{2,18},{3,19},{4,20},{5,21},{6,22},{7,23},{8,24},{9,... | collective-permute-start | bytes 3145736 | tf_op jit(solution)/shard_map/ppermute | solution.py:883
  73.1 30.9 %collective-permute-start.6 = (f32[2,4,2,128,128]{4,3,2,1,0:T(8,128)}, f32[2,4,2,128,128]{4,3,2,1,0:T(8,128)S(1)}, u32[]{:S(2)}, u32[]{:S(2)}) collective-permute-start(f32[2,4,2,128,128]{4,3,2,1,0:T(8,128)} %get-tuple-element.141), channel_id=1, source_target_pairs={{0,8},{1,9},{2,10},{3,11},{4,12},{5,13},{6,14},{7,15},{8,0},{9,1},... | collective-permute-start | bytes 3145736 | tf_op jit(solution)/shard_map/ppermute | solution.py:883
  107.7 73.1 %collective-permute-start.13 = (f32[2,4,5,128,128]{4,3,2,1,0:T(8,128)}, f32[2,4,5,128,128]{4,3,2,1,0:T(8,128)S(1)}, u32[]{:S(2)}, u32[]{:S(2)}) collective-permute-start(f32[2,4,5,128,128]{4,3,2,1,0:T(8,128)} %get-tuple-element.173), channel_id=1, source_target_pairs={{0,16},{1,17},{2,18},{3,19},{4,20},{5,21},{6,22},{7,23},{8,24},{9,... | collective-permute-start | bytes 7864328 | tf_op jit(solution)/shard_map/ppermute | solution.py:883
  107.9 72.9 %collective-permute-start.12 = (f32[2,4,5,128,128]{4,3,2,1,0:T(8,128)}, f32[2,4,5,128,128]{4,3,2,1,0:T(8,128)}, u32[]{:S(2)}, u32[]{:S(2)}) collective-permute-start(f32[2,4,5,128,128]{4,3,2,1,0:T(8,128)} %get-tuple-element.148.refs_7_), channel_id=1, source_target_pairs={{0,8},{1,9},{2,10},{3,11},{4,12},{5,13},{6,14},{7,15},{8,0},{9,1},... | collective-permute-start | bytes 7864328 | tf_op jit(solution)/shard_map/ppermute | solution.py:883
  150.3 26.3 %collective-permute-start.15 = (f32[2,4,136,128]{3,2,1,0:T(8,128)S(1)}, f32[2,4,136,128]{3,2,1,0:T(8,128)}, u32[]{:S(2)}, u32[]{:S(2)}) collective-permute-start(f32[2,4,136,128]{3,2,1,0:T(8,128)S(1)} %select_add_fusion.6.refs_19_), channel_id=1, source_target_pairs={{0,4},{1,5},{2,6},{3,7},{4,0},{5,1},{6,2},{7,3},{8,12},{9,13},{10,... | collective-permute-start | bytes 1671176 | tf_op jit(solution)/shard_map/ppermute | solution.py:883
  185.7 62.4 %collective-permute-start.20 = (f32[2,4,5,128,128]{4,3,2,1,0:T(8,128)}, f32[2,4,5,128,128]{4,3,2,1,0:T(8,128)S(1)}, u32[]{:S(2)}, u32[]{:S(2)}) collective-permute-start(f32[2,4,5,128,128]{4,3,2,1,0:T(8,128)} %get-tuple-element.181.refs_13_), channel_id=1, source_target_pairs={{0,8},{1,9},{2,10},{3,11},{4,12},{5,13},{6,14},{7,15},{8,0},{9,1},... | collective-permute-start | bytes 7864328 | tf_op jit(solution)/shard_map/ppermute | solution.py:883
  186.9 61.2 %collective-permute-start.14 = (f32[2,4,5,128,128]{4,3,2,1,0:T(8,128)}, f32[2,4,5,128,128]{4,3,2,1,0:T(8,128)}, u32[]{:S(2)}, u32[]{:S(2)}) collective-permute-start(f32[2,4,5,128,128]{4,3,2,1,0:T(8,128)} %get-tuple-element.177), channel_id=1, source_target_pairs={{0,16},{1,17},{2,18},{3,19},{4,20},{5,21},{6,22},{7,23},{8,24},{9,... | collective-permute-start | bytes 7864328 | tf_op jit(solution)/shard_map/ppermute | solution.py:883
  224.5 121.3 %reduce-scatter.5.cloned.1.call-start = ((), (), s32[]{:S(2)}) async-start(), calls=%async_computation.3 | async-start | bytes 2621440 | tf_op jit(solution)/shard_map/reduce_scatter | solution.py:942
  247.7 46.8 %collective-permute-start.23 = (f32[2,4,3,128,128]{4,3,2,1,0:T(8,128)}, f32[2,4,3,128,128]{4,3,2,1,0:T(8,128)}, u32[]{:S(2)}, u32[]{:S(2)}) collective-permute-start(f32[2,4,3,128,128]{4,3,2,1,0:T(8,128)} %get-tuple-element.202), channel_id=1, source_target_pairs={{0,16},{1,17},{2,18},{3,19},{4,20},{5,21},{6,22},{7,23},{8,24},{9,... | collective-permute-start | bytes 4718600 | tf_op jit(solution)/shard_map/ppermute | solution.py:883
  247.9 46.6 %collective-permute-start.22 = (f32[2,4,3,128,128]{4,3,2,1,0:T(8,128)}, f32[2,4,3,128,128]{4,3,2,1,0:T(8,128)}, u32[]{:S(2)}, u32[]{:S(2)}) collective-permute-start(f32[2,4,3,128,128]{4,3,2,1,0:T(8,128)} %get-tuple-element.189), channel_id=1, source_target_pairs={{0,8},{1,9},{2,10},{3,11},{4,12},{5,13},{6,14},{7,15},{8,0},{9,1},... | collective-permute-start | bytes 4718600 | tf_op jit(solution)/shard_map/ppermute | solution.py:883
  258.2 53.9 %collective-permute-start.25 = (f32[4,3,128,128]{3,2,1,0:T(8,128)}, f32[4,3,128,128]{3,2,1,0:T(8,128)}, u32[]{:S(2)}, u32[]{:S(2)}) collective-permute-start(f32[4,3,128,128]{3,2,1,0:T(8,128)} %get-tuple-element.194.refs_8_), channel_id=1, source_target_pairs={{0,8},{1,9},{2,10},{3,11},{4,12},{5,13},{6,14},{7,15},{8,0},{9,1},... | collective-permute-start | bytes 2359304 | tf_op jit(solution)/shard_map/ppermute | solution.py:883
  259.4 52.7 %collective-permute-start.24 = (f32[4,3,128,128]{3,2,1,0:T(8,128)}, f32[4,3,128,128]{3,2,1,0:T(8,128)}, u32[]{:S(2)}, u32[]{:S(2)}) collective-permute-start(f32[4,3,128,128]{3,2,1,0:T(8,128)} %get-tuple-element.207), channel_id=1, source_target_pairs={{0,16},{1,17},{2,18},{3,19},{4,20},{5,21},{6,22},{7,23},{8,24},{9,... | collective-permute-start | bytes 2359304 | tf_op jit(solution)/shard_map/ppermute | solution.py:883
  292.9 29.4 %collective-permute-start.21 = (f32[2,1024,1024]{2,1,0:T(8,128)}, f32[2,1024,1024]{2,1,0:T(8,128)}, u32[]{:S(2)}, u32[]{:S(2)}) collective-permute-start(f32[2,1024,1024]{2,1,0:T(8,128)} %get-tuple-element.198), channel_id=1, source_target_pairs={{0,1},{1,0},{2,3},{3,2},{4,5},{5,4},{6,7},{7,6},{8,9},{9,8},{10,11... | collective-permute-start | bytes 25165832 | tf_op jit(solution)/shard_map/ppermute | solution.py:883
  334.7 27.9 %collective-permute-start.34 = (f32[2,6,128,128]{3,2,1,0:T(8,128)}, f32[2,6,128,128]{3,2,1,0:T(8,128)}, u32[]{:S(2)}, u32[]{:S(2)}) collective-permute-start(f32[2,6,128,128]{3,2,1,0:T(8,128)} %dynamic-slice_bitcast_fusion), channel_id=1, source_target_pairs={{0,2},{1,3},{2,0},{3,1},{4,6},{5,7},{6,4},{7,5},{8,10},{9,11},{10,... | collective-permute-start | bytes 2359304 | tf_op jit(solution)/shard_map/ppermute | solution.py:883
  340.0 51.7 %collective-permute-start.36 = (f32[6,128,128]{2,1,0:T(8,128)}, f32[6,128,128]{2,1,0:T(8,128)}, u32[]{:S(2)}, u32[]{:S(2)}) collective-permute-start(f32[6,128,128]{2,1,0:T(8,128)} %get-tuple-element.246), channel_id=1, source_target_pairs={{0,4},{1,5},{2,6},{3,7},{4,0},{5,1},{6,2},{7,3},{8,12},{9,13},{10,... | collective-permute-start | bytes 1179656 | tf_op jit(solution)/shard_map/ppermute | solution.py:883
  342.3 49.4 %collective-permute-start.37 = (f32[6,128,128]{2,1,0:T(8,128)}, f32[6,128,128]{2,1,0:T(8,128)}, u32[]{:S(2)}, u32[]{:S(2)}) collective-permute-start(f32[6,128,128]{2,1,0:T(8,128)} %get-tuple-element.248), channel_id=1, source_target_pairs={{0,2},{1,3},{2,4},{3,5},{4,6},{5,7},{6,0},{7,1},{8,10},{9,11},{10,... | collective-permute-start | bytes 1179656 | tf_op jit(solution)/shard_map/ppermute | solution.py:883
  342.3 49.4 %collective-permute-start.38 = (f32[6,128,128]{2,1,0:T(8,128)}, f32[6,128,128]{2,1,0:T(8,128)}, u32[]{:S(2)}, u32[]{:S(2)}) collective-permute-start(f32[6,128,128]{2,1,0:T(8,128)} %get-tuple-element.247), channel_id=1, source_target_pairs={{0,6},{1,7},{2,0},{3,1},{4,2},{5,3},{6,4},{7,5},{8,14},{9,15},{10,... | collective-permute-start | bytes 1179656 | tf_op jit(solution)/shard_map/ppermute | solution.py:883
  345.6 31.9 %collective-permute-start.31 = (f32[16,128]{1,0:T(8,128)S(1)}, f32[16,128]{1,0:T(8,128)S(1)}, u32[]{:S(2)}, u32[]{:S(2)}) collective-permute-start(f32[16,128]{1,0:T(8,128)S(1)} %get-tuple-element.263), channel_id=1, source_target_pairs={{0,4},{1,5},{2,6},{3,7},{4,0},{5,1},{6,2},{7,3},{8,12},{9,13},{10,... | collective-permute-start | bytes 24584 | tf_op jit(solution)/shard_map/ppermute | solution.py:883
  362.6 27.2 %collective-permute-start.32 = (f32[16,128]{1,0:T(8,128)S(1)}, f32[16,128]{1,0:T(8,128)S(1)}, u32[]{:S(2)}, u32[]{:S(2)}) collective-permute-start(f32[16,128]{1,0:T(8,128)S(1)} %get-tuple-element.265), channel_id=1, source_target_pairs={{0,2},{1,3},{2,4},{3,5},{4,6},{5,7},{6,0},{7,1},{8,10},{9,11},{10,... | collective-permute-start | bytes 24584 | tf_op jit(solution)/shard_map/ppermute | solution.py:883
  (53 other events, 542.8 us)
Sparse Core Ops, SparseCore 0:
  224.6 24.1 reduce-scatter.2
  294.6 40.8 reduce-scatter.4

commit v3 on v2

--- a/solution.py
+++ b/solution.py
@@ -139,7 +139,6 @@
     args = args + [value for _, value in given]
     pieces = [struct((2, 4, 2 * count + extra, 128, 128), f32) for extra in (more, 0)] * 2
     pieces = [struct(v.shape, f32) for v in filled] or pieces
-    skip = 1 if filled else 0
     return ordered_call(
         functools.partial(ffn_kernel, len(given)),
         args,
@@ -151,14 +150,11 @@
         + [
             pl.BlockSpec(
                 (1, 4, 2, 128, 128),
-                lambda k, i, p, n=n: (lax.bitwise_xor(i, lax.div(p[0], 2)), 0, k + n, 0, 0),
+                lambda k, i, p: (lax.bitwise_xor(i, lax.div(p[0], 2)), 0, k, 0, 0),
             )
-            for n in (skip, 0)
         ]
-        + [
-            pl.BlockSpec((2, 2, 2, 128, 128), lambda k, i, p, n=n: (0, i, k + n, 0, 0))
-            for n in (skip, 0)
-        ]
+        * 2
+        + [pl.BlockSpec((2, 2, 2, 128, 128), lambda k, i, p: (0, i, k, 0, 0))] * 2
         + [pl.BlockSpec((1, 1, 256), lambda k, i, p: (k * 2 + i, 0, 0))],
         out_shape=[struct((2, 8, rows, 128), bf16)] * 4
         + pieces
@@ -196,12 +192,8 @@
             once((rows, width), whole),
             once((rows, width), whole),
         ],
-        out_specs=[
-            pl.BlockSpec((2, 1, 1, 128, 128), lambda z, p: (0, z, 4, 0, 0)),
-            pl.BlockSpec((2, 1, 1, 128, 128), lambda z, p: (0, z, 2, 0, 0)),
-        ]
-        * 2,
-        out_shape=[struct((2, 4, 5, 128, 128), f32), struct((2, 4, 3, 128, 128), f32)] * 2,
+        out_specs=[pl.BlockSpec((2, 1, 1, 128, 128), lambda z, p: (0, z, 2, 0, 0))] * 4,
+        out_shape=[struct((2, 4, 3, 128, 128), f32)] * 4,
         cost_estimate=cost("out_grad"),
         name="out_grad",
     )
@@ -265,21 +257,15 @@
         in_specs=[keep, one, two] * 2,
         out_specs=pl.BlockSpec((2, 2 * slots, 128, 128), lambda i: (i, 0, 0, 0)),
         out_shape=struct((4, 2 * slots, 128, 128), f32),
-        cost_estimate=cost("finish"),
+        cost_estimate=cost(f"finish{slots}"),
         name="finish",
     )
 
 
 def qkv_grad_kernel(pos, a1_own, a1_other, *refs):
-    own, other, (x_send, x_keep, y_send, y_keep) = refs[:3], refs[3:12], refs[12:]
+    own, other, (x_send, x_keep, y_send, y_keep) = refs[:3], refs[3:6], refs[6:]
     left = jnp.concatenate([r[0] for r in own], 1)
-    left_other = []
-    for j in range(3):
-        part = lax.div(lax.bitwise_xor(pl.program_id(0), pos[0]) * 3 + j, 4)
-        parts = [r[...] for r in other[3 * j : 3 * j + 3]]
-        chosen = jnp.where(part == 0, parts[0], jnp.where(part == 1, parts[1], parts[2]))
-        left_other.append(chosen.astype(bf16))
-    left_other = jnp.concatenate(left_other, 1)
+    left_other = jnp.concatenate([r[0].astype(bf16) for r in other], 1)
     tile = dot(left, a1_own[...], 0, 0) + dot(left_other, a1_other[...], 0, 0)
     step = pl.program_id(0)
     block = lambda j, n: tile[128 * j : 128 * j + 128, n * 128 : (n + 1) * 128]
@@ -300,28 +286,24 @@
     rows, width = a1[0].shape
     whole = lambda n, p: (0, 0)
 
-    def source(j):
+    def source(j, halves):
         def where(n, p):
             unit = lax.bitwise_xor(n, p[0]) * 3 + j
-            return (lax.div(unit, 4), 0, lax.rem(unit, 4) * 2 + p[1])
+            at = lax.rem(unit, 4)
+            return (lax.div(unit, 4), 0, at * 2 + p[1] if halves else at)
 
         return where
-
-    def other_place(j, part):
-        if part != j:
-            return lambda n, p: (0, [u % 4 for u in range(j, 12, 3) if u // 4 == part][0])
-        return lambda n, p: (0, lax.select(lax.bitwise_xor(n, p[0]) <= j, 0 * n, 0 * n + 3))
 
     out = lambda at: pl.BlockSpec((1, 4, 3, 128, 128), lambda n, p: (at(n), 0, 0, 0, 0))
     return ordered_call(
         qkv_grad_kernel,
-        [pos, *a1] + [grad_proj] * 3 + [part for _ in range(3) for part in other],
+        [pos, *a1] + [grad_proj] * 3 + [other] * 3,
         after,
         prefetch=1,
         grid=(4,),
         in_specs=[once((rows, width), whole)] * 2
-        + [pl.BlockSpec((1, rows, 128), source(j)) for j in range(3)]
-        + [pl.BlockSpec((rows, 128), other_place(j, part)) for j in range(3) for part in range(3)],
+        + [pl.BlockSpec((1, rows, 128), source(j, True)) for j in range(3)]
+        + [pl.BlockSpec((1, rows, 128), source(j, False)) for j in range(3)],
         out_specs=[
             out(lambda n: lax.div(n, 2)),
             out(lambda n: lax.div(n, 2)),
@@ -335,7 +317,7 @@
 
 
 LONG, SHORT = 10**11, 1
-WEIGHTS = {"first_norm": LONG, "hidden0": LONG, "blocks": LONG}
+WEIGHTS = {"first_norm": LONG, "hidden0": LONG, "blocks": LONG, "in_place": LONG, "ends": LONG, "finish2": LONG}
 
 
 def cost(name):
@@ -502,7 +484,7 @@
 
 
 def back_kernel(
-    pos, qf, kf, v, dn, dd, st, ds, fw, matrix, cos, sin1, sin2, gp_o, bias_o, fw_o, *sends
+    pos, qf, kf, v, dn, dd, st, ds, fw, matrix, cos, sin1, sin2, gp_o, send_o, bias_o, fw_o
 ):
     count = qf.shape[0] // LEN_BLK
     step = pl.program_id(1)
@@ -563,7 +545,7 @@
         gp_o[n] = grads[n]
         wide = grads[n].astype(f32)
         other_half = jnp.where(pos[1] == 0, wide[:, 128:], wide[:, :128])
-        sends[n][...] = other_half
+        send_o[n] = other_half
     totals = [column_sum(part.astype(f32)) for part in grads]
     totals.append(column_sum(dq + dk) / fw[...])
 
@@ -669,16 +651,16 @@
         + [s["table"]] * 4,
         out_specs=[
             pl.BlockSpec((3, LEN_BLK * per, HG), lambda h, g, *_: (0, g, h)),
+            pl.BlockSpec((3, LEN_BLK * per, 128), lambda h, g, *_: (0, g, h)),
             pl.BlockSpec((3, 1, HG), lambda h, g, *_: (0, 0, h)),
             s["row"],
-        ]
-        + [pl.BlockSpec((LEN_BLK * per, 128), lambda h, g, *_: (g, h))] * 3,
+        ],
         out_shape=[
             struct((3, rows, 1024), bf16),
+            struct((3, rows, 512), f32),
             struct((3, 1, 1024), f32),
             struct((1, 1024), f32),
-        ]
-        + [struct((rows, 512), f32)] * 3,
+        ],
         cost_estimate=cost("backward"),
         name="backward",
     )
@@ -722,11 +704,13 @@
     return wide, keep
 
 
-def norms_kernel(x, g, gain1, bias1, gain2, bias2, a1_o, a2_o, g_o):
+def norms_kernel(x, g, gain1, bias1, gain2, bias2, a1_o, a2_o, g_o, *x_o):
     xhat, _ = norm_parts(x[...].astype(f32))
     a1_o[...] = (xhat * gain1[...] + bias1[...]).astype(bf16)
     a2_o[...] = (xhat * gain2[...] + bias2[...]).astype(bf16)
     g_o[...] = g[...].astype(g_o.dtype)
+    for out in x_o:
+        out[...] = x[...].astype(f32)
 
 
 def norms(x, g, *vectors, after=(), g_type=f32):
@@ -738,15 +722,17 @@
         after,
         grid=(rows // tile,),
         in_specs=[wide(1024)] * 2 + keep,
-        out_specs=[wide(1024)] * 3,
-        out_shape=[struct((rows, 1024), bf16)] * 2 + [struct((rows, 1024), g_type)],
+        out_specs=[wide(1024)] * (4 if g_type == f32 else 3),
+        out_shape=[struct((rows, 1024), bf16)] * 2
+        + [struct((rows, 1024), g_type)] * (2 if g_type == f32 else 1),
         cost_estimate=cost("norms"),
         name="norms",
     )
 
 
 def hidden_rows_kernel(grad, filled, pos, *refs):
-    acts, weights, (send, keep) = refs[:2], refs[2:6], refs[6 + filled :]
+    acts, weights, outs = refs[:2], refs[2:6], refs[6 + filled :]
+    send, keep = outs[-2:] if not grad else outs[2:4]
     total = None
     for b in range(4):
         act = acts[b % 2]
@@ -764,8 +750,15 @@
     def _():
         keep[...] = total
 
-
-def hidden_rows(pos, acts, weight, grad, sends=None, after=()):
+    if grad:
+        x_own, x_other, sum_o = outs[0], outs[1], outs[4]
+        xhat, _ = norm_parts(jnp.where(step < steps, x_other[...], x_own[...].astype(f32)))
+        sums = [column_sum(total * xhat), column_sum(total)]
+        add_sums(sum_o, sums + [jnp.zeros((6, 1024), f32)])
+
+
+def hidden_rows(pos, acts, weight, rows_in=None, sends=None, after=()):
+    grad = rows_in is not None
     rows, tile = acts[0].shape[2], ROW_TILE
     steps = rows // tile
     act = pl.BlockSpec(
@@ -776,45 +769,28 @@
     else:
         part = lambda b: once((512, 1024), lambda i, p: (2 * b + p[1], 0))
     filled = [] if sends is None else [sends]
+    ours = pl.BlockSpec((tile, 1024), lambda i, p: (lax.max(i - steps, 0), 0))
+    theirs = pl.BlockSpec((tile, 1024), lambda i, p: (lax.min(i, steps - 1), 0))
     return ordered_call(
         functools.partial(hidden_rows_kernel, grad, len(filled)),
-        [pos, *acts] + [weight] * 4 + filled,
+        [pos, *acts] + [weight] * 4 + filled + list(rows_in or ()),
         after,
         prefetch=1,
         grid=(2 * steps,),
         in_specs=[act] * 2
         + [part(b) for b in range(4)]
-        + [pl.BlockSpec(memory_space=pl.ANY)] * len(filled),
+        + [pl.BlockSpec(memory_space=pl.ANY)] * len(filled)
+        + [ours, theirs][: 2 * grad],
         out_specs=[
             pl.BlockSpec((1, tile, 1024), lambda i, p: (int(grad), lax.min(i, steps - 1), 0)),
-            pl.BlockSpec((tile, 1024), lambda i, p: (lax.max(i - steps, 0), 0)),
-        ],
-        out_shape=[struct((2, rows, 1024), f32), struct((rows, 1024), f32)],
+            ours,
+        ]
+        + [pl.BlockSpec((8, 1024), lambda i, p: (0, 0))] * grad,
+        out_shape=[struct((2, rows, 1024), f32), struct((rows, 1024), f32)]
+        + [struct((8, 1024), f32)] * grad,
         input_output_aliases={7: 0} if filled else {},
         cost_estimate=cost(f"hidden{grad:d}"),
         name="hidden_rows",
-    )
-
-
-def result_kernel(x, mixed, own, other, w_out, bias, res_o):
-    out = dot(mixed[...], w_out[...], 1, 0) + (own[...] + other[0])
-    res_o[...] = (x[...].astype(f32) + out + bias[...]).astype(bf16)
-
-
-def result_rows(x, mixed, own, other, w_out, bias, after=()):
-    rows, tile = x.shape[0], ROW_TILE
-    fixed = (w_out, bias)
-    wide, keep = tiles(tile, fixed)
-    return ordered_call(
-        result_kernel,
-        [x, mixed, own, other, *fixed],
-        after,
-        grid=(rows // tile,),
-        in_specs=[wide(1024)] * 3 + [pl.BlockSpec((1, tile, 1024), lambda i: (0, i, 0))] + keep,
-        out_specs=wide(1024),
-        out_shape=struct((rows, 1024), bf16),
-        cost_estimate=cost("result_rows"),
-        name="result_rows",
     )
 
 
@@ -844,27 +820,29 @@
     )
 
 
-def second_norm_kernel(x, part, own, other, gain, out_o, sum_o):
-    xhat, r = norm_parts(x[...].astype(f32))
-    grad = own[...] + other[0]
-    out_o[...] = part[...] + norm_back(grad, xhat, r, gain[...])
-    sums = [column_sum(v) for v in (grad * xhat, grad)]
-    add_sums(sum_o, sums + [jnp.zeros((6, 1024), f32)])
-
-
-def second_norm(x, part, own, other, gain, after=()):
+def ends_kernel(x, mixed, part, own_r, other_r, own_g, other_g, w_out, bias, gain, res_o, out_o):
+    value = x[...].astype(f32)
+    out = dot(mixed[...], w_out[...], 1, 0) + (own_r[...] + other_r[0])
+    res_o[...] = (value + out + bias[...]).astype(bf16)
+    xhat, r = norm_parts(value)
+    out_o[...] = part[...] + norm_back(own_g[...] + other_g[0], xhat, r, gain[...])
+
+
+def ends(x, mixed, part, own_r, own_g, others, w_out, bias, gain, after=()):
     rows, tile = x.shape[0], ROW_TILE
-    wide, keep = tiles(tile, (gain,))
+    fixed = (w_out, bias, gain)
+    wide, keep = tiles(tile, fixed)
+    half = lambda n: pl.BlockSpec((1, tile, 1024), lambda i: (n, i, 0))
     return ordered_call(
-        second_norm_kernel,
-        [x, part, own, other, gain],
+        ends_kernel,
+        [x, mixed, part, own_r, others, own_g, others, *fixed],
         after,
         grid=(rows // tile,),
-        in_specs=[wide(1024)] * 3 + [pl.BlockSpec((1, tile, 1024), lambda i: (1, i, 0))] + keep,
-        out_specs=[wide(1024), pl.BlockSpec((8, 1024), lambda i: (0, 0))],
-        out_shape=[struct((rows, 1024), f32), struct((8, 1024), f32)],
-        cost_estimate=cost("second_norm"),
-        name="second_norm",
+        in_specs=[wide(1024)] * 4 + [half(0), wide(1024), half(1)] + keep,
+        out_specs=[wide(1024)] * 2,
+        out_shape=[struct((rows, 1024), bf16), struct((rows, 1024), f32)],
+        cost_estimate=cost("ends"),
+        name="ends",
     )
 
 
@@ -1037,15 +1015,6 @@
         return self.pick(self.high) + self.two
 
 
-def plane_sum(links, rows):
-    split_rows = rows.reshape((4, 2) + rows.shape[1:])
-    core = lax.rem(lax.axis_index("seq"), 2)
-    pick = lambda i: lax.dynamic_index_in_dim(split_rows, i, 1, keepdims=False)
-    total = pick(core) + links.core(pick(1 - core))
-    total = total + links.x(total)
-    return total + links.y(total)
-
-
 def dct_table(order):
     degree = np.arange(order, dtype=np.float64)[:, None]
     sample = np.arange(order, dtype=np.float64)[None, :]
@@ -1076,6 +1045,31 @@
     full = lax.dot_general(*args, dims, precision=lax.Precision.HIGHEST)
     block = np.arange(HG) // HEAD_DIM
     return jnp.where(block[:, None] == block[None, :], full, 0.0)
+
+
+def in_place_kernel(count, start, blocks, down_o, up_o):
+    for k in range(count):
+        lines = slice(128 * k, 128 * k + 128)
+        for half in range(2):
+            down_o[lines, 128 * half : 128 * half + 128] = blocks[start + 2 * k + half]
+            up_o[half, k] = blocks[2 * k + half]
+
+
+def in_place(blocks, count, after, start=None):
+    return ordered_call(
+        functools.partial(in_place_kernel, count, start or 2 * count),
+        [blocks],
+        after,
+        grid=(1,),
+        in_specs=[pl.BlockSpec(blocks.shape, lambda i: (0, 0, 0))],
+        out_specs=[
+            pl.BlockSpec((128 * count, 256), lambda i: (0, 0)),
+            pl.BlockSpec((2, count, 128, 128), lambda i: (0, 0, 0, 0)),
+        ],
+        out_shape=[struct((128 * count, 256), f32), struct((2, count, 128, 128), f32)],
+        cost_estimate=cost("in_place"),
+        name="in_place",
+    )
 
 
 def blocks_kernel(left, right, out):
@@ -1143,9 +1137,8 @@
     g = cotangent.reshape(rows, width)
     row = lambda v: v.reshape(1, -1)
     gains = row(ln1_gain), row(ln1_bias), row(ln2_gain), row(ln2_bias)
-    x_other = links.core(x.astype(f32))
-    a1, a2, g_wide = norms(x, g, *gains)
-    g_other = links.core(g_wide)
+    a1, a2, g_wide, x_wide = norms(x, g, *gains)
+    x_other, g_other = links.core(x_wide), links.core(g_wide)
 
     forth = head_blocks(directions, True)
     turns = rotation_tables(places.astype(f32))
@@ -1153,8 +1146,9 @@
 
     qf, kf, v, state = features(a1, w_qkv, row(b_qkv), weights, forth, turns, valid)
     forward = Carried(links, state, False)
+    x_other = hold(x_other, [state])
     a1_o, a2_o, g_o = norms(
-        hold(x_other, [state]), hold(g_other, [state]), *gains, g_type=bf16, after=[state]
+        x_other, hold(g_other, [state]), *gains, g_type=bf16, after=[state]
     )
     ffn = functools.partial(
         ffn_chunk,
@@ -1185,16 +1179,15 @@
         pos, mixed, [hold(part, [back]) for part in mixed_other], (g, g_o), after=held
     )
     c2 = ffn(3, 1, earlier=c1[:4], filled=out_pieces, after=[reverse.far(out_pieces[0])])
-    first = list(c2[4:8])
+    held = [c2[8]]
     z0 = None
     if tuned:
         g1.arrived(c2[8])
         g0.second_with(g1)
-        first[0::2] = g1.second_in(*first[0::2], 0)
-        z0 = g0.done()
-    g2 = Group(links, *first, at=2)
-    state_later = reverse.done(c2[8])
-    grad_proj, bias_qkv, grad_feat, *grad_send = backward(
+        held = [g1.second()]
+    state_later = reverse.done(held[0])
+    g2 = Group(links, *c2[4:8])
+    grad_proj, grad_send, bias_qkv, grad_feat = backward(
         pos,
         qf,
         kf,
@@ -1206,82 +1199,94 @@
         weights,
         back,
         turns,
-        after=[first[0], z0],
-    )
-    grad_other = [links.core(part) for part in grad_send]
+        after=held,
+    )
+    grad_other = links.core(grad_send)
+    if tuned:
+        z0 = g0.done(grad_proj)
+        early = reduce_z(z0)
     last_parts = qkv_grad(
-        pos, (a1, a1_o), grad_proj, [hold(part, [grad_proj]) for part in grad_other]
-    )
-    g3 = Group(links, *last_parts)
+        pos, (a1, a1_o), grad_proj, hold(grad_other, [grad_proj, z0]), after=[z0]
+    )
     acts = c2[:4]
     held = [last_parts[0]]
+    pieces = list(last_parts)
     if tuned:
         g2.arrived(last_parts[0])
-        g1.second_with(g2)
-        z1 = g1.done()
-        early = reduce_z(z0), reduce_z(z1)
-        held = [z1, g2.second()]
-    own_g = hidden_rows(pos, acts[2:], w_up, True, after=held)
-    own_r = hidden_rows(pos, acts[:2], w_down, False, own_g[0], after=[own_g[1]])
+        held = [g2.second()]
+        z1 = g1.done(*held)
+        later = Halves(links, z1)
+        pieces[0::2] = [hold(piece, [z1]) for piece in pieces[0::2]]
+        held = [z1]
+    g3 = Group(links, *pieces)
+    own_g = hidden_rows(pos, acts[2:], w_up, (x, x_other), after=held)
+    held = [own_g[1]]
+    if tuned:
+        z2 = g2.done(own_g[1])
+        middle = Halves(links, z2)
+        held += [z2, early]
+    own_r = hidden_rows(pos, acts[:2], w_down, sends=own_g[0], after=held)
     others = links.core(own_r[0])
     held = [own_r[1]]
     if tuned:
+        held = [later.stage_two(own_r[1]), middle.stage_two(own_r[1])]
         g3.arrived(own_r[1])
-        held = [g3.second()]
+        held.append(g3.second())
     partial, sums1 = first_norm(x, g, grad_proj, w_qkv, row(ln1_gain), after=held)
-    held = [partial]
-    if tuned:
-        z2 = g2.done(partial)
-        middle = Halves(links, z2)
-        z3 = g3.done(partial)
-        tail = Line(links, z3)
-        held = [z2, z3]
-    grad_input, sums2 = second_norm(
-        x, partial, own_g[1], hold(others, [partial]), row(ln2_gain), after=held
-    )
-    if tuned:
-        middle.stage_two(grad_input)
-    result = result_rows(
-        x,
-        mixed,
-        own_r[1],
-        hold(others, [partial]),
-        w_out,
-        row(b_out + b_down),
-        after=[grad_input],
-    )
-
     half_up = jnp.concatenate([c[8].reshape(-1, 2, 2, 128) for c in (c0, c1, c2)], 0)
     half_up = half_up.transpose(1, 2, 0, 3).reshape(4, 1, 512)
     b_up_grad = jnp.where(core == np.arange(2)[None, :, None], half_up, 0.0).reshape(-1)
     vectors = [
         sums1[0],
         sums1[1],
-        sums2[0],
-        sums2[1],
+        own_g[2][0],
+        own_g[2][1],
         bias_qkv.reshape(-1),
         sums1[2],
         b_up_grad,
         grad_feat[0],
     ]
+    lines = jnp.concatenate([v_.reshape(links.ns, -1) for v_ in vectors], 1)
+    held = [partial]
     if tuned:
-        lines = jnp.concatenate([v_.reshape(8, -1, 128) for v_ in vectors], 1)
-        lines = plane_sum(links, jnp.pad(lines, ((0, 0), (0, 3), (0, 0))))
-        lines = Line(links, lines).done()
+        lines = jnp.pad(lines.reshape(8, 13, 128), ((0, 0), (0, 3), (0, 0)))
+        lines = reduce_z(lines.reshape(4, 32, 128))
+        z3 = g3.done(partial)
+        later = later.done(z3)
+        tail = Line(links, z3)
+        held = [z3]
+    result, grad_input = ends(
+        x,
+        mixed,
+        partial,
+        own_r[1],
+        own_g[1],
+        hold(others, [partial]),
+        w_out,
+        row(b_out + b_down),
+        row(ln2_gain),
+        after=held,
+    )
+
+    if tuned:
+        lines = hold(lines, [result]).reshape(2, 16, 128)
+        pick = lambda i: lax.dynamic_index_in_dim(lines, i, 0, keepdims=False)
+        lines, lines_other = pick(core), links.core(pick(1 - core))
+        first_down, first_up = in_place(early, 1, [lines])
+        lines = lines + hold(lines_other, [first_down])
+        second_down, second_up = in_place(later, 2, [lines])
+        lines = lines + hold(links.x(lines), [second_down])
+        middle = middle.done(second_down)
+        third_down, third_up = in_place(middle, 1, [lines], start=3)
+        lines = lines + hold(links.y(lines), [third_down])
+        tail = tail.done(third_down).reshape(6, 128, 128)
         shares, at = [], 0
         for v_ in vectors:
             n = v_.shape[0] // 1024
             shares.append(lines[at : at + n].reshape(-1))
             at += n
-        tail = tail.done(lines)
-        middle = middle.done(lines)
-        sizes = (1, 2, 1)
-        parts = [*early, middle]
-        units = [v_[: 2 * n].reshape(n, 2, 128, 128) for v_, n in zip(parts, sizes)]
-        halves = jnp.concatenate(units, 0).swapaxes(0, 1)
-        start = (2, 4, 3)
-        units = [v_[m : m + 2 * n].reshape(n, 2, 128, 128) for v_, n, m in zip(parts, sizes, start)]
-        w_down_grad = jnp.concatenate(units, 0).transpose(0, 2, 1, 3).reshape(512, 256)
+        halves = jnp.concatenate([first_up, second_up, third_up], 1)
+        w_down_grad = jnp.concatenate([first_down, second_down, third_down], 0)
         w_out_grad = jnp.concatenate([middle[2], middle[5]], 1)
         blocks = [[tail[i] for i in (0, 3, 2)], [tail[i] for i in (1, 4, 5)]]
         blocks = jnp.stack([jnp.stack(b, 0) for b in blocks], 0)
@@ -1312,15 +1317,15 @@
         both = lambda send, keep: jnp.stack([keep, send], 0)
         groups = (c0, c1, c2)
         slots = lambda pair, n, m, k: both(pair[0][:, :, m : m + n], pair[1][:, :, k : k + n])
-        sizes = ((2, 0, 0), (4, 0, 0), (2, 2, 0))
+        sizes = ((2, 0, 0), (4, 0, 0), (2, 0, 0))
         up = [slots(c[4:6], *size) for c, size in zip(groups, sizes)]
         up = jnp.concatenate(up, 3).reshape(2, 2, 4, 4, 2, 128, 128)
         up = of_core(up.transpose(2, 4, 6, 1, 0, 3, 5).reshape(1024, 4, 512), 2)
         down = [slots(c[6:8], *size) for c, size in zip(groups, sizes)]
         down = jnp.concatenate(down, 3).reshape(2, 2, 4, 4, 2, 128, 128)
         down = of_core(down.transpose(2, 3, 5, 0, 1, 4, 6).reshape(4, 512, 1024), 1)
-        by_x = slots(out_pieces[:2], 1, 4, 2).swapaxes(0, 1)
-        out = jnp.concatenate([by_x, slots(out_pieces[2:], 1, 4, 2)], 3)
+        by_x = slots(out_pieces[:2], 1, 2, 2).swapaxes(0, 1)
+        out = jnp.concatenate([by_x, slots(out_pieces[2:], 1, 2, 2)], 3)
         out = out.transpose(2, 4, 0, 1, 3, 5).reshape(4, 128, 1024)
         by_x = both(*last_parts[:2]).swapaxes(0, 1)
         by_y = both(*last_parts[2:])

time: 431 us -> 396 us (0.919)
  the two profiles are of different devices: /device:TPU:1 before, /device:TPU:16 now
where the time goes in v3:
time: 396 us; the launch traced here: 389 us
  Pallas kernels  257 us (65%)
  starting transfers between devices  33.6 us (8%)
  waiting for transfers between devices  31.1 us (8%)
  local copies, waits for them, and re-layouts  26.3 us (7%)
  other arithmetic  24.9 us (6%)
  between operations  15 us (4%)
    pallas_call x26, Pallas kernels, ordered_call(): pl.pallas_call(body, grid_spec=pltpu.PrefetchScalarGridSpec(num_scalar_pr...  257 us
    ppermute x39, starting transfers between devices, send(): return lax.ppermute(value, ('batch', 'seq'), pairs)  33.5 us
    ppermute x39, waiting for transfers between devices, send(): return lax.ppermute(value, ('batch', 'seq'), pairs)  31.1 us
    unnamed x103, local copies, waits for them, and re-layouts  9.56 us
  transfers between devices with their start and end apart: 41, of which 10 were waited for; matrix products, arithmetic and copies ran while one was open for 10% of the time, Pallas kernels for 64%

profile of v3, /device:TPU:16, one launch (start us, length us, event | category | flops | bytes accessed | tf_op | source)
XLA Modules:
  0.0 389.1 jit_solution(5008862466695890510)
XLA Ops:
  7.3 7.5 %norms.2 = (bf16[1024,1024]{1,0:T(8,128)(2,1)}, bf16[1024,1024]{1,0:T(8,128)(2,1)}, f32[1024,1024]{1,0:T(8,128)}, f32[1024,1024]{1,0:T(8,128)}) custom-call(bf16[1024,1024]{1,0:T(8,128)(2,1)} %bitcast.137, bf16[1024,1024]{1,0:T(8,128)(2,1)} %bitcast.127, f32[1,1024]{1,0:T(1,128)} %bitcast.175, f32[1,1024]{1,0:T(1,128)} %bitcast.171, f32[1,1024]{1,0:T(1,128)} %bitcast.178, ...), custom_call_target="tpu_custom_call" | custom-call | flops 1 | bytes 1 | tf_op jit(solution)/shard_map/norms/pallas_call | solution.py:53
  19.5 17.1 %features.1 = (bf16[1024,1024]{1,0:T(8,128)(2,1)}, bf16[1024,1024]{1,0:T(8,128)(2,1)}, bf16[1024,1024]{1,0:T(8,128)(2,1)}, f32[4,4,136,128]{3,2,1,0:T(8,128)}) custom-call(bf16[1024,1024]{1,0:T(8,128)(2,1)} %get-tuple-element.135.refs_0_.refs_1_, bf16[1024,3072]{1,0:T(8,128)(2,1)} %refs_3_.7, bf16[1024,3072]{1,0:T(8,128)(2,1)} %refs_3_.7, ...), custom_call_target="tpu_custom_call" | custom-call | flops 1 | bytes 1 | tf_op jit(solution)/shard_map/features/pallas_call | solution.py:53
  37.8 7.1 %norms.3 = (bf16[1024,1024]{1,0:T(8,128)(2,1)}, bf16[1024,1024]{1,0:T(8,128)(2,1)}, bf16[1024,1024]{1,0:T(8,128)(2,1)}) custom-call(f32[1024,1024]{1,0:T(8,128)} %collective-permute-done.1.refs_0_.refs_8_, f32[1024,1024]{1,0:T(8,128)} %collective-permute-done.2.refs_1_, f32[1,1024]{1,0:T(1,128)} %bitcast.176, f32[1,1024]{1,0:T(1,128)} %bitcast.172, ...), custom_call_target="tpu_custom_call" | custom-call | flops 1 | bytes 1 | tf_op jit(solution)/shard_map/norms/pallas_call | solution.py:53
  47.2 16.9 %ffn_chunk.3 = (bf16[2,8,1024,128]{3,2,1,0:T(8,128)(2,1)}, bf16[2,8,1024,128]{3,2,1,0:T(8,128)(2,1)}, bf16[2,8,1024,128]{3,2,1,0:T(8,128)(2,1)}, bf16[2,8,1024,1...) custom-call(s32[2]{0:T(128)} %pad_add_fusion.refs_0_, ...), custom_call_target="tpu_custom_call" | custom-call | flops 1 | bytes 1 | tf_op jit(solution)/shard_map/ffn_chunk/pallas_call | solution.py:53
  68.7 27.1 %ffn_chunk.4 = (bf16[2,8,1024,128]{3,2,1,0:T(8,128)(2,1)}, bf16[2,8,1024,128]{3,2,1,0:T(8,128)(2,1)}, bf16[2,8,1024,128]{3,2,1,0:T(8,128)(2,1)}, bf16[2,8,1024,1...) custom-call(s32[2]{0:T(128)} %pad_add_fusion.refs_0_, ...), custom_call_target="tpu_custom_call", output_to_operand_aliasing={{0}: (11, {}), {1}: (12, {}), {2}: (13, {}), {3}: (14, {})} | custom-call | flops 1 | bytes 1 | tf_op jit(solution)/shard_map/ffn_chunk/pallas_call | solution.py:53
  103.8 17.6 %mixing.1 = (bf16[1024,1024]{1,0:T(8,128)(2,1)}, bf16[1024,1024]{1,0:T(8,128)(2,1)}, f32[4,1024,128]{2,1,0:T(8,128)}, f32[4,4,136,128]{3,2,1,0:T(8,128)}, f32[1024,256]{1,0:T(8,128)}, /*index=5*/f32[1024,256]{1,0:T(8,128)}) custom-call(s32[2]{0:T(128)} %pad_add_fusion.refs_0_, bf16[1024,1024]{1,0:T(8,128)(2,1)} %bitcast.130, bf16[1024,1024]{1,0:T(8,128)(2,1)} %refs_7_.7, ...), custom_call_target="tpu_custom_call" | custom-call | flops 1 | bytes 1 | tf_op jit(solution)/shard_map/mixing/pallas_call | solution.py:53
  129.2 8.0 %out_grad.1 = (f32[2,4,3,128,128]{4,3,2,1,0:T(8,128)}, f32[2,4,3,128,128]{4,3,2,1,0:T(8,128)}, f32[2,4,3,128,128]{4,3,2,1,0:T(8,128)}, f32[2,4,3,128,128]{4,3,2,1,0:T(8,128)}) custom-call(s32[2]{0:T(128)} %pad_add_fusion.refs_0_, bf16[1024,1024]{1,0:T(8,128)(2,1)} %get-tuple-element.166.refs_2_.refs_1_, f32[1024,256]{1,0:T(8,128)} %collective-permute-done.10.refs_2_, ...), custom_call_target="tpu_custom_call" | custom-call | flops 1 | bytes 1 | tf_op jit(solution)/shard_map/out_grad/pallas_call | solution.py:53
  137.2 6.0 %collective-permute-done.9 = f32[2,4,136,128]{3,2,1,0:T(8,128)} collective-permute-done((f32[2,4,136,128]{3,2,1,0:T(8,128)S(1)}, f32[2,4,136,128]{3,2,1,0:T(8,128)}, u32[]{:S(2)}, u32[]{:S(2)}) %collective-permute-start.9) | collective-permute-done | bytes 557088 | tf_op jit(solution)/shard_map/ppermute | solution.py:861
  146.1 16.8 %ffn_chunk.5 = (bf16[2,8,1024,128]{3,2,1,0:T(8,128)(2,1)}, bf16[2,8,1024,128]{3,2,1,0:T(8,128)(2,1)}, bf16[2,8,1024,128]{3,2,1,0:T(8,128)(2,1)}, bf16[2,8,1024,1...) custom-call(s32[2]{0:T(128)} %pad_add_fusion.refs_0_, ...), custom_call_target="tpu_custom_call", output_to_operand_aliasing={{0}: (11, {}), {1}: (12, {}), {2}: (13, {}), {3}: (14, {}),... | custom-call | flops 1 | bytes 1 | tf_op jit(solution)/shard_map/ffn_chunk/pallas_call | solution.py:53
  164.4 3.4 second_stage.5
  175.1 27.5 %backward.1 = (bf16[3,1024,1024]{2,1,0:T(8,128)(2,1)}, f32[3,1024,512]{2,1,0:T(8,128)}, f32[3,1,1024]{2,1,0:T(1,128)}, f32[1,1024]{1,0:T(1,128)}) custom-call(s32[2]{0:T(128)} %pad_add_fusion.refs_0_, bf16[1024,1024]{1,0:T(8,128)(2,1)} %get-tuple-element.136.refs_3_.refs_1_, bf16[1024,1024]{1,0:T(8,128)(2,1)} %get-tuple-element.137.refs_4_.refs_2_, ...), custom_call_target="tpu_custom_call" | custom-call | flops 1 | bytes 1 | tf_op jit(solution)/shard_map/backward/pallas_call | solution.py:53
  202.7 4.1 %finish.4.refs_9_ = f32[4,4,128,128]{3,2,1,0:T(8,128)} custom-call(f32[2,4,2,128,128]{4,3,2,1,0:T(8,128)} %get-tuple-element.157.refs_0_, f32[2,4,2,128,128]{4,3,2,1,0:T(8,128)} %collective-permute-done.6.refs_1_, f32[2,4,5,128,128]{4,3,2,1,0:T(8,128)} %copy-done.1, f32[2,4,2,128,128]{4,3,2,1,0:T(8,128)} %get-tuple-element.160.refs_2_.refs_3_, ...), custom_call_target="tpu_custom_call" | custom-call | flops 99999997952 | bytes 1 | tf_op jit(solution)/shard_map/finish/pallas_call | solution.py:53
  208.9 4.2 %collective-permute-done.18.refs_6_.refs_7_.refs_8_ = f32[3,1024,512]{2,1,0:T(8,128)} collective-permute-done((f32[3,1024,512]{2,1,0:T(8,128)}, f32[3,1024,512]{2,1,0:T(8,128)}, u32[]{:S(2)}, u32[]{:S(2)}) %collective-permute-start.18) | collective-permute-done | bytes 6291488 | tf_op jit(solution)/shard_map/ppermute | solution.py:861
  213.2 14.0 %qkv_grad.1 = (f32[2,4,3,128,128]{4,3,2,1,0:T(8,128)}, f32[2,4,3,128,128]{4,3,2,1,0:T(8,128)}, f32[2,4,3,128,128]{4,3,2,1,0:T(8,128)}, f32[2,4,3,128,128]{4,3,2,1,0:T(8,128)}) custom-call(s32[2]{0:T(128)} %pad_add_fusion.refs_0_, bf16[1024,1024]{1,0:T(8,128)(2,1)} %get-tuple-element.135.refs_0_.refs_1_, bf16[1024,1024]{1,0:T(8,128)(2,1)} %get-tuple-element.144.refs_2_, ...), custom_call_target="tpu_custom_call" | custom-call | flops 1 | bytes 1 | tf_op jit(solution)/shard_map/qkv_grad/pallas_call | solution.py:53
  236.2 4.1 %finish.5.refs_9_ = f32[4,8,128,128]{3,2,1,0:T(8,128)} custom-call(f32[2,4,4,128,128]{4,3,2,1,0:T(8,128)} %get-tuple-element.177.refs_0_, f32[2,4,5,128,128]{4,3,2,1,0:T(8,128)} %collective-permute-done.13.refs_1_.refs_5_, f32[4,4,128,128]{3,2,1,0:T(8,128)} %collective-permute-done.16.refs_2_, f32[2,4,4,128,128]{4,3,2,1,0:T(8,128)} %get-tuple-element.187.refs_2_.refs_3_, ...), custom_call_target="tpu_custom_call" | custom-call | flops 1 | bytes 1 | tf_op jit(solution)/shard_map/finish/pallas_call | solution.py:53
  243.8 3.1 collective-permute-start.21
  246.9 19.7 %hidden_rows.2 = (f32[2,1024,1024]{2,1,0:T(8,128)}, f32[1024,1024]{1,0:T(8,128)}, f32[8,1024]{1,0:T(8,128)}) custom-call(s32[2]{0:T(128)} %pad_add_fusion.refs_0_, bf16[2,8,1024,128]{3,2,1,0:T(8,128)(2,1)} %get-tuple-element.210.refs_1_, bf16[2,8,1024,128]{3,2,1,0:T(8,128)(2,1)} %get-tuple-element.211.refs_2_, bf16[1024,4096]{1,0:T(8,128)(2,1)} %refs_6_.8, ...), custom_call_target="tpu_custom_call" | custom-call | flops 1 | bytes 1 | tf_op jit(solution)/shard_map/hidden_rows/pallas_call | solution.py:53
  269.8 3.3 finish.6.refs_9_
  275.3 16.1 %hidden_rows.3 = (f32[2,1024,1024]{2,1,0:T(8,128)}, f32[1024,1024]{1,0:T(8,128)}) custom-call(s32[2]{0:T(128)} %pad_add_fusion.refs_0_, bf16[2,8,1024,128]{3,2,1,0:T(8,128)(2,1)} %get-tuple-element.208.refs_1_, bf16[2,8,1024,128]{3,2,1,0:T(8,128)(2,1)} %get-tuple-element.209.refs_2_, bf16[4096,1024]{1,0:T(8,128)(2,1)} %refs_6_.9, ...), custom_call_target="tpu_custom_call", output_to_operand_aliasing={{0}: (7, {})} | custom-call | flops 99999997952 | bytes 1 | tf_op jit(solution)/shard_map/hidden_rows/pallas_call | solution.py:53
  302.3 14.3 %first_norm.1 = (f32[1024,1024]{1,0:T(8,128)}, f32[8,1024]{1,0:T(8,128)}) custom-call(bf16[1024,1024]{1,0:T(8,128)(2,1)} %bitcast.139, bf16[1024,1024]{1,0:T(8,128)(2,1)} %bitcast.133, bf16[3,1024,1024]{2,1,0:T(8,128)(2,1)} %get-tuple-element.192.refs_3_.refs_4_.refs_5_.refs_2_, bf16[1024,3072]{1,0:T(8,128)(2,1)} %refs_3_.7, f32[1,1024]{1,0:T(1,128)} %bitcast.177, ...), custom_call_target="tpu_custom_call" | custom-call | flops 99999997952 | bytes 1 | tf_op jit(solution)/shard_map/first_norm/pallas_call | solution.py:53
  320.5 3.3 finish.7.refs_10_
  328.5 3.5 collective-permute-start.35
  336.1 13.7 %ends.1 = (bf16[1024,1024]{1,0:T(8,128)(2,1)}, f32[1024,1024]{1,0:T(8,128)}) custom-call(bf16[1024,1024]{1,0:T(8,128)(2,1)} %bitcast.140, bf16[1024,1024]{1,0:T(8,128)(2,1)} %get-tuple-element.166.refs_2_.refs_1_, f32[1024,1024]{1,0:T(8,128)} %get-tuple-element.228.refs_2_, f32[1024,1024]{1,0:T(8,128)} %get-tuple-element.217.refs_3_, ...), custom_call_target="tpu_custom_call" | custom-call | flops 99999997952 | bytes 1 | tf_op jit(solution)/shard_map/ends/pallas_call | solution.py:53
  360.9 9.9 %collective-permute-done.36 = f32[6,128,128]{2,1,0:T(8,128)} collective-permute-done((f32[6,128,128]{2,1,0:T(8,128)}, f32[6,128,128]{2,1,0:T(8,128)}, u32[]{:S(2)}, u32[]{:S(2)}) %collective-permute-start.36) | collective-permute-done | bytes 393248 | tf_op jit(solution)/shard_map/ppermute | solution.py:861
  (253 shorter events, 105.7 us)
Async XLA Ops:
  7.2 268.1 %reduce-scatter.3.cloned.1.call-start = ((), (), s32[]{:S(2)}) async-start(), calls=%async_computation.2 | async-start | bytes 1310720 | tf_op jit(solution)/shard_map/reduce_scatter | solution.py:920
  14.8 23.0 %collective-permute-start.1 = (f32[1024,1024]{1,0:T(8,128)}, f32[1024,1024]{1,0:T(8,128)}, u32[]{:S(2)}, u32[]{:S(2)}) collective-permute-start(f32[1024,1024]{1,0:T(8,128)} %get-tuple-element.140), channel_id=1, source_target_pairs={{0,1},{1,0},{2,3},{3,2},{4,5},{5,4},{6,7},{7,6},{8,9},{9,8},{10,11... | collective-permute-start | bytes 12582920 | tf_op jit(solution)/shard_map/ppermute | solution.py:861
  65.3 30.5 %collective-permute-start.4 = (f32[2,4,136,128]{3,2,1,0:T(8,128)S(1)}, f32[2,4,136,128]{3,2,1,0:T(8,128)}, u32[]{:S(2)}, u32[]{:S(2)}) collective-permute-start(f32[2,4,136,128]{3,2,1,0:T(8,128)S(1)} %select_add_fusion.7.refs_15_), channel_id=1, source_target_pairs={{0,4},{1,5},{2,6},{3,7},{4,0},{5,1},{6,2},{7,3},{8,12},{9,13},{10,... | collective-permute-start | bytes 1671176 | tf_op jit(solution)/shard_map/ppermute | solution.py:861
  65.7 32.4 %collective-permute-start.7 = (f32[2,4,2,128,128]{4,3,2,1,0:T(8,128)}, f32[2,4,2,128,128]{4,3,2,1,0:T(8,128)}, u32[]{:S(2)}, u32[]{:S(2)}) collective-permute-start(f32[2,4,2,128,128]{4,3,2,1,0:T(8,128)} %get-tuple-element.161), channel_id=1, source_target_pairs={{0,16},{1,17},{2,18},{3,19},{4,20},{5,21},{6,22},{7,23},{8,24},{9,... | collective-permute-start | bytes 3145736 | tf_op jit(solution)/shard_map/ppermute | solution.py:861
  67.2 30.9 %collective-permute-start.6 = (f32[2,4,2,128,128]{4,3,2,1,0:T(8,128)}, f32[2,4,2,128,128]{4,3,2,1,0:T(8,128)}, u32[]{:S(2)}, u32[]{:S(2)}) collective-permute-start(f32[2,4,2,128,128]{4,3,2,1,0:T(8,128)} %get-tuple-element.158), channel_id=1, source_target_pairs={{0,8},{1,9},{2,10},{3,11},{4,12},{5,13},{6,14},{7,15},{8,0},{9,1},... | collective-permute-start | bytes 3145736 | tf_op jit(solution)/shard_map/ppermute | solution.py:861
  100.5 62.4 %collective-permute-start.14 = (f32[2,4,5,128,128]{4,3,2,1,0:T(8,128)}, f32[2,4,5,128,128]{4,3,2,1,0:T(8,128)S(1)}, u32[]{:S(2)}, u32[]{:S(2)}) collective-permute-start(f32[2,4,5,128,128]{4,3,2,1,0:T(8,128)} %get-tuple-element.188), channel_id=1, source_target_pairs={{0,16},{1,17},{2,18},{3,19},{4,20},{5,21},{6,22},{7,23},{8,24},{9,... | collective-permute-start | bytes 7864328 | tf_op jit(solution)/shard_map/ppermute | solution.py:861
  101.0 61.9 %collective-permute-start.13 = (f32[2,4,5,128,128]{4,3,2,1,0:T(8,128)}, f32[2,4,5,128,128]{4,3,2,1,0:T(8,128)}, u32[]{:S(2)}, u32[]{:S(2)}) collective-permute-start(f32[2,4,5,128,128]{4,3,2,1,0:T(8,128)} %get-tuple-element.165.refs_7_), channel_id=1, source_target_pairs={{0,8},{1,9},{2,10},{3,11},{4,12},{5,13},{6,14},{7,15},{8,0},{9,1},... | collective-permute-start | bytes 7864328 | tf_op jit(solution)/shard_map/ppermute | solution.py:861
  144.5 24.9 %collective-permute-start.12 = (f32[2,4,136,128]{3,2,1,0:T(8,128)S(1)}, f32[2,4,136,128]{3,2,1,0:T(8,128)}, u32[]{:S(2)}, u32[]{:S(2)}) collective-permute-start(f32[2,4,136,128]{3,2,1,0:T(8,128)S(1)} %select_add_fusion.6.refs_19_), channel_id=1, source_target_pairs={{0,4},{1,5},{2,6},{3,7},{4,0},{5,1},{6,2},{7,3},{8,12},{9,13},{10,... | collective-permute-start | bytes 1671176 | tf_op jit(solution)/shard_map/ppermute | solution.py:861
  170.8 56.4 %collective-permute-start.19 = (f32[2,4,3,128,128]{4,3,2,1,0:T(8,128)}, f32[2,4,3,128,128]{4,3,2,1,0:T(8,128)S(1)}, u32[]{:S(2)}, u32[]{:S(2)}) collective-permute-start(f32[2,4,3,128,128]{4,3,2,1,0:T(8,128)} %get-tuple-element.203), channel_id=1, source_target_pairs={{0,16},{1,17},{2,18},{3,19},{4,20},{5,21},{6,22},{7,23},{8,24},{9,... | collective-permute-start | bytes 4718600 | tf_op jit(solution)/shard_map/ppermute | solution.py:861
  172.4 54.8 %collective-permute-start.17 = (f32[2,4,3,128,128]{4,3,2,1,0:T(8,128)}, f32[2,4,3,128,128]{4,3,2,1,0:T(8,128)S(1)}, u32[]{:S(2)}, u32[]{:S(2)}) collective-permute-start(f32[2,4,3,128,128]{4,3,2,1,0:T(8,128)} %get-tuple-element.195), channel_id=1, source_target_pairs={{0,8},{1,9},{2,10},{3,11},{4,12},{5,13},{6,14},{7,15},{8,0},{9,1},... | collective-permute-start | bytes 4718600 | tf_op jit(solution)/shard_map/ppermute | solution.py:861
  206.8 143.0 %reduce-scatter.5.cloned.1.call-start = ((), (), s32[]{:S(2)}) async-start(), calls=%async_computation.3 | async-start | bytes 81920 | tf_op jit(solution)/shard_map/reduce_scatter | solution.py:920
  206.9 29.3 %collective-permute-start.20 = (f32[4,4,128,128]{3,2,1,0:T(8,128)}, f32[4,4,128,128]{3,2,1,0:T(8,128)}, u32[]{:S(2)}, u32[]{:S(2)}) collective-permute-start(f32[4,4,128,128]{3,2,1,0:T(8,128)} %get-tuple-element.190.refs_13_), channel_id=1, source_target_pairs={{0,8},{1,9},{2,10},{3,11},{4,12},{5,13},{6,14},{7,15},{8,0},{9,1},... | collective-permute-start | bytes 3145736 | tf_op jit(solution)/shard_map/ppermute | solution.py:861
  207.5 28.7 %collective-permute-start.16 = (f32[4,4,128,128]{3,2,1,0:T(8,128)}, f32[4,4,128,128]{3,2,1,0:T(8,128)}, u32[]{:S(2)}, u32[]{:S(2)}) collective-permute-start(f32[4,4,128,128]{3,2,1,0:T(8,128)} %get-tuple-element.193), channel_id=1, source_target_pairs={{0,16},{1,17},{2,18},{3,19},{4,20},{5,21},{6,22},{7,23},{8,24},{9,... | collective-permute-start | bytes 3145736 | tf_op jit(solution)/shard_map/ppermute | solution.py:861
  231.8 36.2 %collective-permute-start.23 = (f32[4,3,128,128]{3,2,1,0:T(8,128)}, f32[4,3,128,128]{3,2,1,0:T(8,128)S(1)}, u32[]{:S(2)}, u32[]{:S(2)}) collective-permute-start(f32[4,3,128,128]{3,2,1,0:T(8,128)} %get-tuple-element.205), channel_id=1, source_target_pairs={{0,8},{1,9},{2,10},{3,11},{4,12},{5,13},{6,14},{7,15},{8,0},{9,1},... | collective-permute-start | bytes 2359304 | tf_op jit(solution)/shard_map/ppermute | solution.py:861
  232.3 35.7 %collective-permute-start.22 = (f32[4,3,128,128]{3,2,1,0:T(8,128)}, f32[4,3,128,128]{3,2,1,0:T(8,128)S(1)}, u32[]{:S(2)}, u32[]{:S(2)}) collective-permute-start(f32[4,3,128,128]{3,2,1,0:T(8,128)} %get-tuple-element.214), channel_id=1, source_target_pairs={{0,16},{1,17},{2,18},{3,19},{4,20},{5,21},{6,22},{7,23},{8,24},{9,... | collective-permute-start | bytes 2359304 | tf_op jit(solution)/shard_map/ppermute | solution.py:861
  240.3 54.7 %collective-permute-start.26 = (f32[2,4,3,128,128]{4,3,2,1,0:T(8,128)}, f32[2,4,3,128,128]{4,3,2,1,0:T(8,128)}, u32[]{:S(2)}, u32[]{:S(2)}) collective-permute-start(f32[2,4,3,128,128]{4,3,2,1,0:T(8,128)} %get-tuple-element.225), channel_id=1, source_target_pairs={{0,16},{1,17},{2,18},{3,19},{4,20},{5,21},{6,22},{7,23},{8,24},{9,... | collective-permute-start | bytes 4718600 | tf_op jit(solution)/shard_map/ppermute | solution.py:861
  240.9 54.1 %collective-permute-start.25 = (f32[2,4,3,128,128]{4,3,2,1,0:T(8,128)}, f32[2,4,3,128,128]{4,3,2,1,0:T(8,128)}, u32[]{:S(2)}, u32[]{:S(2)}) collective-permute-start(f32[2,4,3,128,128]{4,3,2,1,0:T(8,128)} %get-tuple-element.221), channel_id=1, source_target_pairs={{0,8},{1,9},{2,10},{3,11},{4,12},{5,13},{6,14},{7,15},{8,0},{9,1},... | collective-permute-start | bytes 4718600 | tf_op jit(solution)/shard_map/ppermute | solution.py:861
  243.8 47.6 %collective-permute-start.21 = (f32[2,8,128,128]{3,2,1,0:T(8,128)S(1)}, f32[2,8,128,128]{3,2,1,0:T(8,128)}, u32[]{:S(2)}, u32[]{:S(2)}) collective-permute-start(f32[2,8,128,128]{3,2,1,0:T(8,128)S(1)} %dynamic-slice_bitcast_fusion), channel_id=1, source_target_pairs={{0,2},{1,3},{2,0},{3,1},{4,6},{5,7},{6,4},{7,5},{8,10},{9,11},{10,... | collective-permute-start | bytes 3145736 | tf_op jit(solution)/shard_map/ppermute | solution.py:861
  291.4 44.8 %collective-permute-start.27 = (f32[2,1024,1024]{2,1,0:T(8,128)}, f32[2,1024,1024]{2,1,0:T(8,128)}, u32[]{:S(2)}, u32[]{:S(2)}) collective-permute-start(f32[2,1024,1024]{2,1,0:T(8,128)} %get-tuple-element.229), channel_id=1, source_target_pairs={{0,1},{1,0},{2,3},{3,2},{4,5},{5,4},{6,7},{7,6},{8,9},{9,8},{10,11... | collective-permute-start | bytes 25165832 | tf_op jit(solution)/shard_map/ppermute | solution.py:861
  292.5 33.7 %collective-permute-start.32 = (f32[8,128,128]{2,1,0:T(8,128)S(1)}, f32[8,128,128]{2,1,0:T(8,128)}, u32[]{:S(2)}, u32[]{:S(2)}) collective-permute-start(f32[8,128,128]{2,1,0:T(8,128)S(1)} %bitcast_add_fusion.1.refs_5_), channel_id=1, source_target_pairs={{0,4},{1,5},{2,6},{3,7},{4,0},{5,1},{6,2},{7,3},{8,12},{9,13},{10,... | collective-permute-start | bytes 1572872 | tf_op jit(solution)/shard_map/ppermute | solution.py:861
  301.7 53.6 %collective-permute-start.34 = (f32[6,128,128]{2,1,0:T(8,128)}, f32[6,128,128]{2,1,0:T(8,128)}, u32[]{:S(2)}, u32[]{:S(2)}) collective-permute-start(f32[6,128,128]{2,1,0:T(8,128)} %bitcast_add_fusion.4.refs_6_), channel_id=1, source_target_pairs={{0,4},{1,5},{2,6},{3,7},{4,0},{5,1},{6,2},{7,3},{8,12},{9,13},{10,... | collective-permute-start | bytes 1179656 | tf_op jit(solution)/shard_map/ppermute | solution.py:861
  328.5 32.4 %collective-permute-start.35 = (f32[6,128,128]{2,1,0:T(8,128)}, f32[6,128,128]{2,1,0:T(8,128)}, u32[]{:S(2)}, u32[]{:S(2)}) collective-permute-start(f32[6,128,128]{2,1,0:T(8,128)} %get-tuple-element.278), channel_id=1, source_target_pairs={{0,4},{1,5},{2,6},{3,7},{4,0},{5,1},{6,2},{7,3},{8,12},{9,13},{10,... | collective-permute-start | bytes 1179656 | tf_op jit(solution)/shard_map/ppermute | solution.py:861
  332.0 38.7 %collective-permute-start.36 = (f32[6,128,128]{2,1,0:T(8,128)}, f32[6,128,128]{2,1,0:T(8,128)}, u32[]{:S(2)}, u32[]{:S(2)}) collective-permute-start(f32[6,128,128]{2,1,0:T(8,128)} %get-tuple-element.280), channel_id=1, source_target_pairs={{0,2},{1,3},{2,4},{3,5},{4,6},{5,7},{6,0},{7,1},{8,10},{9,11},{10,... | collective-permute-start | bytes 1179656 | tf_op jit(solution)/shard_map/ppermute | solution.py:861
  332.0 40.5 %collective-permute-start.37 = (f32[6,128,128]{2,1,0:T(8,128)}, f32[6,128,128]{2,1,0:T(8,128)}, u32[]{:S(2)}, u32[]{:S(2)}) collective-permute-start(f32[6,128,128]{2,1,0:T(8,128)} %get-tuple-element.279), channel_id=1, source_target_pairs={{0,6},{1,7},{2,0},{3,1},{4,2},{5,3},{6,4},{7,5},{8,14},{9,15},{10,... | collective-permute-start | bytes 1179656 | tf_op jit(solution)/shard_map/ppermute | solution.py:861
  (63 other events, 526.9 us)
Sparse Core Ops, SparseCore 0:
  206.9 27.4 reduce-scatter.2
  318.5 24.2 reduce-scatter.4

commit v4 on v3

--- a/solution.py
+++ b/solution.py
@@ -231,32 +231,58 @@
     )
 
 
-def finish_kernel(at, slots, cut, u_keep, u_one, u_two, d_keep, d_one, d_two, out):
+def finish_kernel(at, slots, cut, direct, pos, u_keep, u_one, u_two, d_keep, d_one, d_two, *refs):
+    outs = refs[-4:] if direct else refs[-2:]
+    more = refs[: -len(outs)]
     own = slice(at, at + slots)
-    for n, (keep, one, two) in enumerate(((u_keep, u_one, u_two), (d_keep, d_one, d_two))):
+    step = pl.program_id(0)
+    parts = []
+    for keep, one, two in ((u_keep, u_one, u_two), (d_keep, d_one, d_two)):
         if cut is None:
             second = two[...]
         else:
             second = two[0, :, cut[0] : cut[1]].reshape(2, slots, 128, 128)
-        out[:, n * slots : (n + 1) * slots] = keep[0] + one[0, :, own] + second
-
-
-def finish(keeps, ones, at, twos, cut):
+        parts.append((keep[0] + one[0, :, own] + second).reshape(2, slots * 128, 128))
+    both = jnp.concatenate(parts + [rows[...] for rows in more], 1)
+    if not direct:
+        kept, sent = swapped(lax.rem(pos[2], 2), both[0], both[1])
+        outs[0][0], outs[1][0] = kept, sent
+        return
+
+    def put(out, value):
+        out[...] = value
+
+    for low in range(2):
+        ahead = lax.rem(2 * step + low - pos[2] + 4, 4)
+        for n, out in enumerate(outs):
+            pl.when(ahead == n)(functools.partial(put, out, both[low]))
+
+
+def finish(pos, keeps, ones, at, twos, cut, more=(), direct=False):
     slots, total = keeps[0].shape[2], ones[0].shape[2]
-    keep = pl.BlockSpec((1, 2, slots, 128, 128), lambda i: (0, i, 0, 0, 0))
-    one = pl.BlockSpec((1, 2, total, 128, 128), lambda i: (0, i, 0, 0, 0))
+    keep = pl.BlockSpec((1, 2, slots, 128, 128), lambda i, p: (0, i, 0, 0, 0))
+    one = pl.BlockSpec((1, 2, total, 128, 128), lambda i, p: (0, i, 0, 0, 0))
     if cut is None:
-        two = pl.BlockSpec((2, slots, 128, 128), lambda i: (i, 0, 0, 0))
+        two = pl.BlockSpec((2, slots, 128, 128), lambda i, p: (i, 0, 0, 0))
     else:
-        two = pl.BlockSpec((1, 4, twos[0].shape[2], 128, 128), lambda i: (i, 0, 0, 0, 0))
+        two = pl.BlockSpec((1, 4, twos[0].shape[2], 128, 128), lambda i, p: (i, 0, 0, 0, 0))
+    lines = 256 * slots + sum(m.shape[1] for m in more)
+    if direct:
+        out = [pl.BlockSpec((lines, 128), lambda i, p: (0, 0))] * 4
+        shapes = [struct((lines, 128), f32)] * 4
+    else:
+        out = [pl.BlockSpec((1, lines, 128), lambda i, p: (i, 0, 0))] * 2
+        shapes = [struct((2, lines, 128), f32)] * 2
     return ordered_call(
-        functools.partial(finish_kernel, at, slots, cut),
-        [keeps[0], ones[0], twos[0], keeps[1], ones[1], twos[1]],
+        functools.partial(finish_kernel, at, slots, cut, direct),
+        [pos, keeps[0], ones[0], twos[0], keeps[1], ones[1], twos[1], *more],
         [],
+        prefetch=1,
         grid=(2,),
-        in_specs=[keep, one, two] * 2,
-        out_specs=pl.BlockSpec((2, 2 * slots, 128, 128), lambda i: (i, 0, 0, 0)),
-        out_shape=struct((4, 2 * slots, 128, 128), f32),
+        in_specs=[keep, one, two] * 2
+        + [pl.BlockSpec((2, m.shape[1], 128), lambda i, p: (i, 0, 0)) for m in more],
+        out_specs=out,
+        out_shape=shapes,
         cost_estimate=cost(f"finish{slots}"),
         name="finish",
     )
@@ -371,7 +397,7 @@
 
 
 def feature_kernel(
-    a1, wq, wk, wv, bq, bk, bv, fw, matrix, cos, sin1, sin2, valid, qf_o, kf_o, v_o, st_o
+    pos, a1, wq, wk, wv, bq, bk, bv, fw, matrix, cos, sin1, sin2, valid, qf_o, kf_o, v_o, own, send
 ):
     x = a1[...]
     count = x.shape[0] // LEN_BLK
@@ -392,19 +418,36 @@
         kf_o[rows(i)] = kf
         k[i] = kf
         v_o[rows(i)] = v[i]
+    states = []
     for i in range(count):
         state = [
             dot(k[i][:, 128 * p : 128 * p + 128], v[i][:, 128 * p : 128 * p + 128], 0, 0)
             for p in range(2)
         ]
-        st_o[i, 0, :128] = pack(state[0], state[1])
         norm = jnp.sum(k[i].astype(f32), axis=0, keepdims=True)
-        st_o[i, 0, 128:] = norm_rows(norm[:, :128], norm[:, 128:])
+        lines = norm_rows(norm[:, :128], norm[:, 128:])
+        states.append(jnp.concatenate([pack(state[0], state[1]), lines], 0))
+    put_states(pos[1], states, own, send)
 
 
 def norm_rows(first, second):
     line = iota((8, 128), 0)
     return jnp.where(line == 0, first, jnp.where(line == 1, second, 0.0))
+
+
+def put_states(core, states, own, send):
+    half = len(states) // 2
+    for j in range(half):
+        first, second = states[j], states[half + j]
+        own[j, 0] = jnp.where(core == 0, first, second)
+        send[j, 0] = jnp.where(core == 0, second, first)
+
+
+def state_of(core, pair, i):
+    here, there = pair
+    half = here.shape[0]
+    j = i % half
+    return jnp.where(core == i // half, here[j, 0], there[j, 0])
 
 
 def scores(qp, kp, causal):
@@ -419,7 +462,7 @@
     return iota((n, n), 0) >= iota((n, n), 1)
 
 
-def mix_kernel(pos, g, wo, qf, kf, v, st, mix_o, dn_o, dd_o, ds_o, *sends):
+def mix_kernel(pos, g, wo, qf, kf, v, here, there, mix_o, dn_o, dd_o, own, send, *sends):
     count = qf.shape[0] // LEN_BLK
     mask = pair_mask()
     lane = iota((1, 128), 1)
@@ -434,9 +477,10 @@
     grad_mixed = dot(g[...], wo[...], 1, 1)
     both = {}
     for i in range(count):
-        state = unpack(st[i, 0, :128])
+        carried = state_of(pos[1], (here, there), i)
+        state = unpack(carried[:128])
         for p in range(2):
-            column = to_column(st[i, 0, 128 + p : 129 + p])
+            column = to_column(carried[128 + p : 129 + p])
             norm = jnp.where(mask, jnp.broadcast_to(column, (128, 128)), 0.0)
             hi, lo = split(jnp.concatenate([state[p], norm], 1))
             qp = q[i, p]
@@ -466,14 +510,15 @@
     for i, p in cells:
         d0, d1 = sums[i, p]
         norms[i, p] = column_sum(q[i, p].astype(f32) * jnp.where(first, d0, d1))
+    states = []
     for i in range(count):
         lines = jnp.zeros((LEN_BLK, 128), f32)
         for p in range(2):
             d0, d1 = sums[i, p]
             lines = jnp.where(lane == 2 * p, d0, jnp.where(lane == 2 * p + 1, d1, lines))
         dd_o[0, rows(i)] = lines
-        ds_o[i, 0, :128] = pack(grads[i, 0], grads[i, 1])
-        ds_o[i, 0, 128:] = norm_rows(norms[i, 0], norms[i, 1])
+        lines = norm_rows(norms[i, 0], norms[i, 1])
+        states.append(jnp.concatenate([pack(grads[i, 0], grads[i, 1]), lines], 0))
         other_half = jnp.where(pos[1] == 0, mixes[i, 1].astype(f32), mixes[i, 0].astype(f32))
 
         def put(out, lines=rows(i), other_half=other_half):
@@ -481,13 +526,17 @@
 
         for n, out in enumerate(sends):
             pl.when(lax.div(pl.program_id(0), 2) == n)(functools.partial(put, out))
+    put_states(pos[1], states, own, send)
 
 
 def back_kernel(
-    pos, qf, kf, v, dn, dd, st, ds, fw, matrix, cos, sin1, sin2, gp_o, send_o, bias_o, fw_o
+    pos, qf, kf, v, dn, dd, here, there, l_here, l_there, fw, matrix, cos, sin1, sin2, *outs
 ):
+    gp_o, send_o, bias_o, fw_o = outs
     count = qf.shape[0] // LEN_BLK
     step = pl.program_id(1)
+    before = [state_of(pos[1], (here, there), i) for i in range(count)]
+    after = [state_of(pos[1], (l_here, l_there), i) for i in range(count)]
     causal = lower(LEN_BLK)
     lane = iota((1, 128), 1)
     first = lane < 64
@@ -513,7 +562,7 @@
         ]
     dq, dk, dv = {}, {}, {}
     for i in range(count):
-        state, later = unpack(st[i, 0, :128]), unpack(ds[i, 0, :128])
+        state, later = unpack(before[i][:128]), unpack(after[i][:128])
         for p in range(2):
             c = i, p
             s_hi, s_lo = split(state[p])
@@ -528,9 +577,9 @@
         dv[c] = dv[c] + dot(jnp.concatenate(s[c], 0), jnp.concatenate(each_head(d[c]), 0), 0, 0)
     for i, p in cells:
         c = i, p
-        norm = jnp.where(first, *col[c]) * st[i, 0, 128 + p : 129 + p]
+        norm = jnp.where(first, *col[c]) * before[i][128 + p : 129 + p]
         dq[c] = (dq[c] + norm) * q[c].astype(f32)
-        dk[c] = (dk[c] + ds[i, 0, 128 + p : 129 + p]) * k[c].astype(f32)
+        dk[c] = (dk[c] + after[i][128 + p : 129 + p]) * k[c].astype(f32)
     whole = lambda parts: jnp.concatenate(
         [jnp.concatenate([parts[i, 0], parts[i, 1]], 1) for i in range(count)], 0
     )
@@ -568,52 +617,55 @@
         grid=(4, seqs // per),
         wide=pl.BlockSpec((rows, 1024), lambda h, g, *_: (g, 0)),
         head=pl.BlockSpec((rows, HG), lambda h, g, *_: (g, h)),
-        state=pl.BlockSpec((per, 1, 136, 128), lambda h, g, *_: (g, h, 0, 0)),
+        state=pl.BlockSpec((seqs // 2, 1, 136, 128), lambda h, g, *_: (0, h, 0, 0)),
         row=pl.BlockSpec((1, HG), lambda h, g, *_: (0, h)),
         table=pl.BlockSpec((256, 256), lambda h, g, *_: (0, 0)),
         dden=pl.BlockSpec((1, rows, 128), lambda h, g, *_: (h, g, 0)),
     )
 
 
-def features(a1, w_qkv, b_qkv, feat_weight, matrix, turns, valid, after=(), per=4):
+def features(pos, a1, w_qkv, b_qkv, feat_weight, matrix, turns, valid, after=()):
     rows = a1.shape[0]
-    seqs = rows // LEN_BLK
+    seqs = per = rows // LEN_BLK
     s = attention_specs(seqs, per)
-    weights = [pl.BlockSpec((1024, HG), lambda h, g, o=o: (0, 4 * o + h)) for o in range(3)]
-    biases = [pl.BlockSpec((1, HG), lambda h, g, o=o: (0, 4 * o + h)) for o in range(3)]
+    weights = [pl.BlockSpec((1024, HG), lambda h, g, *_, o=o: (0, 4 * o + h)) for o in range(3)]
+    biases = [pl.BlockSpec((1, HG), lambda h, g, *_, o=o: (0, 4 * o + h)) for o in range(3)]
     return ordered_call(
         feature_kernel,
-        [a1, w_qkv, w_qkv, w_qkv, b_qkv, b_qkv, b_qkv, feat_weight, matrix, *turns, valid],
+        [pos, a1, w_qkv, w_qkv, w_qkv, b_qkv, b_qkv, b_qkv, feat_weight, matrix, *turns, valid],
         after,
+        prefetch=1,
         grid=s["grid"],
         in_specs=[s["wide"], *weights, *biases, s["row"]]
         + [s["table"]] * 4
-        + [pl.BlockSpec((LEN_BLK * per, 1), lambda h, g: (g, 0))],
-        out_specs=[s["head"]] * 3 + [s["state"]],
-        out_shape=[struct((rows, 1024), bf16)] * 3 + [struct((seqs, 4, 136, 128), f32)],
+        + [pl.BlockSpec((LEN_BLK * per, 1), lambda h, g, *_: (g, 0))],
+        out_specs=[s["head"]] * 3 + [s["state"]] * 2,
+        out_shape=[struct((rows, 1024), bf16)] * 3
+        + [struct((seqs // 2, 4, 136, 128), f32)] * 2,
         cost_estimate=cost("features"),
         name="features",
     )
 
 
-def mixing(pos, g, w_out, qf, kf, v, state, after=(), per=2):
+def mixing(pos, g, w_out, qf, kf, v, state, after=()):
     rows = g.shape[0]
-    seqs = rows // LEN_BLK
+    seqs = per = rows // LEN_BLK
     steps = seqs // per
     s = attention_specs(seqs, per)
     return ordered_call(
         mix_kernel,
-        [pos, g, w_out, qf, kf, v, state],
+        [pos, g, w_out, qf, kf, v, *state],
         after,
         prefetch=1,
         grid=s["grid"],
         in_specs=[s["wide"], pl.BlockSpec((HG, 1024), lambda h, g, *_: (h, 0))]
         + [s["head"]] * 3
-        + [s["state"]],
+        + [s["state"]] * 2,
         out_specs=[
             s["head"],
             s["head"],
             s["dden"],
+            s["state"],
             s["state"],
             pl.BlockSpec(
                 (LEN_BLK * per, 128),
@@ -628,7 +680,8 @@
             struct((rows, 1024), bf16),
             struct((rows, 1024), bf16),
             struct((4, rows, 128), f32),
-            struct((seqs, 4, 136, 128), f32),
+            struct((seqs // 2, 4, 136, 128), f32),
+            struct((seqs // 2, 4, 136, 128), f32),
             struct((rows, 256), f32),
             struct((rows, 256), f32),
         ],
@@ -642,12 +695,14 @@
     s = attention_specs(seqs, per)
     return ordered_call(
         back_kernel,
-        [pos, qf, kf, v, dn, dd, state, later, feat_weight, matrix, *turns],
+        [pos, qf, kf, v, dn, dd, *state, *later, feat_weight, matrix, *turns],
         after,
         prefetch=1,
         grid=s["grid"],
         in_specs=[s["head"]] * 4
-        + [s["dden"], s["state"], s["state"], s["row"]]
+        + [s["dden"]]
+        + [s["state"]] * 4
+        + [s["row"]]
         + [s["table"]] * 4,
         out_specs=[
             pl.BlockSpec((3, LEN_BLK * per, HG), lambda h, g, *_: (0, g, h)),
@@ -910,36 +965,24 @@
         self.twos = group.ones[::-1]
         self.cut = (0, group.at) if group.at else (group.slots, total)
 
-    def done(self, *behind):
+    def done(self, pos, *behind, more=(), direct=False):
         twos = [hold(two, behind) for two in self.twos]
-        return finish(self.keeps, self.ones, self.at, twos, self.cut)
-
-
-def reduce_z(value):
-    groups = [[0, 2, 4, 6], [1, 3, 5, 7]]
-    return lax.psum_scatter(
-        value, "seq", scatter_dimension=0, axis_index_groups=groups, tiled=True
-    )[0]
+        return finish(pos, self.keeps, self.ones, self.at, twos, self.cut, more, direct)
 
 
 class Carried:
-    def __init__(self, links, state, reverse):
-        self.links, self.state, self.reverse = links, state, reverse
+    def __init__(self, links, own, sent, reverse):
+        self.links, self.own, self.sent, self.reverse = links, own, sent, reverse
         self.sign = -1 if reverse else 1
-        self.mine = self.sum = None
+        self.core = lax.rem(lax.axis_index("seq"), 2)
         if links.tuned:
-            self.core = lax.rem(lax.axis_index("seq"), 2)
-            self.half = state.shape[0] // 2
-            self.other = links.core(self.of_half(1 - self.core))
-
-    def of_half(self, which):
-        return lax.dynamic_slice_in_dim(self.state, which * self.half, self.half, 0)
+            self.other = links.core(sent)
 
     def near(self, *behind):
         if not self.links.tuned:
             return None
         self.other = hold(self.other, behind)
-        self.mine = self.of_half(self.core) + self.other
+        self.mine = self.own + self.other
         self.one, self.one_kept = self.links.ring(self.mine, self.sign * 2)
         return self.mine
 
@@ -954,53 +997,46 @@
     def done(self, *behind):
         links = self.links
         if not links.tuned:
-            total, step = self.state, 1
+            halves = jnp.stack([self.own, self.sent], 0)
+            total, step = jnp.where(self.core == 0, halves, halves[::-1]), 1
             while step < links.ns:
                 total = total + links.shift(total, self.sign * step)
                 step *= 2
-            return links.shift(total, self.sign)
+            total = links.shift(total, self.sign)
+            return tuple(jnp.where(self.core == 0, total, total[::-1]))
         self.two = hold(self.two, behind)
         before = self.one + jnp.where(self.two_kept, self.two, 0.0)
         second = self.core == (0 if self.reverse else 1)
         here = before + jnp.where(second, self.other, 0.0)
-        there = before + jnp.where(second, 0.0, self.of_half(self.core))
-        rest = links.core(there)
-        low = jnp.where(self.core == 0, here, rest)
-        high = jnp.where(self.core == 0, rest, here)
-        return jnp.concatenate([low, high], 0)
+        there = before + jnp.where(second, 0.0, self.own)
+        return here, links.core(there)
 
 
 class Line:
-    def __init__(self, links, value):
-        self.z = lax.div(lax.axis_index("seq"), 2)
-        self.value = value
-        self.parts = []
-        for by in (2, 1, 3):
-            part = self.pick(lax.rem(self.z + by, 4))
-            self.parts.append(links.send(part, lambda b, s: (b, (s + 2 * by) % 8)))
-
-    def pick(self, at):
-        return lax.dynamic_index_in_dim(self.value, at, 0, keepdims=False)
+    def __init__(self, links, parts):
+        self.mine = parts[0]
+        self.parts = [
+            links.send(parts[by], lambda b, s, by=by: (b, (s + 2 * by) % 8)) for by in (2, 1, 3)
+        ]
 
     def done(self, *behind):
-        total = self.pick(self.z)
+        total = self.mine
         for part in self.parts:
             total = total + hold(part, behind)
         return total
 
 
 class Halves:
-    def __init__(self, links, value):
-        self.links = links
+    def __init__(self, links, kept, sent):
+        self.links, self.kept = links, kept
         self.z = lax.div(lax.axis_index("seq"), 2)
-        both = value.reshape((2, 2) + value.shape[1:])
-        low = lax.rem(self.z, 2)
-        pick = lambda i: lax.dynamic_index_in_dim(both, i, 1, keepdims=False)
-        self.kept = pick(low)
-        self.one = links.send(pick(1 - low), lambda b, s: (b, s ^ 2))
+        self.one = links.send(sent, lambda b, s: (b, s ^ 2))
+
+    def arrived(self, *behind):
+        self.one = hold(self.one, behind)
 
     def stage_two(self, *behind):
-        self.one = hold(self.one, behind)
+        self.arrived(*behind)
         self.high = lax.div(self.z, 2)
         out = self.pick(1 - self.high)
         self.two = self.links.send(out, lambda b, s: (b, s ^ 4))
@@ -1010,8 +1046,11 @@
         at = lambda v: lax.dynamic_index_in_dim(v, i, 0, keepdims=False)
         return at(self.kept) + at(self.one)
 
+    def landed(self, *behind):
+        self.two = hold(self.two, behind)
+
     def done(self, *behind):
-        self.two = hold(self.two, behind)
+        self.landed(*behind)
         return self.pick(self.high) + self.two
 
 
@@ -1055,7 +1094,8 @@
             up_o[half, k] = blocks[2 * k + half]
 
 
-def in_place(blocks, count, after, start=None):
+def in_place(rows, count, after, start=None):
+    blocks = rows.reshape(-1, 128, 128)
     return ordered_call(
         functools.partial(in_place_kernel, count, start or 2 * count),
         [blocks],
@@ -1129,7 +1169,7 @@
     place = lax.axis_index("seq")
     me = lax.axis_index("batch") if tuned else 0 * place
     core = lax.rem(place, 2)
-    pos = jnp.stack([me, core]).astype(jnp.int32)
+    pos = jnp.stack([me, core, lax.div(place, 2)]).astype(jnp.int32)
     places = place * block + jnp.arange(block, dtype=jnp.int32)
     valid = (places[None, :] < lengths[:, None]) & ((key_mask == 1) | (places[None, :] == 0))
     valid = valid.astype(f32).reshape(rows, 1)
@@ -1144,8 +1184,10 @@
     turns = rotation_tables(places.astype(f32))
     weights = row(feat_weight)
 
-    qf, kf, v, state = features(a1, w_qkv, row(b_qkv), weights, forth, turns, valid)
-    forward = Carried(links, state, False)
+    qf, kf, v, state, state_sent = features(
+        pos, a1, w_qkv, row(b_qkv), weights, forth, turns, valid
+    )
+    forward = Carried(links, state, state_sent, False)
     x_other = hold(x_other, [state])
     a1_o, a2_o, g_o = norms(
         x_other, hold(g_other, [state]), *gains, g_type=bf16, after=[state]
@@ -1168,10 +1210,10 @@
         first[0::2] = g0.second_in(*first[0::2], 4)
     g1 = Group(links, *first)
     state_in = forward.done(c1[8])
-    mixed, dn, dd, state_grad, *mixed_send = mixing(
+    mixed, dn, dd, grad_own, grad_sent, *mixed_send = mixing(
         pos, g, w_out, qf, kf, v, state_in, after=first[:1]
     )
-    reverse = Carried(links, state_grad, True)
+    reverse = Carried(links, grad_own, grad_sent, True)
     mixed_other = [links.core(part) for part in mixed_send]
     back = head_blocks_after(directions, [mixed])
     held = [reverse.near(back)]
@@ -1202,34 +1244,37 @@
         after=held,
     )
     grad_other = links.core(grad_send)
+    held = [grad_proj]
     if tuned:
-        z0 = g0.done(grad_proj)
-        early = reduce_z(z0)
-    last_parts = qkv_grad(
-        pos, (a1, a1_o), grad_proj, hold(grad_other, [grad_proj, z0]), after=[z0]
-    )
+        z0, z0_sent = g0.done(pos, grad_proj)
+        g2.arrived(z0)
+        held = [z0, g2.second()]
+    grad_other = hold(grad_other, held)
+    if tuned:
+        early = Halves(links, z0, hold(z0_sent, [grad_other]))
+    last_parts = qkv_grad(pos, (a1, a1_o), grad_proj, grad_other, after=held)
     acts = c2[:4]
     held = [last_parts[0]]
     pieces = list(last_parts)
     if tuned:
-        g2.arrived(last_parts[0])
-        held = [g2.second()]
-        z1 = g1.done(*held)
-        later = Halves(links, z1)
+        z1, z1_sent = g1.done(pos, last_parts[0])
+        later = Halves(links, z1, z1_sent)
         pieces[0::2] = [hold(piece, [z1]) for piece in pieces[0::2]]
-        held = [z1]
+        early.arrived(last_parts[0])
+        held = [z1, early.one]
     g3 = Group(links, *pieces)
     own_g = hidden_rows(pos, acts[2:], w_up, (x, x_other), after=held)
     held = [own_g[1]]
     if tuned:
-        z2 = g2.done(own_g[1])
-        middle = Halves(links, z2)
-        held += [z2, early]
+        z2, z2_sent = g2.done(pos, own_g[1])
+        middle = Halves(links, z2, z2_sent)
+        held += [z2, early.stage_two()]
     own_r = hidden_rows(pos, acts[:2], w_down, sends=own_g[0], after=held)
     others = links.core(own_r[0])
     held = [own_r[1]]
     if tuned:
-        held = [later.stage_two(own_r[1]), middle.stage_two(own_r[1])]
+        early.landed(own_r[1])
+        held = [later.stage_two(early.two), middle.stage_two(early.two)]
         g3.arrived(own_r[1])
         held.append(g3.second())
     partial, sums1 = first_norm(x, g, grad_proj, w_qkv, row(ln1_gain), after=held)
@@ -1250,11 +1295,10 @@
     held = [partial]
     if tuned:
         lines = jnp.pad(lines.reshape(8, 13, 128), ((0, 0), (0, 3), (0, 0)))
-        lines = reduce_z(lines.reshape(4, 32, 128))
-        z3 = g3.done(partial)
-        later = later.done(z3)
+        z3 = g3.done(pos, partial, more=(lines.reshape(4, 32, 128),), direct=True)
+        later = later.done(z3[0])
         tail = Line(links, z3)
-        held = [z3]
+        held = [z3[0]]
     result, grad_input = ends(
         x,
         mixed,
@@ -1269,17 +1313,17 @@
     )
 
     if tuned:
-        lines = hold(lines, [result]).reshape(2, 16, 128)
+        first_down, first_up = in_place(early.done(result), 1, [result])
+        second_down, second_up = in_place(later, 2, [first_down])
+        middle = middle.done(second_down)
+        third_down, third_up = in_place(middle, 1, [second_down], start=3)
+        tail = tail.done(third_down)
+        lines = tail[768:].reshape(2, 16, 128)
         pick = lambda i: lax.dynamic_index_in_dim(lines, i, 0, keepdims=False)
-        lines, lines_other = pick(core), links.core(pick(1 - core))
-        first_down, first_up = in_place(early, 1, [lines])
-        lines = lines + hold(lines_other, [first_down])
-        second_down, second_up = in_place(later, 2, [lines])
-        lines = lines + hold(links.x(lines), [second_down])
-        middle = middle.done(second_down)
-        third_down, third_up = in_place(middle, 1, [lines], start=3)
-        lines = lines + hold(links.y(lines), [third_down])
-        tail = tail.done(third_down).reshape(6, 128, 128)
+        lines = pick(core) + links.core(pick(1 - core))
+        corner = links.send(lines, lambda b, s: (b ^ 3, s))
+        lines = lines + links.x(lines) + links.y(lines) + corner
+        tail = tail[:768].reshape(6, 128, 128)
         shares, at = [], 0
         for v_ in vectors:
             n = v_.shape[0] // 1024
@@ -1287,7 +1331,7 @@
             at += n
         halves = jnp.concatenate([first_up, second_up, third_up], 1)
         w_down_grad = jnp.concatenate([first_down, second_down, third_down], 0)
-        w_out_grad = jnp.concatenate([middle[2], middle[5]], 1)
+        w_out_grad = jnp.concatenate([middle[256:384], middle[640:768]], 1)
         blocks = [[tail[i] for i in (0, 3, 2)], [tail[i] for i in (1, 4, 5)]]
         blocks = jnp.stack([jnp.stack(b, 0) for b in blocks], 0)
         halves = jnp.concatenate([halves, blocks], 1)

time: 396 us -> 384 us (0.970)
  between operations: 15 us -> 1.52 us
  local copies, waits for them, and re-layouts: 26.3 us -> 19.9 us
    squeeze x4 -> x0, local copies, waits for them, and re-layouts: 5.66 us -> none  [the longest x2 3.35 us: __init__(): pick = lambda i: lax.dynamic_index_in_dim(both, i, 1, keepdims=False)]
    ppermute x39 -> x42, starting transfers between devices: 33.5 us -> 37 us  [send(): return lax.ppermute(value, ('batch', 'seq'), pairs)]
    unnamed x103 -> x109, local copies, waits for them, and re-layouts: 9.56 us -> 12 us
    ppermute x39 -> x42, waiting for transfers between devices: 31.1 us -> 30.8 us  [send(): return lax.ppermute(value, ('batch', 'seq'), pairs)]
  transfers between devices with their start and end apart: 41 -> 42, of which waited for: 10 -> 12; matrix products, arithmetic and copies ran while one was open for 10% -> 8% of each run, Pallas kernels for 64% -> 67%
where the time goes in v4:
time: 384 us; the launch traced here: 377 us
  Pallas kernels  260 us (68%)
  starting transfers between devices  37 us (10%)
  waiting for transfers between devices  30.8 us (8%)
  other arithmetic  27 us (7%)
  local copies, waits for them, and re-layouts  19.9 us (5%)
    pallas_call x26, Pallas kernels, ordered_call(): pl.pallas_call(body, grid_spec=pltpu.PrefetchScalarGridSpec(num_scalar_pr...  260 us
    ppermute x42, starting transfers between devices, send(): return lax.ppermute(value, ('batch', 'seq'), pairs)  37 us
    ppermute x42, waiting for transfers between devices, send(): return lax.ppermute(value, ('batch', 'seq'), pairs)  30.8 us
    unnamed x109, local copies, waits for them, and re-layouts  12 us
  transfers between devices with their start and end apart: 42, of which 12 were waited for; matrix products, arithmetic and copies ran while one was open for 8% of the time, Pallas kernels for 67%

profile of v4, /device:TPU:16, one launch (start us, length us, event | category | flops | bytes accessed | tf_op | source)
XLA Modules:
  0.0 377.2 jit_solution(10141740144944694570)
XLA Ops:
  0.7 7.5 %norms.2 = (bf16[1024,1024]{1,0:T(8,128)(2,1)}, bf16[1024,1024]{1,0:T(8,128)(2,1)}, f32[1024,1024]{1,0:T(8,128)}, f32[1024,1024]{1,0:T(8,128)}) custom-call(bf16[1024,1024]{1,0:T(8,128)(2,1)} %bitcast.118, bf16[1024,1024]{1,0:T(8,128)(2,1)} %bitcast.111, f32[1,1024]{1,0:T(1,128)} %bitcast.157, f32[1,1024]{1,0:T(1,128)} %bitcast.153, f32[1,1024]{1,0:T(1,128)} %bitcast.160, ...), custom_call_target="tpu_custom_call" | custom-call | flops 1 | bytes 1 | tf_op jit(solution)/shard_map/norms/pallas_call | solution.py:53
  13.5 17.8 %features.1 = (bf16[1024,1024]{1,0:T(8,128)(2,1)}, bf16[1024,1024]{1,0:T(8,128)(2,1)}, bf16[1024,1024]{1,0:T(8,128)(2,1)}, f32[2,4,136,128]{3,2,1,0:T(8,128)}, f32[2,4,136,128]{3,2,1,0:T(8,128)}) custom-call(s32[3]{0:T(128)} %pad_add_fusion.refs_0_, bf16[1024,1024]{1,0:T(8,128)(2,1)} %get-tuple-element.147.refs_1_, bf16[1024,3072]{1,0:T(8,128)(2,1)} %refs_3_.7, ...), custom_call_target="tpu_custom_call" | custom-call | flops 1 | bytes 1 | tf_op jit(solution)/shard_map/features/pallas_call | solution.py:53
  31.4 7.1 %norms.3 = (bf16[1024,1024]{1,0:T(8,128)(2,1)}, bf16[1024,1024]{1,0:T(8,128)(2,1)}, bf16[1024,1024]{1,0:T(8,128)(2,1)}) custom-call(f32[1024,1024]{1,0:T(8,128)} %collective-permute-done.1.refs_0_.refs_8_, f32[1024,1024]{1,0:T(8,128)} %collective-permute-done.2.refs_1_, f32[1,1024]{1,0:T(1,128)} %bitcast.158, f32[1,1024]{1,0:T(1,128)} %bitcast.154, ...), custom_call_target="tpu_custom_call" | custom-call | flops 1 | bytes 1 | tf_op jit(solution)/shard_map/norms/pallas_call | solution.py:53
  40.4 16.7 %ffn_chunk.3 = (bf16[2,8,1024,128]{3,2,1,0:T(8,128)(2,1)}, bf16[2,8,1024,128]{3,2,1,0:T(8,128)(2,1)}, bf16[2,8,1024,128]{3,2,1,0:T(8,128)(2,1)}, bf16[2,8,1024,1...) custom-call(s32[3]{0:T(128)} %pad_add_fusion.refs_0_, ...), custom_call_target="tpu_custom_call" | custom-call | flops 1 | bytes 1 | tf_op jit(solution)/shard_map/ffn_chunk/pallas_call | solution.py:53
  61.7 27.1 %ffn_chunk.4 = (bf16[2,8,1024,128]{3,2,1,0:T(8,128)(2,1)}, bf16[2,8,1024,128]{3,2,1,0:T(8,128)(2,1)}, bf16[2,8,1024,128]{3,2,1,0:T(8,128)(2,1)}, bf16[2,8,1024,1...) custom-call(s32[3]{0:T(128)} %pad_add_fusion.refs_0_, ...), custom_call_target="tpu_custom_call", output_to_operand_aliasing={{0}: (11, {}), {1}: (12, {}), {2}: (13, {}), {3}: (14, {})} | custom-call | flops 1 | bytes 1 | tf_op jit(solution)/shard_map/ffn_chunk/pallas_call | solution.py:53
  96.2 16.3 %mixing.1 = (bf16[1024,1024]{1,0:T(8,128)(2,1)}, bf16[1024,1024]{1,0:T(8,128)(2,1)}, f32[4,1024,128]{2,1,0:T(8,128)}, f32[2,4,136,128]{3,2,1,0:T(8,128)}, f32[2,...) custom-call(s32[3]{0:T(128)} %pad_add_fusion.refs_0_, bf16[1024,1024]{1,0:T(8,128)(2,1)} %bitcast.114, ...), custom_call_target="tpu_custom_call" | custom-call | flops 1 | bytes 1 | tf_op jit(solution)/shard_map/mixing/pallas_call | solution.py:53
  119.8 8.2 %out_grad.1 = (f32[2,4,3,128,128]{4,3,2,1,0:T(8,128)}, f32[2,4,3,128,128]{4,3,2,1,0:T(8,128)}, f32[2,4,3,128,128]{4,3,2,1,0:T(8,128)}, f32[2,4,3,128,128]{4,3,2,1,0:T(8,128)}) custom-call(s32[3]{0:T(128)} %pad_add_fusion.refs_0_, bf16[1024,1024]{1,0:T(8,128)(2,1)} %get-tuple-element.179.refs_2_.refs_1_, f32[1024,256]{1,0:T(8,128)} %collective-permute-done.10.refs_2_, ...), custom_call_target="tpu_custom_call" | custom-call | flops 1 | bytes 1 | tf_op jit(solution)/shard_map/out_grad/pallas_call | solution.py:53
  128.0 5.8 %collective-permute-done.9 = f32[2,4,136,128]{3,2,1,0:T(8,128)} collective-permute-done((f32[2,4,136,128]{3,2,1,0:T(8,128)S(1)}, f32[2,4,136,128]{3,2,1,0:T(8,128)}, u32[]{:S(2)}, u32[]{:S(2)}) %collective-permute-start.9) | collective-permute-done | bytes 557088 | tf_op jit(solution)/shard_map/ppermute | solution.py:916
  137.5 16.7 %ffn_chunk.5 = (bf16[2,8,1024,128]{3,2,1,0:T(8,128)(2,1)}, bf16[2,8,1024,128]{3,2,1,0:T(8,128)(2,1)}, bf16[2,8,1024,128]{3,2,1,0:T(8,128)(2,1)}, bf16[2,8,1024,1...) custom-call(s32[3]{0:T(128)} %pad_add_fusion.refs_0_, ...), custom_call_target="tpu_custom_call", output_to_operand_aliasing={{0}: (11, {}), {1}: (12, {}), {2}: (13, {}), {3}: (14, {}),... | custom-call | flops 1 | bytes 1 | tf_op jit(solution)/shard_map/ffn_chunk/pallas_call | solution.py:53
  155.7 3.5 second_stage.5
  167.9 27.6 %backward.1 = (bf16[3,1024,1024]{2,1,0:T(8,128)(2,1)}, f32[3,1024,512]{2,1,0:T(8,128)}, f32[3,1,1024]{2,1,0:T(1,128)}, f32[1,1024]{1,0:T(1,128)}) custom-call(s32[3]{0:T(128)} %pad_add_fusion.refs_0_, bf16[1024,1024]{1,0:T(8,128)(2,1)} %get-tuple-element.148.refs_3_.refs_1_, bf16[1024,1024]{1,0:T(8,128)(2,1)} %get-tuple-element.149.refs_4_.refs_2_, ...), custom_call_target="tpu_custom_call" | custom-call | flops 1 | bytes 1 | tf_op jit(solution)/shard_map/backward/pallas_call | solution.py:53
  195.6 4.8 %finish.4 = (f32[2,512,128]{2,1,0:T(8,128)}, f32[2,512,128]{2,1,0:T(8,128)}) custom-call(s32[3]{0:T(128)} %pad_add_fusion.refs_0_, f32[2,4,2,128,128]{4,3,2,1,0:T(8,128)} %get-tuple-element.170.refs_0_.refs_1_, f32[2,4,2,128,128]{4,3,2,1,0:T(8,128)} %collective-permute-done.6.refs_1_.refs_2_, f32[2,4,5,128,128]{4,3,2,1,0:T(8,128)} %copy-done, ...), custom_call_target="tpu_custom_call" | custom-call | flops 99999997952 | bytes 1 | tf_op jit(solution)/shard_map/finish/pallas_call | solution.py:53
  203.3 2.9 second_stage.6
  212.9 13.8 %qkv_grad.1 = (f32[2,4,3,128,128]{4,3,2,1,0:T(8,128)}, f32[2,4,3,128,128]{4,3,2,1,0:T(8,128)}, f32[2,4,3,128,128]{4,3,2,1,0:T(8,128)}, f32[2,4,3,128,128]{4,3,2,1,0:T(8,128)}) custom-call(s32[3]{0:T(128)} %pad_add_fusion.refs_0_, bf16[1024,1024]{1,0:T(8,128)(2,1)} %get-tuple-element.147.refs_1_, bf16[1024,1024]{1,0:T(8,128)(2,1)} %get-tuple-element.157.refs_2_, ...), custom_call_target="tpu_custom_call" | custom-call | flops 1 | bytes 1 | tf_op jit(solution)/shard_map/qkv_grad/pallas_call | solution.py:53
  226.8 4.8 %finish.5 = (f32[2,1024,128]{2,1,0:T(8,128)}, f32[2,1024,128]{2,1,0:T(8,128)}) custom-call(s32[3]{0:T(128)} %pad_add_fusion.refs_0_, f32[2,4,4,128,128]{4,3,2,1,0:T(8,128)} %get-tuple-element.191.refs_0_.refs_1_, f32[2,4,5,128,128]{4,3,2,1,0:T(8,128)} %collective-permute-done.13.refs_1_.refs_6_.refs_2_, f32[4,4,128,128]{3,2,1,0:T(8,128)} %collective-permute-done.16.refs_3_, ...), custom_call_target="tpu_custom_call" | custom-call | flops 1 | bytes 1 | tf_op jit(solution)/shard_map/finish/pallas_call | solution.py:53
  234.4 19.9 %hidden_rows.2 = (f32[2,1024,1024]{2,1,0:T(8,128)}, f32[1024,1024]{1,0:T(8,128)}, f32[8,1024]{1,0:T(8,128)}) custom-call(s32[3]{0:T(128)} %pad_add_fusion.refs_0_, bf16[2,8,1024,128]{3,2,1,0:T(8,128)(2,1)} %get-tuple-element.230.refs_1_, bf16[2,8,1024,128]{3,2,1,0:T(8,128)(2,1)} %get-tuple-element.231.refs_2_, bf16[1024,4096]{1,0:T(8,128)(2,1)} %refs_6_.8, ...), custom_call_target="tpu_custom_call" | custom-call | flops 1 | bytes 1 | tf_op jit(solution)/shard_map/hidden_rows/pallas_call | solution.py:53
  258.5 4.0 %finish.6 = (f32[2,768,128]{2,1,0:T(8,128)}, f32[2,768,128]{2,1,0:T(8,128)}) custom-call(s32[3]{0:T(128)} %pad_add_fusion.refs_0_, f32[2,4,3,128,128]{4,3,2,1,0:T(8,128)} %get-tuple-element.212.refs_0_.refs_1_, f32[2,4,3,128,128]{4,3,2,1,0:T(8,128)} %copy-done.2, f32[4,3,128,128]{3,2,1,0:T(8,128)} %collective-permute-done.24.refs_3_, ...), custom_call_target="tpu_custom_call" | custom-call | flops 1 | bytes 1 | tf_op jit(solution)/shard_map/finish/pallas_call | solution.py:53
  263.2 16.1 %hidden_rows.3 = (f32[2,1024,1024]{2,1,0:T(8,128)}, f32[1024,1024]{1,0:T(8,128)}) custom-call(s32[3]{0:T(128)} %pad_add_fusion.refs_0_, bf16[2,8,1024,128]{3,2,1,0:T(8,128)(2,1)} %get-tuple-element.228.refs_1_, bf16[2,8,1024,128]{3,2,1,0:T(8,128)(2,1)} %get-tuple-element.229.refs_2_, bf16[4096,1024]{1,0:T(8,128)(2,1)} %refs_6_.9, ...), custom_call_target="tpu_custom_call", output_to_operand_aliasing={{0}: (7, {})} | custom-call | flops 99999997952 | bytes 1 | tf_op jit(solution)/shard_map/hidden_rows/pallas_call | solution.py:53
  289.0 2.8 second_stage.7
  294.7 14.3 %first_norm.1 = (f32[1024,1024]{1,0:T(8,128)}, f32[8,1024]{1,0:T(8,128)}) custom-call(bf16[1024,1024]{1,0:T(8,128)(2,1)} %bitcast.120, bf16[1024,1024]{1,0:T(8,128)(2,1)} %bitcast.117, bf16[3,1024,1024]{2,1,0:T(8,128)(2,1)} %get-tuple-element.206.refs_3_.refs_4_.refs_5_.refs_2_, bf16[1024,3072]{1,0:T(8,128)(2,1)} %refs_3_.7, f32[1,1024]{1,0:T(1,128)} %bitcast.159, ...), custom_call_target="tpu_custom_call" | custom-call | flops 99999997952 | bytes 1 | tf_op jit(solution)/shard_map/first_norm/pallas_call | solution.py:53
  313.2 4.5 %finish.7 = (f32[800,128]{1,0:T(8,128)}, f32[800,128]{1,0:T(8,128)}, f32[800,128]{1,0:T(8,128)}, f32[800,128]{1,0:T(8,128)}) custom-call(s32[3]{0:T(128)} %pad_add_fusion.refs_0_, f32[2,4,3,128,128]{4,3,2,1,0:T(8,128)} %get-tuple-element.243.refs_0_.refs_1_, f32[2,4,3,128,128]{4,3,2,1,0:T(8,128)} %copy-done.4, f32[4,3,128,128]{3,2,1,0:T(8,128)} %copy-done.23, ...), custom_call_target="tpu_custom_call" | custom-call | flops 1 | bytes 1 | tf_op jit(solution)/shard_map/finish/pallas_call | solution.py:53
  322.7 13.8 %ends.1 = (bf16[1024,1024]{1,0:T(8,128)(2,1)}, f32[1024,1024]{1,0:T(8,128)}) custom-call(bf16[1024,1024]{1,0:T(8,128)(2,1)} %bitcast.121, bf16[1024,1024]{1,0:T(8,128)(2,1)} %get-tuple-element.179.refs_2_.refs_1_, f32[1024,1024]{1,0:T(8,128)} %get-tuple-element.251.refs_2_, f32[1024,1024]{1,0:T(8,128)} %get-tuple-element.238.refs_3_, ...), custom_call_target="tpu_custom_call" | custom-call | flops 99999997952 | bytes 1 | tf_op jit(solution)/shard_map/ends/pallas_call | solution.py:53
  345.6 4.5 %collective-permute-done.32 = f32[800,128]{1,0:T(8,128)} collective-permute-done((f32[800,128]{1,0:T(8,128)}, f32[800,128]{1,0:T(8,128)}, u32[]{:S(2)}, u32[]{:S(2)}) %collective-permute-start.32) | collective-permute-done | bytes 409632 | tf_op jit(solution)/shard_map/ppermute | solution.py:916
  350.1 10.7 %collective-permute-done.35 = f32[800,128]{1,0:T(8,128)} collective-permute-done((f32[800,128]{1,0:T(8,128)}, f32[800,128]{1,0:T(8,128)}, u32[]{:S(2)}, u32[]{:S(2)}) %collective-permute-start.35) | collective-permute-done | bytes 409632 | tf_op jit(solution)/shard_map/ppermute | solution.py:916
  (251 shorter events, 104.6 us)
Async XLA Ops:
  8.2 23.2 %collective-permute-start.1 = (f32[1024,1024]{1,0:T(8,128)}, f32[1024,1024]{1,0:T(8,128)}, u32[]{:S(2)}, u32[]{:S(2)}) collective-permute-start(f32[1024,1024]{1,0:T(8,128)} %get-tuple-element.153), channel_id=1, source_target_pairs={{0,1},{1,0},{2,3},{3,2},{4,5},{5,4},{6,7},{7,6},{8,9},{9,8},{10,11... | collective-permute-start | bytes 12582920 | tf_op jit(solution)/shard_map/ppermute | solution.py:916
  58.2 30.6 %collective-permute-start.4 = (f32[2,4,136,128]{3,2,1,0:T(8,128)S(1)}, f32[2,4,136,128]{3,2,1,0:T(8,128)}, u32[]{:S(2)}, u32[]{:S(2)}) collective-permute-start(f32[2,4,136,128]{3,2,1,0:T(8,128)S(1)} %select_add_fusion.7.refs_15_), channel_id=1, source_target_pairs={{0,4},{1,5},{2,6},{3,7},{4,0},{5,1},{6,2},{7,3},{8,12},{9,13},{10,... | collective-permute-start | bytes 1671176 | tf_op jit(solution)/shard_map/ppermute | solution.py:916
  58.7 32.4 %collective-permute-start.7 = (f32[2,4,2,128,128]{4,3,2,1,0:T(8,128)}, f32[2,4,2,128,128]{4,3,2,1,0:T(8,128)S(1)}, u32[]{:S(2)}, u32[]{:S(2)}) collective-permute-start(f32[2,4,2,128,128]{4,3,2,1,0:T(8,128)} %get-tuple-element.174), channel_id=1, source_target_pairs={{0,16},{1,17},{2,18},{3,19},{4,20},{5,21},{6,22},{7,23},{8,24},{9,... | collective-permute-start | bytes 3145736 | tf_op jit(solution)/shard_map/ppermute | solution.py:916
  60.2 30.9 %collective-permute-start.6 = (f32[2,4,2,128,128]{4,3,2,1,0:T(8,128)}, f32[2,4,2,128,128]{4,3,2,1,0:T(8,128)}, u32[]{:S(2)}, u32[]{:S(2)}) collective-permute-start(f32[2,4,2,128,128]{4,3,2,1,0:T(8,128)} %get-tuple-element.171), channel_id=1, source_target_pairs={{0,8},{1,9},{2,10},{3,11},{4,12},{5,13},{6,14},{7,15},{8,0},{9,1},... | collective-permute-start | bytes 3145736 | tf_op jit(solution)/shard_map/ppermute | solution.py:916
  94.4 59.8 %collective-permute-start.14 = (f32[2,4,5,128,128]{4,3,2,1,0:T(8,128)}, f32[2,4,5,128,128]{4,3,2,1,0:T(8,128)S(1)}, u32[]{:S(2)}, u32[]{:S(2)}) collective-permute-start(f32[2,4,5,128,128]{4,3,2,1,0:T(8,128)} %get-tuple-element.202), channel_id=1, source_target_pairs={{0,16},{1,17},{2,18},{3,19},{4,20},{5,21},{6,22},{7,23},{8,24},{9,... | collective-permute-start | bytes 7864328 | tf_op jit(solution)/shard_map/ppermute | solution.py:916
  94.9 59.3 %collective-permute-start.13 = (f32[2,4,5,128,128]{4,3,2,1,0:T(8,128)}, f32[2,4,5,128,128]{4,3,2,1,0:T(8,128)}, u32[]{:S(2)}, u32[]{:S(2)}) collective-permute-start(f32[2,4,5,128,128]{4,3,2,1,0:T(8,128)} %get-tuple-element.178.refs_8_), channel_id=1, source_target_pairs={{0,8},{1,9},{2,10},{3,11},{4,12},{5,13},{6,14},{7,15},{8,0},{9,1},... | collective-permute-start | bytes 7864328 | tf_op jit(solution)/shard_map/ppermute | solution.py:916
  135.9 25.1 %collective-permute-start.12 = (f32[2,4,136,128]{3,2,1,0:T(8,128)}, f32[2,4,136,128]{3,2,1,0:T(8,128)}, u32[]{:S(2)}, u32[]{:S(2)}) collective-permute-start(f32[2,4,136,128]{3,2,1,0:T(8,128)} %select_add_fusion.6.refs_19_), channel_id=1, source_target_pairs={{0,4},{1,5},{2,6},{3,7},{4,0},{5,1},{6,2},{7,3},{8,12},{9,13},{10,... | collective-permute-start | bytes 1671176 | tf_op jit(solution)/shard_map/ppermute | solution.py:916
  163.1 37.4 %collective-permute-start.19 = (f32[2,4,3,128,128]{4,3,2,1,0:T(8,128)}, f32[2,4,3,128,128]{4,3,2,1,0:T(8,128)S(1)}, u32[]{:S(2)}, u32[]{:S(2)}) collective-permute-start(f32[2,4,3,128,128]{4,3,2,1,0:T(8,128)} %get-tuple-element.216), channel_id=1, source_target_pairs={{0,16},{1,17},{2,18},{3,19},{4,20},{5,21},{6,22},{7,23},{8,24},{9,... | collective-permute-start | bytes 4718600 | tf_op jit(solution)/shard_map/ppermute | solution.py:916
  164.6 37.4 %collective-permute-start.18 = (f32[2,4,3,128,128]{4,3,2,1,0:T(8,128)}, f32[2,4,3,128,128]{4,3,2,1,0:T(8,128)S(1)}, u32[]{:S(2)}, u32[]{:S(2)}) collective-permute-start(f32[2,4,3,128,128]{4,3,2,1,0:T(8,128)} %get-tuple-element.213), channel_id=1, source_target_pairs={{0,8},{1,9},{2,10},{3,11},{4,12},{5,13},{6,14},{7,15},{8,0},{9,1},... | collective-permute-start | bytes 4718600 | tf_op jit(solution)/shard_map/ppermute | solution.py:916
  166.1 60.6 %collective-permute-start.20 = (f32[4,4,128,128]{3,2,1,0:T(8,128)}, f32[4,4,128,128]{3,2,1,0:T(8,128)}, u32[]{:S(2)}, u32[]{:S(2)}) collective-permute-start(f32[4,4,128,128]{3,2,1,0:T(8,128)} %get-tuple-element.204.refs_15_), channel_id=1, source_target_pairs={{0,8},{1,9},{2,10},{3,11},{4,12},{5,13},{6,14},{7,15},{8,0},{9,1},... | collective-permute-start | bytes 3145736 | tf_op jit(solution)/shard_map/ppermute | solution.py:916
  166.6 60.1 %collective-permute-start.16 = (f32[4,4,128,128]{3,2,1,0:T(8,128)}, f32[4,4,128,128]{3,2,1,0:T(8,128)}, u32[]{:S(2)}, u32[]{:S(2)}) collective-permute-start(f32[4,4,128,128]{3,2,1,0:T(8,128)} %get-tuple-element.207), channel_id=1, source_target_pairs={{0,16},{1,17},{2,18},{3,19},{4,20},{5,21},{6,22},{7,23},{8,24},{9,... | collective-permute-start | bytes 3145736 | tf_op jit(solution)/shard_map/ppermute | solution.py:916
  206.2 48.1 %collective-permute-start.25 = (f32[4,3,128,128]{3,2,1,0:T(8,128)}, f32[4,3,128,128]{3,2,1,0:T(8,128)}, u32[]{:S(2)}, u32[]{:S(2)}) collective-permute-start(f32[4,3,128,128]{3,2,1,0:T(8,128)} %get-tuple-element.218.refs_10_), channel_id=1, source_target_pairs={{0,8},{1,9},{2,10},{3,11},{4,12},{5,13},{6,14},{7,15},{8,0},{9,1},... | collective-permute-start | bytes 2359304 | tf_op jit(solution)/shard_map/ppermute | solution.py:916
  207.6 46.6 %collective-permute-start.24 = (f32[4,3,128,128]{3,2,1,0:T(8,128)}, f32[4,3,128,128]{3,2,1,0:T(8,128)}, u32[]{:S(2)}, u32[]{:S(2)}) collective-permute-start(f32[4,3,128,128]{3,2,1,0:T(8,128)} %get-tuple-element.234), channel_id=1, source_target_pairs={{0,16},{1,17},{2,18},{3,19},{4,20},{5,21},{6,22},{7,23},{8,24},{9,... | collective-permute-start | bytes 2359304 | tf_op jit(solution)/shard_map/ppermute | solution.py:916
  208.2 25.4 %collective-permute-start.22 = (f32[2,512,128]{2,1,0:T(8,128)}, f32[2,512,128]{2,1,0:T(8,128)S(1)}, u32[]{:S(2)}, u32[]{:S(2)}) collective-permute-start(f32[2,512,128]{2,1,0:T(8,128)} %get-tuple-element.226), channel_id=1, source_target_pairs={{0,2},{1,3},{2,0},{3,1},{4,6},{5,7},{6,4},{7,5},{8,10},{9,11},{10,... | collective-permute-start | bytes 1572872 | tf_op jit(solution)/shard_map/ppermute | solution.py:916
  231.5 55.9 %collective-permute-start.28 = (f32[2,4,3,128,128]{4,3,2,1,0:T(8,128)}, f32[2,4,3,128,128]{4,3,2,1,0:T(8,128)S(1)}, u32[]{:S(2)}, u32[]{:S(2)}) collective-permute-start(f32[2,4,3,128,128]{4,3,2,1,0:T(8,128)} %get-tuple-element.248), channel_id=1, source_target_pairs={{0,16},{1,17},{2,18},{3,19},{4,20},{5,21},{6,22},{7,23},{8,24},{9,... | collective-permute-start | bytes 4718600 | tf_op jit(solution)/shard_map/ppermute | solution.py:916
  233.0 54.3 %collective-permute-start.27 = (f32[2,4,3,128,128]{4,3,2,1,0:T(8,128)}, f32[2,4,3,128,128]{4,3,2,1,0:T(8,128)S(1)}, u32[]{:S(2)}, u32[]{:S(2)}) collective-permute-start(f32[2,4,3,128,128]{4,3,2,1,0:T(8,128)} %get-tuple-element.244), channel_id=1, source_target_pairs={{0,8},{1,9},{2,10},{3,11},{4,12},{5,13},{6,14},{7,15},{8,0},{9,1},... | collective-permute-start | bytes 4718600 | tf_op jit(solution)/shard_map/ppermute | solution.py:916
  233.6 46.6 %collective-permute-start.21 = (f32[2,1024,128]{2,1,0:T(8,128)}, f32[2,1024,128]{2,1,0:T(8,128)}, u32[]{:S(2)}, u32[]{:S(2)}) collective-permute-start(f32[2,1024,128]{2,1,0:T(8,128)} %get-tuple-element.224), channel_id=1, source_target_pairs={{0,2},{1,3},{2,0},{3,1},{4,6},{5,7},{6,4},{7,5},{8,10},{9,11},{10,... | collective-permute-start | bytes 3145736 | tf_op jit(solution)/shard_map/ppermute | solution.py:916
  255.9 24.2 %collective-permute-start.23 = (f32[512,128]{1,0:T(8,128)}, f32[512,128]{1,0:T(8,128)}, u32[]{:S(2)}, u32[]{:S(2)}) collective-permute-start(f32[512,128]{1,0:T(8,128)} %add_bitcast_fusion.2.refs_10_), channel_id=1, source_target_pairs={{0,4},{1,5},{2,6},{3,7},{4,0},{5,1},{6,2},{7,3},{8,12},{9,13},{10,... | collective-permute-start | bytes 786440 | tf_op jit(solution)/shard_map/ppermute | solution.py:916
  280.1 42.6 %collective-permute-start.29 = (f32[2,1024,1024]{2,1,0:T(8,128)}, f32[2,1024,1024]{2,1,0:T(8,128)}, u32[]{:S(2)}, u32[]{:S(2)}) collective-permute-start(f32[2,1024,1024]{2,1,0:T(8,128)} %get-tuple-element.252), channel_id=1, source_target_pairs={{0,1},{1,0},{2,3},{3,2},{4,5},{5,4},{6,7},{7,6},{8,9},{9,8},{10,11... | collective-permute-start | bytes 25165832 | tf_op jit(solution)/shard_map/ppermute | solution.py:916
  282.3 35.4 %collective-permute-start.34 = (f32[1024,128]{1,0:T(8,128)}, f32[1024,128]{1,0:T(8,128)}, u32[]{:S(2)}, u32[]{:S(2)}) collective-permute-start(f32[1024,128]{1,0:T(8,128)} %add_bitcast_fusion.refs_5_), channel_id=1, source_target_pairs={{0,4},{1,5},{2,6},{3,7},{4,0},{5,1},{6,2},{7,3},{8,12},{9,13},{10,... | collective-permute-start | bytes 1572872 | tf_op jit(solution)/shard_map/ppermute | solution.py:916
  284.9 56.9 %collective-permute-start.33 = (f32[768,128]{1,0:T(8,128)}, f32[768,128]{1,0:T(8,128)}, u32[]{:S(2)}, u32[]{:S(2)}) collective-permute-start(f32[768,128]{1,0:T(8,128)} %add_bitcast_fusion.1.refs_6_), channel_id=1, source_target_pairs={{0,4},{1,5},{2,6},{3,7},{4,0},{5,1},{6,2},{7,3},{8,12},{9,13},{10,... | collective-permute-start | bytes 1179656 | tf_op jit(solution)/shard_map/ppermute | solution.py:916
  317.7 32.4 %collective-permute-start.32 = (f32[800,128]{1,0:T(8,128)}, f32[800,128]{1,0:T(8,128)}, u32[]{:S(2)}, u32[]{:S(2)}) collective-permute-start(f32[800,128]{1,0:T(8,128)} %get-tuple-element.264), channel_id=1, source_target_pairs={{0,4},{1,5},{2,6},{3,7},{4,0},{5,1},{6,2},{7,3},{8,12},{9,13},{10,... | collective-permute-start | bytes 1228808 | tf_op jit(solution)/shard_map/ppermute | solution.py:916
  318.6 42.2 %collective-permute-start.35 = (f32[800,128]{1,0:T(8,128)}, f32[800,128]{1,0:T(8,128)}, u32[]{:S(2)}, u32[]{:S(2)}) collective-permute-start(f32[800,128]{1,0:T(8,128)} %get-tuple-element.272), channel_id=1, source_target_pairs={{0,2},{1,3},{2,4},{3,5},{4,6},{5,7},{6,0},{7,1},{8,10},{9,11},{10,... | collective-permute-start | bytes 1228808 | tf_op jit(solution)/shard_map/ppermute | solution.py:916
  319.4 44.0 %collective-permute-start.36 = (f32[800,128]{1,0:T(8,128)}, f32[800,128]{1,0:T(8,128)}, u32[]{:S(2)}, u32[]{:S(2)}) collective-permute-start(f32[800,128]{1,0:T(8,128)} %get-tuple-element.274), channel_id=1, source_target_pairs={{0,6},{1,7},{2,0},{3,1},{4,2},{5,3},{6,4},{7,5},{8,14},{9,15},{10,... | collective-permute-start | bytes 1228808 | tf_op jit(solution)/shard_map/ppermute | solution.py:916
  (67 other events, 610.2 us)

commit v5 on v4

--- a/solution.py
+++ b/solution.py
@@ -390,6 +390,12 @@
     return jnp.sum(jnp.where(eye, jnp.broadcast_to(row, (128, 128)), 0.0), axis=1, keepdims=True)
 
 
+def column_of(row):
+    n = row.shape[1]
+    eye = iota((n, n), 0) == iota((n, n), 1)
+    return jnp.sum(jnp.where(eye, jnp.broadcast_to(row, (n, n)), 0.0), axis=1, keepdims=True)
+
+
 def each_head(x):
     mask = iota((1, 128), 1) < 64
     zero = jnp.zeros_like(x)
@@ -414,7 +420,7 @@
     k = [three(part, *halves) for part in k]
     for i in range(count):
         qf_o[rows(i)] = (weight * jnp.exp(q[i])).astype(bf16)
-        kf = (weight * jnp.exp(k[i])).astype(bf16) * valid[rows(i)].astype(bf16)
+        kf = (weight * jnp.exp(k[i])).astype(bf16) * column_of(valid[i : i + 1]).astype(bf16)
         kf_o[rows(i)] = kf
         k[i] = kf
         v_o[rows(i)] = v[i]
@@ -638,7 +644,7 @@
         grid=s["grid"],
         in_specs=[s["wide"], *weights, *biases, s["row"]]
         + [s["table"]] * 4
-        + [pl.BlockSpec((LEN_BLK * per, 1), lambda h, g, *_: (g, 0))],
+        + [pl.BlockSpec((per, LEN_BLK), lambda h, g, *_: (g, 0))],
         out_specs=[s["head"]] * 3 + [s["state"]] * 2,
         out_shape=[struct((rows, 1024), bf16)] * 3
         + [struct((seqs // 2, 4, 136, 128), f32)] * 2,
@@ -1172,7 +1178,7 @@
     pos = jnp.stack([me, core, lax.div(place, 2)]).astype(jnp.int32)
     places = place * block + jnp.arange(block, dtype=jnp.int32)
     valid = (places[None, :] < lengths[:, None]) & ((key_mask == 1) | (places[None, :] == 0))
-    valid = valid.astype(f32).reshape(rows, 1)
+    valid = valid.astype(f32)
     x = hidden_in.reshape(rows, width)
     g = cotangent.reshape(rows, width)
     row = lambda v: v.reshape(1, -1)
@@ -1274,9 +1280,10 @@
     held = [own_r[1]]
     if tuned:
         early.landed(own_r[1])
-        held = [later.stage_two(early.two), middle.stage_two(early.two)]
-        g3.arrived(own_r[1])
+        held = [later.stage_two(early.two)]
+        g3.arrived(*held)
         held.append(g3.second())
+        held.append(middle.stage_two(*held))
     partial, sums1 = first_norm(x, g, grad_proj, w_qkv, row(ln1_gain), after=held)
     half_up = jnp.concatenate([c[8].reshape(-1, 2, 2, 128) for c in (c0, c1, c2)], 0)
     half_up = half_up.transpose(1, 2, 0, 3).reshape(4, 1, 512)

time: 384 us -> 382 us (level)
    unnamed x109 -> x111, local copies, waits for them, and re-layouts: 12 us -> 10.2 us
  transfers between devices with their start and end apart: 42 -> 42, of which waited for: 12 -> 11; matrix products, arithmetic and copies ran while one was open for 8% -> 8% of each run, Pallas kernels for 67% -> 67%
where the time goes in v5:
time: 382 us; the launch traced here: 375 us
  Pallas kernels  260 us (68%)
  starting transfers between devices  37.5 us (10%)
  waiting for transfers between devices  30.7 us (8%)
  other arithmetic  26.9 us (7%)
  local copies, waits for them, and re-layouts  18.1 us (5%)
    pallas_call x26, Pallas kernels, ordered_call(): pl.pallas_call(body, grid_spec=pltpu.PrefetchScalarGridSpec(num_scalar_pr...  260 us
    ppermute x42, starting transfers between devices, send(): return lax.ppermute(value, ('batch', 'seq'), pairs)  37.5 us
    ppermute x42, waiting for transfers between devices, send(): return lax.ppermute(value, ('batch', 'seq'), pairs)  30.7 us
    unnamed x111, local copies, waits for them, and re-layouts  10.2 us
  transfers between devices with their start and end apart: 42, of which 11 were waited for; matrix products, arithmetic and copies ran while one was open for 8% of the time, Pallas kernels for 67%

profile of v5, /device:TPU:16, one launch (start us, length us, event | category | flops | bytes accessed | tf_op | source)
XLA Modules:
  0.0 375.4 jit_solution(8109690261808969444)
XLA Ops:
  0.7 7.5 %norms.2 = (bf16[1024,1024]{1,0:T(8,128)(2,1)}, bf16[1024,1024]{1,0:T(8,128)(2,1)}, f32[1024,1024]{1,0:T(8,128)}, f32[1024,1024]{1,0:T(8,128)}) custom-call(bf16[1024,1024]{1,0:T(8,128)(2,1)} %bitcast.113, bf16[1024,1024]{1,0:T(8,128)(2,1)} %bitcast.106, f32[1,1024]{1,0:T(1,128)} %bitcast.150, f32[1,1024]{1,0:T(1,128)} %bitcast.146, f32[1,1024]{1,0:T(1,128)} %bitcast.153, ...), custom_call_target="tpu_custom_call" | custom-call | flops 1 | bytes 1 | tf_op jit(solution)/shard_map/norms/pallas_call | solution.py:53
  13.0 17.6 %features.1 = (bf16[1024,1024]{1,0:T(8,128)(2,1)}, bf16[1024,1024]{1,0:T(8,128)(2,1)}, bf16[1024,1024]{1,0:T(8,128)(2,1)}, f32[2,4,136,128]{3,2,1,0:T(8,128)}, f32[2,4,136,128]{3,2,1,0:T(8,128)}) custom-call(s32[3]{0:T(128)} %pad_add_fusion.refs_0_, bf16[1024,1024]{1,0:T(8,128)(2,1)} %get-tuple-element.147.refs_1_, bf16[1024,3072]{1,0:T(8,128)(2,1)} %refs_3_.7, ...), custom_call_target="tpu_custom_call" | custom-call | flops 1 | bytes 1 | tf_op jit(solution)/shard_map/features/pallas_call | solution.py:53
  30.8 7.1 %norms.3 = (bf16[1024,1024]{1,0:T(8,128)(2,1)}, bf16[1024,1024]{1,0:T(8,128)(2,1)}, bf16[1024,1024]{1,0:T(8,128)(2,1)}) custom-call(f32[1024,1024]{1,0:T(8,128)} %collective-permute-done.1.refs_0_.refs_8_, f32[1024,1024]{1,0:T(8,128)} %collective-permute-done.2.refs_1_, f32[1,1024]{1,0:T(1,128)} %bitcast.151, f32[1,1024]{1,0:T(1,128)} %bitcast.147, ...), custom_call_target="tpu_custom_call" | custom-call | flops 1 | bytes 1 | tf_op jit(solution)/shard_map/norms/pallas_call | solution.py:53
  39.8 16.7 %ffn_chunk.3 = (bf16[2,8,1024,128]{3,2,1,0:T(8,128)(2,1)}, bf16[2,8,1024,128]{3,2,1,0:T(8,128)(2,1)}, bf16[2,8,1024,128]{3,2,1,0:T(8,128)(2,1)}, bf16[2,8,1024,1...) custom-call(s32[3]{0:T(128)} %pad_add_fusion.refs_0_, ...), custom_call_target="tpu_custom_call" | custom-call | flops 1 | bytes 1 | tf_op jit(solution)/shard_map/ffn_chunk/pallas_call | solution.py:53
  61.0 27.1 %ffn_chunk.4 = (bf16[2,8,1024,128]{3,2,1,0:T(8,128)(2,1)}, bf16[2,8,1024,128]{3,2,1,0:T(8,128)(2,1)}, bf16[2,8,1024,128]{3,2,1,0:T(8,128)(2,1)}, bf16[2,8,1024,1...) custom-call(s32[3]{0:T(128)} %pad_add_fusion.refs_0_, ...), custom_call_target="tpu_custom_call", output_to_operand_aliasing={{0}: (11, {}), {1}: (12, {}), {2}: (13, {}), {3}: (14, {})} | custom-call | flops 1 | bytes 1 | tf_op jit(solution)/shard_map/ffn_chunk/pallas_call | solution.py:53
  95.5 16.3 %mixing.1 = (bf16[1024,1024]{1,0:T(8,128)(2,1)}, bf16[1024,1024]{1,0:T(8,128)(2,1)}, f32[4,1024,128]{2,1,0:T(8,128)}, f32[2,4,136,128]{3,2,1,0:T(8,128)}, f32[2,...) custom-call(s32[3]{0:T(128)} %pad_add_fusion.refs_0_, bf16[1024,1024]{1,0:T(8,128)(2,1)} %bitcast.109, ...), custom_call_target="tpu_custom_call" | custom-call | flops 1 | bytes 1 | tf_op jit(solution)/shard_map/mixing/pallas_call | solution.py:53
  119.1 8.2 %out_grad.1 = (f32[2,4,3,128,128]{4,3,2,1,0:T(8,128)}, f32[2,4,3,128,128]{4,3,2,1,0:T(8,128)}, f32[2,4,3,128,128]{4,3,2,1,0:T(8,128)}, f32[2,4,3,128,128]{4,3,2,1,0:T(8,128)}) custom-call(s32[3]{0:T(128)} %pad_add_fusion.refs_0_, bf16[1024,1024]{1,0:T(8,128)(2,1)} %get-tuple-element.179.refs_2_.refs_1_, f32[1024,256]{1,0:T(8,128)} %collective-permute-done.10.refs_2_, ...), custom_call_target="tpu_custom_call" | custom-call | flops 1 | bytes 1 | tf_op jit(solution)/shard_map/out_grad/pallas_call | solution.py:53
  127.3 5.8 %collective-permute-done.9 = f32[2,4,136,128]{3,2,1,0:T(8,128)} collective-permute-done((f32[2,4,136,128]{3,2,1,0:T(8,128)S(1)}, f32[2,4,136,128]{3,2,1,0:T(8,128)}, u32[]{:S(2)}, u32[]{:S(2)}) %collective-permute-start.9) | collective-permute-done | bytes 557088 | tf_op jit(solution)/shard_map/ppermute | solution.py:922
  136.8 16.7 %ffn_chunk.5 = (bf16[2,8,1024,128]{3,2,1,0:T(8,128)(2,1)}, bf16[2,8,1024,128]{3,2,1,0:T(8,128)(2,1)}, bf16[2,8,1024,128]{3,2,1,0:T(8,128)(2,1)}, bf16[2,8,1024,1...) custom-call(s32[3]{0:T(128)} %pad_add_fusion.refs_0_, ...), custom_call_target="tpu_custom_call", output_to_operand_aliasing={{0}: (11, {}), {1}: (12, {}), {2}: (13, {}), {3}: (14, {}),... | custom-call | flops 1 | bytes 1 | tf_op jit(solution)/shard_map/ffn_chunk/pallas_call | solution.py:53
  155.0 3.5 second_stage.5
  167.2 27.6 %backward.1 = (bf16[3,1024,1024]{2,1,0:T(8,128)(2,1)}, f32[3,1024,512]{2,1,0:T(8,128)}, f32[3,1,1024]{2,1,0:T(1,128)}, f32[1,1024]{1,0:T(1,128)}) custom-call(s32[3]{0:T(128)} %pad_add_fusion.refs_0_, bf16[1024,1024]{1,0:T(8,128)(2,1)} %get-tuple-element.148.refs_3_.refs_1_, bf16[1024,1024]{1,0:T(8,128)(2,1)} %get-tuple-element.149.refs_4_.refs_2_, ...), custom_call_target="tpu_custom_call" | custom-call | flops 1 | bytes 1 | tf_op jit(solution)/shard_map/backward/pallas_call | solution.py:53
  194.9 4.8 %finish.4 = (f32[2,512,128]{2,1,0:T(8,128)}, f32[2,512,128]{2,1,0:T(8,128)}) custom-call(s32[3]{0:T(128)} %pad_add_fusion.refs_0_, f32[2,4,2,128,128]{4,3,2,1,0:T(8,128)} %get-tuple-element.170.refs_0_.refs_1_, f32[2,4,2,128,128]{4,3,2,1,0:T(8,128)} %collective-permute-done.6.refs_1_.refs_2_, f32[2,4,5,128,128]{4,3,2,1,0:T(8,128)} %copy-done, ...), custom_call_target="tpu_custom_call" | custom-call | flops 99999997952 | bytes 1 | tf_op jit(solution)/shard_map/finish/pallas_call | solution.py:53
  202.6 2.9 second_stage.6
  212.3 13.8 %qkv_grad.1 = (f32[2,4,3,128,128]{4,3,2,1,0:T(8,128)}, f32[2,4,3,128,128]{4,3,2,1,0:T(8,128)}, f32[2,4,3,128,128]{4,3,2,1,0:T(8,128)}, f32[2,4,3,128,128]{4,3,2,1,0:T(8,128)}) custom-call(s32[3]{0:T(128)} %pad_add_fusion.refs_0_, bf16[1024,1024]{1,0:T(8,128)(2,1)} %get-tuple-element.147.refs_1_, bf16[1024,1024]{1,0:T(8,128)(2,1)} %get-tuple-element.157.refs_2_, ...), custom_call_target="tpu_custom_call" | custom-call | flops 1 | bytes 1 | tf_op jit(solution)/shard_map/qkv_grad/pallas_call | solution.py:53
  226.1 4.8 %finish.5 = (f32[2,1024,128]{2,1,0:T(8,128)}, f32[2,1024,128]{2,1,0:T(8,128)}) custom-call(s32[3]{0:T(128)} %pad_add_fusion.refs_0_, f32[2,4,4,128,128]{4,3,2,1,0:T(8,128)} %get-tuple-element.191.refs_0_.refs_1_, f32[2,4,5,128,128]{4,3,2,1,0:T(8,128)} %collective-permute-done.13.refs_1_.refs_6_.refs_2_, f32[4,4,128,128]{3,2,1,0:T(8,128)} %collective-permute-done.16.refs_3_, ...), custom_call_target="tpu_custom_call" | custom-call | flops 1 | bytes 1 | tf_op jit(solution)/shard_map/finish/pallas_call | solution.py:53
  232.9 19.9 %hidden_rows.2 = (f32[2,1024,1024]{2,1,0:T(8,128)}, f32[1024,1024]{1,0:T(8,128)}, f32[8,1024]{1,0:T(8,128)}) custom-call(s32[3]{0:T(128)} %pad_add_fusion.refs_0_, bf16[2,8,1024,128]{3,2,1,0:T(8,128)(2,1)} %get-tuple-element.230.refs_1_, bf16[2,8,1024,128]{3,2,1,0:T(8,128)(2,1)} %get-tuple-element.231.refs_2_, bf16[1024,4096]{1,0:T(8,128)(2,1)} %refs_6_.8, ...), custom_call_target="tpu_custom_call" | custom-call | flops 1 | bytes 1 | tf_op jit(solution)/shard_map/hidden_rows/pallas_call | solution.py:53
  253.8 3.3 collective-permute-start.23
  257.2 4.0 %finish.6 = (f32[2,768,128]{2,1,0:T(8,128)}, f32[2,768,128]{2,1,0:T(8,128)}) custom-call(s32[3]{0:T(128)} %pad_add_fusion.refs_0_, f32[2,4,3,128,128]{4,3,2,1,0:T(8,128)} %get-tuple-element.212.refs_0_.refs_1_, f32[2,4,3,128,128]{4,3,2,1,0:T(8,128)} %copy-done.2, f32[4,3,128,128]{3,2,1,0:T(8,128)} %collective-permute-done.24.refs_3_, ...), custom_call_target="tpu_custom_call" | custom-call | flops 1 | bytes 1 | tf_op jit(solution)/shard_map/finish/pallas_call | solution.py:53
  261.2 15.9 %hidden_rows.3 = (f32[2,1024,1024]{2,1,0:T(8,128)}, f32[1024,1024]{1,0:T(8,128)}) custom-call(s32[3]{0:T(128)} %pad_add_fusion.refs_0_, bf16[2,8,1024,128]{3,2,1,0:T(8,128)(2,1)} %get-tuple-element.228.refs_1_, bf16[2,8,1024,128]{3,2,1,0:T(8,128)(2,1)} %get-tuple-element.229.refs_2_, bf16[4096,1024]{1,0:T(8,128)(2,1)} %refs_6_.9, ...), custom_call_target="tpu_custom_call", output_to_operand_aliasing={{0}: (7, {})} | custom-call | flops 99999997952 | bytes 1 | tf_op jit(solution)/shard_map/hidden_rows/pallas_call | solution.py:53
  291.6 14.3 %first_norm.1 = (f32[1024,1024]{1,0:T(8,128)}, f32[8,1024]{1,0:T(8,128)}) custom-call(bf16[1024,1024]{1,0:T(8,128)(2,1)} %bitcast.115, bf16[1024,1024]{1,0:T(8,128)(2,1)} %bitcast.112, bf16[3,1024,1024]{2,1,0:T(8,128)(2,1)} %get-tuple-element.206.refs_3_.refs_4_.refs_5_.refs_2_, bf16[1024,3072]{1,0:T(8,128)(2,1)} %refs_3_.7, f32[1,1024]{1,0:T(1,128)} %bitcast.152, ...), custom_call_target="tpu_custom_call" | custom-call | flops 99999997952 | bytes 1 | tf_op jit(solution)/shard_map/first_norm/pallas_call | solution.py:53
  310.2 4.6 %finish.7 = (f32[800,128]{1,0:T(8,128)}, f32[800,128]{1,0:T(8,128)}, f32[800,128]{1,0:T(8,128)}, f32[800,128]{1,0:T(8,128)}) custom-call(s32[3]{0:T(128)} %pad_add_fusion.refs_0_, f32[2,4,3,128,128]{4,3,2,1,0:T(8,128)} %get-tuple-element.241.refs_0_.refs_1_, f32[2,4,3,128,128]{4,3,2,1,0:T(8,128)} %copy-done.4, f32[4,3,128,128]{3,2,1,0:T(8,128)} %copy-done.21, ...), custom_call_target="tpu_custom_call" | custom-call | flops 1 | bytes 1 | tf_op jit(solution)/shard_map/finish/pallas_call | solution.py:53
  321.3 13.8 %ends.1 = (bf16[1024,1024]{1,0:T(8,128)(2,1)}, f32[1024,1024]{1,0:T(8,128)}) custom-call(bf16[1024,1024]{1,0:T(8,128)(2,1)} %bitcast.116, bf16[1024,1024]{1,0:T(8,128)(2,1)} %get-tuple-element.179.refs_2_.refs_1_, f32[1024,1024]{1,0:T(8,128)} %get-tuple-element.251.refs_2_, f32[1024,1024]{1,0:T(8,128)} %get-tuple-element.238.refs_3_, ...), custom_call_target="tpu_custom_call" | custom-call | flops 99999997952 | bytes 1 | tf_op jit(solution)/shard_map/ends/pallas_call | solution.py:53
  344.1 4.5 %collective-permute-done.32 = f32[800,128]{1,0:T(8,128)} collective-permute-done((f32[800,128]{1,0:T(8,128)}, f32[800,128]{1,0:T(8,128)}, u32[]{:S(2)}, u32[]{:S(2)}) %collective-permute-start.32) | collective-permute-done | bytes 409632 | tf_op jit(solution)/shard_map/ppermute | solution.py:922
  348.6 10.4 %collective-permute-done.35 = f32[800,128]{1,0:T(8,128)} collective-permute-done((f32[800,128]{1,0:T(8,128)}, f32[800,128]{1,0:T(8,128)}, u32[]{:S(2)}, u32[]{:S(2)}) %collective-permute-start.35) | collective-permute-done | bytes 409632 | tf_op jit(solution)/shard_map/ppermute | solution.py:922
  (253 shorter events, 102.9 us)
Async XLA Ops:
  57.6 30.5 %collective-permute-start.4 = (f32[2,4,136,128]{3,2,1,0:T(8,128)S(1)}, f32[2,4,136,128]{3,2,1,0:T(8,128)}, u32[]{:S(2)}, u32[]{:S(2)}) collective-permute-start(f32[2,4,136,128]{3,2,1,0:T(8,128)S(1)} %select_add_fusion.7.refs_15_), channel_id=1, source_target_pairs={{0,4},{1,5},{2,6},{3,7},{4,0},{5,1},{6,2},{7,3},{8,12},{9,13},{10,... | collective-permute-start | bytes 1671176 | tf_op jit(solution)/shard_map/ppermute | solution.py:922
  58.0 32.4 %collective-permute-start.7 = (f32[2,4,2,128,128]{4,3,2,1,0:T(8,128)}, f32[2,4,2,128,128]{4,3,2,1,0:T(8,128)S(1)}, u32[]{:S(2)}, u32[]{:S(2)}) collective-permute-start(f32[2,4,2,128,128]{4,3,2,1,0:T(8,128)} %get-tuple-element.174), channel_id=1, source_target_pairs={{0,16},{1,17},{2,18},{3,19},{4,20},{5,21},{6,22},{7,23},{8,24},{9,... | collective-permute-start | bytes 3145736 | tf_op jit(solution)/shard_map/ppermute | solution.py:922
  59.5 30.8 %collective-permute-start.6 = (f32[2,4,2,128,128]{4,3,2,1,0:T(8,128)}, f32[2,4,2,128,128]{4,3,2,1,0:T(8,128)}, u32[]{:S(2)}, u32[]{:S(2)}) collective-permute-start(f32[2,4,2,128,128]{4,3,2,1,0:T(8,128)} %get-tuple-element.171), channel_id=1, source_target_pairs={{0,8},{1,9},{2,10},{3,11},{4,12},{5,13},{6,14},{7,15},{8,0},{9,1},... | collective-permute-start | bytes 3145736 | tf_op jit(solution)/shard_map/ppermute | solution.py:922
  93.7 59.8 %collective-permute-start.14 = (f32[2,4,5,128,128]{4,3,2,1,0:T(8,128)}, f32[2,4,5,128,128]{4,3,2,1,0:T(8,128)S(1)}, u32[]{:S(2)}, u32[]{:S(2)}) collective-permute-start(f32[2,4,5,128,128]{4,3,2,1,0:T(8,128)} %get-tuple-element.202), channel_id=1, source_target_pairs={{0,16},{1,17},{2,18},{3,19},{4,20},{5,21},{6,22},{7,23},{8,24},{9,... | collective-permute-start | bytes 7864328 | tf_op jit(solution)/shard_map/ppermute | solution.py:922
  94.2 59.3 %collective-permute-start.13 = (f32[2,4,5,128,128]{4,3,2,1,0:T(8,128)}, f32[2,4,5,128,128]{4,3,2,1,0:T(8,128)}, u32[]{:S(2)}, u32[]{:S(2)}) collective-permute-start(f32[2,4,5,128,128]{4,3,2,1,0:T(8,128)} %get-tuple-element.178.refs_8_), channel_id=1, source_target_pairs={{0,8},{1,9},{2,10},{3,11},{4,12},{5,13},{6,14},{7,15},{8,0},{9,1},... | collective-permute-start | bytes 7864328 | tf_op jit(solution)/shard_map/ppermute | solution.py:922
  135.2 25.2 %collective-permute-start.12 = (f32[2,4,136,128]{3,2,1,0:T(8,128)}, f32[2,4,136,128]{3,2,1,0:T(8,128)}, u32[]{:S(2)}, u32[]{:S(2)}) collective-permute-start(f32[2,4,136,128]{3,2,1,0:T(8,128)} %select_add_fusion.6.refs_19_), channel_id=1, source_target_pairs={{0,4},{1,5},{2,6},{3,7},{4,0},{5,1},{6,2},{7,3},{8,12},{9,13},{10,... | collective-permute-start | bytes 1671176 | tf_op jit(solution)/shard_map/ppermute | solution.py:922
  162.4 37.4 %collective-permute-start.19 = (f32[2,4,3,128,128]{4,3,2,1,0:T(8,128)}, f32[2,4,3,128,128]{4,3,2,1,0:T(8,128)S(1)}, u32[]{:S(2)}, u32[]{:S(2)}) collective-permute-start(f32[2,4,3,128,128]{4,3,2,1,0:T(8,128)} %get-tuple-element.216), channel_id=1, source_target_pairs={{0,16},{1,17},{2,18},{3,19},{4,20},{5,21},{6,22},{7,23},{8,24},{9,... | collective-permute-start | bytes 4718600 | tf_op jit(solution)/shard_map/ppermute | solution.py:922
  163.9 37.4 %collective-permute-start.18 = (f32[2,4,3,128,128]{4,3,2,1,0:T(8,128)}, f32[2,4,3,128,128]{4,3,2,1,0:T(8,128)S(1)}, u32[]{:S(2)}, u32[]{:S(2)}) collective-permute-start(f32[2,4,3,128,128]{4,3,2,1,0:T(8,128)} %get-tuple-element.213), channel_id=1, source_target_pairs={{0,8},{1,9},{2,10},{3,11},{4,12},{5,13},{6,14},{7,15},{8,0},{9,1},... | collective-permute-start | bytes 4718600 | tf_op jit(solution)/shard_map/ppermute | solution.py:922
  165.4 60.7 %collective-permute-start.20 = (f32[4,4,128,128]{3,2,1,0:T(8,128)}, f32[4,4,128,128]{3,2,1,0:T(8,128)}, u32[]{:S(2)}, u32[]{:S(2)}) collective-permute-start(f32[4,4,128,128]{3,2,1,0:T(8,128)} %get-tuple-element.204.refs_15_), channel_id=1, source_target_pairs={{0,8},{1,9},{2,10},{3,11},{4,12},{5,13},{6,14},{7,15},{8,0},{9,1},... | collective-permute-start | bytes 3145736 | tf_op jit(solution)/shard_map/ppermute | solution.py:922
  165.9 60.2 %collective-permute-start.16 = (f32[4,4,128,128]{3,2,1,0:T(8,128)}, f32[4,4,128,128]{3,2,1,0:T(8,128)}, u32[]{:S(2)}, u32[]{:S(2)}) collective-permute-start(f32[4,4,128,128]{3,2,1,0:T(8,128)} %get-tuple-element.207), channel_id=1, source_target_pairs={{0,16},{1,17},{2,18},{3,19},{4,20},{5,21},{6,22},{7,23},{8,24},{9,... | collective-permute-start | bytes 3145736 | tf_op jit(solution)/shard_map/ppermute | solution.py:922
  205.5 47.4 %collective-permute-start.25 = (f32[4,3,128,128]{3,2,1,0:T(8,128)}, f32[4,3,128,128]{3,2,1,0:T(8,128)}, u32[]{:S(2)}, u32[]{:S(2)}) collective-permute-start(f32[4,3,128,128]{3,2,1,0:T(8,128)} %get-tuple-element.218.refs_10_), channel_id=1, source_target_pairs={{0,8},{1,9},{2,10},{3,11},{4,12},{5,13},{6,14},{7,15},{8,0},{9,1},... | collective-permute-start | bytes 2359304 | tf_op jit(solution)/shard_map/ppermute | solution.py:922
  206.9 45.9 %collective-permute-start.24 = (f32[4,3,128,128]{3,2,1,0:T(8,128)}, f32[4,3,128,128]{3,2,1,0:T(8,128)}, u32[]{:S(2)}, u32[]{:S(2)}) collective-permute-start(f32[4,3,128,128]{3,2,1,0:T(8,128)} %get-tuple-element.234), channel_id=1, source_target_pairs={{0,16},{1,17},{2,18},{3,19},{4,20},{5,21},{6,22},{7,23},{8,24},{9,... | collective-permute-start | bytes 2359304 | tf_op jit(solution)/shard_map/ppermute | solution.py:922
  207.5 25.0 %collective-permute-start.22 = (f32[2,512,128]{2,1,0:T(8,128)S(1)}, f32[2,512,128]{2,1,0:T(8,128)}, u32[]{:S(2)}, u32[]{:S(2)}) collective-permute-start(f32[2,512,128]{2,1,0:T(8,128)S(1)} %copy-done.49), channel_id=1, source_target_pairs={{0,2},{1,3},{2,0},{3,1},{4,6},{5,7},{6,4},{7,5},{8,10},{9,11},{10,... | collective-permute-start | bytes 1572872 | tf_op jit(solution)/shard_map/ppermute | solution.py:922
  230.9 50.9 %collective-permute-start.27 = (f32[2,4,3,128,128]{4,3,2,1,0:T(8,128)}, f32[2,4,3,128,128]{4,3,2,1,0:T(8,128)S(1)}, u32[]{:S(2)}, u32[]{:S(2)}) collective-permute-start(f32[2,4,3,128,128]{4,3,2,1,0:T(8,128)} %get-tuple-element.246), channel_id=1, source_target_pairs={{0,16},{1,17},{2,18},{3,19},{4,20},{5,21},{6,22},{7,23},{8,24},{9,... | collective-permute-start | bytes 4718600 | tf_op jit(solution)/shard_map/ppermute | solution.py:922
  232.4 45.7 %collective-permute-start.21 = (f32[2,1024,128]{2,1,0:T(8,128)}, f32[2,1024,128]{2,1,0:T(8,128)}, u32[]{:S(2)}, u32[]{:S(2)}) collective-permute-start(f32[2,1024,128]{2,1,0:T(8,128)} %get-tuple-element.224), channel_id=1, source_target_pairs={{0,2},{1,3},{2,0},{3,1},{4,6},{5,7},{6,4},{7,5},{8,10},{9,11},{10,... | collective-permute-start | bytes 3145736 | tf_op jit(solution)/shard_map/ppermute | solution.py:922
  232.4 49.4 %collective-permute-start.26 = (f32[2,4,3,128,128]{4,3,2,1,0:T(8,128)}, f32[2,4,3,128,128]{4,3,2,1,0:T(8,128)S(1)}, u32[]{:S(2)}, u32[]{:S(2)}) collective-permute-start(f32[2,4,3,128,128]{4,3,2,1,0:T(8,128)} %get-tuple-element.242), channel_id=1, source_target_pairs={{0,8},{1,9},{2,10},{3,11},{4,12},{5,13},{6,14},{7,15},{8,0},{9,1},... | collective-permute-start | bytes 4718600 | tf_op jit(solution)/shard_map/ppermute | solution.py:922
  253.8 24.2 %collective-permute-start.23 = (f32[512,128]{1,0:T(8,128)S(1)}, f32[512,128]{1,0:T(8,128)S(1)}, u32[]{:S(2)}, u32[]{:S(2)}) collective-permute-start(f32[512,128]{1,0:T(8,128)S(1)} %add_bitcast_fusion.2.refs_10_), channel_id=1, source_target_pairs={{0,4},{1,5},{2,6},{3,7},{4,0},{5,1},{6,2},{7,3},{8,12},{9,13},{10,... | collective-permute-start | bytes 786440 | tf_op jit(solution)/shard_map/ppermute | solution.py:922
  261.1 26.7 %collective-permute-start.28 = (f32[2,768,128]{2,1,0:T(8,128)}, f32[2,768,128]{2,1,0:T(8,128)}, u32[]{:S(2)}, u32[]{:S(2)}) collective-permute-start(f32[2,768,128]{2,1,0:T(8,128)} %get-tuple-element.249), channel_id=1, source_target_pairs={{0,2},{1,3},{2,0},{3,1},{4,6},{5,7},{6,4},{7,5},{8,10},{9,11},{10,... | collective-permute-start | bytes 2359304 | tf_op jit(solution)/shard_map/ppermute | solution.py:922
  278.0 43.2 %collective-permute-start.29 = (f32[2,1024,1024]{2,1,0:T(8,128)}, f32[2,1024,1024]{2,1,0:T(8,128)}, u32[]{:S(2)}, u32[]{:S(2)}) collective-permute-start(f32[2,1024,1024]{2,1,0:T(8,128)} %get-tuple-element.252), channel_id=1, source_target_pairs={{0,1},{1,0},{2,3},{3,2},{4,5},{5,4},{6,7},{7,6},{8,9},{9,8},{10,11... | collective-permute-start | bytes 25165832 | tf_op jit(solution)/shard_map/ppermute | solution.py:922
  280.2 34.6 %collective-permute-start.34 = (f32[1024,128]{1,0:T(8,128)}, f32[1024,128]{1,0:T(8,128)}, u32[]{:S(2)}, u32[]{:S(2)}) collective-permute-start(f32[1024,128]{1,0:T(8,128)} %add_bitcast_fusion.refs_5_), channel_id=1, source_target_pairs={{0,4},{1,5},{2,6},{3,7},{4,0},{5,1},{6,2},{7,3},{8,12},{9,13},{10,... | collective-permute-start | bytes 1572872 | tf_op jit(solution)/shard_map/ppermute | solution.py:922
  290.2 50.1 %collective-permute-start.33 = (f32[768,128]{1,0:T(8,128)}, f32[768,128]{1,0:T(8,128)}, u32[]{:S(2)}, u32[]{:S(2)}) collective-permute-start(f32[768,128]{1,0:T(8,128)} %add_bitcast_fusion.1.refs_7_), channel_id=1, source_target_pairs={{0,4},{1,5},{2,6},{3,7},{4,0},{5,1},{6,2},{7,3},{8,12},{9,13},{10,... | collective-permute-start | bytes 1179656 | tf_op jit(solution)/shard_map/ppermute | solution.py:922
  314.7 33.9 %collective-permute-start.32 = (f32[800,128]{1,0:T(8,128)}, f32[800,128]{1,0:T(8,128)}, u32[]{:S(2)}, u32[]{:S(2)}) collective-permute-start(f32[800,128]{1,0:T(8,128)} %get-tuple-element.264), channel_id=1, source_target_pairs={{0,4},{1,5},{2,6},{3,7},{4,0},{5,1},{6,2},{7,3},{8,12},{9,13},{10,... | collective-permute-start | bytes 1228808 | tf_op jit(solution)/shard_map/ppermute | solution.py:922
  317.2 41.8 %collective-permute-start.35 = (f32[800,128]{1,0:T(8,128)}, f32[800,128]{1,0:T(8,128)}, u32[]{:S(2)}, u32[]{:S(2)}) collective-permute-start(f32[800,128]{1,0:T(8,128)} %get-tuple-element.272), channel_id=1, source_target_pairs={{0,2},{1,3},{2,4},{3,5},{4,6},{5,7},{6,0},{7,1},{8,10},{9,11},{10,... | collective-permute-start | bytes 1228808 | tf_op jit(solution)/shard_map/ppermute | solution.py:922
  318.1 43.5 %collective-permute-start.36 = (f32[800,128]{1,0:T(8,128)}, f32[800,128]{1,0:T(8,128)}, u32[]{:S(2)}, u32[]{:S(2)}) collective-permute-start(f32[800,128]{1,0:T(8,128)} %get-tuple-element.274), channel_id=1, source_target_pairs={{0,6},{1,7},{2,0},{3,1},{4,2},{5,3},{6,4},{7,5},{8,14},{9,15},{10,... | collective-permute-start | bytes 1228808 | tf_op jit(solution)/shard_map/ppermute | solution.py:922
  (69 other events, 615.2 us)
